TPU v7x, 128 devices: a whole 4x4x4 slice. The times are simulated.
128 devices in a mesh: row: 8 (over y, z_hi), col: 16 (over z_lo, x, core).
Axes of the slice: x: 4, y: 4, z: 4 (z_hi: 2, z_lo: 2; z = z_hi * 2 + z_lo), core: 2. Of those that a mesh axis runs over, the one named last changes fastest.
Arguments:
- orbitals: float32 [256, 256, 2048], P(None, ('row', 'col')), may hold values from -53 to 53, as said below
- potential: float32 [256, 2048], P(('row', 'col')), may hold values from 0.5 to 4
Outputs:
- correlation: float32 [256, 256], P(('row', 'col'))
- projected: float32 [256, 256], P(('row', 'col'))
- relayed: float32 [256, 256, 2048], P('col', 'row')
- relayed_applied: float32 [256, 256, 2048], P('col', 'row')
Inputs may be any that keep to these rules, and one draw needn't show every extreme that they name: `orbitals`: real values.
All inputs are finite; a program needn't handle non-finite values.
Results may differ from a plain program's by a relative error of at most 0.00007.
Values sent between devices are 32-bit elements; how exact they have to be, the bound alone decides.
No kernel may reach another device: no remote copies, remote signals or barrier semaphores. Data moves between devices by JAX's collectives and lax.ppermute only.
A program may use at most 128 MiB of HBM per device.

v0:
```python
import jax
import jax.numpy as jnp
from jax import lax
from jax.sharding import PartitionSpec as P


def extended(block, sides, width):
    for axis, dim in sides:
        count = lax.axis_size(axis)
        forward = [(i, i + 1) for i in range(count - 1)]
        backward = [(target, source) for source, target in forward]
        low = lax.ppermute(
            lax.slice_in_dim(block, block.shape[dim] - width, None, axis=dim), axis, forward
        )
        high = lax.ppermute(lax.slice_in_dim(block, 0, width, axis=dim), axis, backward)
        block = jnp.concatenate([low, block, high], axis=dim)
    return block


def apply_hamiltonian(orbitals, padded, potential):
    across = padded[:, 2:, :] + padded[:, :-2, :]
    within = jnp.roll(orbitals, 1, axis=2) + jnp.roll(orbitals, -1, axis=2)
    return (2.0 + potential)[None] * orbitals - 0.5 * across - 0.5 * within


def local(orbitals, potential):
    count_orb = orbitals.shape[0]
    padded = extended(orbitals, ((("row", "col"), 1),), 1)
    applied = apply_hamiltonian(orbitals, padded, potential)
    devices = lax.axis_size(("row", "col"))
    points = orbitals.shape[1] * orbitals.shape[2] * devices
    flattened = orbitals.reshape(count_orb, -1)
    applied_flat = applied.reshape(count_orb, -1)
    with_self = lax.dot_general(
        flattened,
        flattened,
        (((1,), (1,)), ((), ())),
        precision=lax.Precision.HIGHEST,
        preferred_element_type=jnp.float32,
    )
    with_applied = lax.dot_general(
        flattened,
        applied_flat,
        (((1,), (1,)), ((), ())),
        precision=lax.Precision.HIGHEST,
        preferred_element_type=jnp.float32,
    )
    summed = lax.psum_scatter(
        jnp.concatenate([with_self, with_applied], axis=1) / points,
        ("row", "col"),
        scatter_dimension=0,
        tiled=True,
    )
    correlation = summed[:, :count_orb]
    projected = summed[:, count_orb:]
    relayed, relayed_applied = (
        lax.all_to_all(orbitals, "col", split_axis=0, concat_axis=1, tiled=True),
        lax.all_to_all(applied, "col", split_axis=0, concat_axis=1, tiled=True),
    )
    return (correlation, projected, relayed, relayed_applied)


def solution(mesh):
    in_specs = (P(None, ("row", "col"), None), P(("row", "col"), None))
    out_specs = (
        P(("row", "col"), None),
        P(("row", "col"), None),
        P("col", "row", None),
        P("col", "row", None),
    )
    return jax.shard_map(local, mesh=mesh, in_specs=in_specs, out_specs=out_specs, check_vma=False)
```

profile of v0, /device:TPU:1, one launch (start us, length us, event | category | flops | bytes accessed | tf_op | source)
XLA Modules:
  0.0 328.7 jit_solution(1594036340415127818)
XLA Ops:
  7.2 7.8 %fusion.14 = (f32[256,1,2048]{2,1,0:T(1,128)S(1)}, f32[256,1,2048]{2,1,0:T(1,128)S(1)}) fusion(f32[256,2,2048]{2,1,0:T(2,128)} %param.2), kind=kLoop, calls=%fused_computation.21 | loop fusion | bytes 8388608 | tf_op jit(solution)/shard_map/slice | solution.py:15
  14.9 0.9 copy.39
  15.8 3.3 %collective-permute-start = (f32[256,1,2048]{2,0,1:T(8,128)S(1)}, f32[256,1,2048]{2,0,1:T(8,128)}, u32[]{:S(2)}, u32[]{:S(2)}) collective-permute-start(f32[256,1,2048]{2,0,1:T(8,128)S(1)} %copy.39), channel_id=1, source_target_pairs={{1,0},{2,1},{3,2},{4,3},{5,4},{6,5},{7,6},{8,7},{9,8},{10,9},{11,1... | collective-permute-start | bytes 6291464 | tf_op jit(solution)/shard_map/ppermute | solution.py:15
  19.2 2.2 copy.38
  21.4 0.0 copy-start.3
  21.4 3.2 collective-permute-start.1
  24.6 8.2 %all-to-all-start = ((f32[256,2,2048]{2,1,0:T(2,128)}), f32[256,2,2048]{2,1,0:T(2,128)}, u32[]{:S(2)}, u32[]{:S(2)}) async-start(f32[256,2,2048]{2,1,0:T(2,128)} %param.2), calls=%async_computation | async-start | bytes 8388608 | tf_op jit(solution)/shard_map/all_to_all | solution.py:57
  32.8 2.1 fusion.13
  34.9 0.0 copy-done.3
  34.9 11.7 %fusion.12 = (f32[256,2,2047]{2,1,0:T(2,128)S(1)}, f32[256,2,2047]{2,1,0:T(2,128)}) fusion(f32[256,2,2048]{2,1,0:T(2,128)} %param.2), kind=kLoop, calls=%fused_computation.19 | loop fusion | bytes 16769024 | tf_op jit(solution)/shard_map/jit(_roll_static)/slice | solution.py:22
  46.6 0.0 copy-start
  46.6 0.0 copy-start.2
  46.6 6.6 %collective-permute-done = f32[256,1,2048]{2,0,1:T(8,128)} collective-permute-done((f32[256,1,2048]{2,0,1:T(8,128)S(1)}, f32[256,1,2048]{2,0,1:T(8,128)}, u32[]{:S(2)}, u32[]{:S(2)}) %collective-permute-start) | collective-permute-done | bytes 2097184 | tf_op jit(solution)/shard_map/ppermute | solution.py:15
  53.2 3.7 %copy.17 = f32[256,1,2048]{2,1,0:T(1,128)S(1)} copy(f32[256,1,2048]{2,0,1:T(8,128)} %collective-permute-done) | data formatting | bytes 4194304 | tf_op jit(solution)/shard_map/ppermute | solution.py:15
  57.0 5.0 %collective-permute-done.1 = f32[256,1,2048]{2,0,1:T(8,128)} collective-permute-done((f32[256,1,2048]{2,0,1:T(8,128)}, f32[256,1,2048]{2,0,1:T(8,128)}, u32[]{:S(2)}, u32[]{:S(2)}) %collective-permute-start.1) | collective-permute-done | bytes 2097184 | tf_op jit(solution)/shard_map/ppermute | solution.py:12
  62.0 3.7 %copy.19 = f32[256,1,2048]{2,1,0:T(1,128)S(1)} copy(f32[256,1,2048]{2,0,1:T(8,128)} %collective-permute-done.1) | data formatting | bytes 4194304 | tf_op jit(solution)/shard_map/ppermute | solution.py:12
  65.8 0.0 copy-done
  65.8 0.0 copy-done.2
  65.8 15.9 %fusion.3 = f32[256,2,2048]{2,1,0:T(2,128)} fusion(f32[256,2,2048]{2,1,0:T(2,128)S(1)} %copy-done, f32[256,1,2048]{2,1,0:T(1,128)S(1)} %copy.19, f32[256,1,2048]{2,1,0:T(1,128)S(1)} %copy.17, f32[256,2,2047]{2,1,0:T(2,128)S(1)} %copy-done.2, f32[256,2,1]{2,1,0:T(2,128)} %get-tuple-element.15, f32[256,2,1]{2,1,0:T(2,128)S(1)} %get-tuple-element.14, ...), kind=kLoop, calls=%fused_computation.4 | loop fusion | flops 11534336 | bytes 20987904 | tf_op jit(solution)/shard_map/sub | solution.py:23
  81.7 20.3 %all-to-all-done = f32[256,2,2048]{2,1,0:T(2,128)} async-done(((f32[256,2,2048]{2,1,0:T(2,128)}), f32[256,2,2048]{2,1,0:T(2,128)}, u32[]{:S(2)}, u32[]{:S(2)}) %all-to-all-start) | async-done | bytes 4194336 | tf_op jit(solution)/shard_map/all_to_all | solution.py:57
  102.0 7.9 %all-to-all-start.1 = ((f32[256,2,2048]{2,1,0:T(2,128)}), f32[256,2,2048]{2,1,0:T(2,128)}, u32[]{:S(2)}, u32[]{:S(2)}) async-start(f32[256,2,2048]{2,1,0:T(2,128)} %fusion.3), calls=%async_computation.1 | async-start | bytes 8388608 | tf_op jit(solution)/shard_map/all_to_all | solution.py:58
  109.9 0.0 all-reduce.3.cloned.1.call-start
  109.9 0.0 copy-start.1
  110.0 17.3 %convolution_bitcast_fusion = f32[256,256]{0,1:T(8,128)S(1)} fusion(f32[256,2,2048]{2,1,0:T(2,128)} %param.2), kind=kOutput, calls=%fused_computation.13 | convolution fusion | flops 3221225472 | bytes 4456448 | tf_op jit(solution)/shard_map/dot_general | solution.py:34
  127.2 0.0 copy-done.1
  127.2 15.5 %fusion.7 = f32[256,256]{0,1:T(8,128)S(1)} fusion(f32[256,2,2048]{2,1,0:T(2,128)} %fusion.3, f32[256,2,2048]{2,1,0:T(2,128)S(1)} %copy-done.1), kind=kOutput, calls=%fused_computation.12 | convolution fusion | flops 3221225472 | bytes 8650752 | tf_op jit(solution)/shard_map/dot_general | solution.py:41
  142.7 0.8 maximum_multiply_fusion
  143.6 0.0 all-reduce.3.cloned.1.call-update
  143.6 149.7 %all-reduce.3.cloned.1.call-done = f32[256,512]{0,1:T(8,128)} async-done(((f32[256,512]{0,1:T(8,128)}), f32[256,512]{0,1:T(8,128)}) %all-reduce.3.cloned.1.call-update) | async-done | bytes 524304
  293.3 1.1 fusion.15
  294.4 0.7 copy.24
  295.1 0.7 copy.25
  295.8 6.9 %copy.41 = f32[16,16,2,2048]{3,2,0,1:T(2,128)} copy(f32[16,16,2,2048]{3,2,1,0:T(2,128)} %bitcast.3) | data formatting | bytes 8388608 | tf_op jit(solution)/shard_map/all_to_all | solution.py:57
  302.6 6.0 %all_to_all.29 = f32[16,32,2048]{2,1,0:T(8,128)} reshape(f32[16,16,2,2048]{3,2,1,0:T(2,128)} %bitcast.16) | data formatting | bytes 8388608 | tf_op jit(solution)/shard_map/all_to_all | solution.py:57
  308.7 0.0 all-to-all-done.1
  308.7 6.9 %copy.40 = f32[16,16,2,2048]{3,2,0,1:T(2,128)} copy(f32[16,16,2,2048]{3,2,1,0:T(2,128)} %bitcast.5) | data formatting | bytes 8388608 | tf_op jit(solution)/shard_map/all_to_all | solution.py:58
  315.6 6.0 %all_to_all.33 = f32[16,32,2048]{2,1,0:T(8,128)} reshape(f32[16,16,2,2048]{3,2,1,0:T(2,128)} %bitcast.17) | data formatting | bytes 8388608 | tf_op jit(solution)/shard_map/all_to_all | solution.py:58
  (1 shorter events, 0.0 us)
Async XLA Ops:
  15.8 37.4 %collective-permute-start = (f32[256,1,2048]{2,0,1:T(8,128)S(1)}, f32[256,1,2048]{2,0,1:T(8,128)}, u32[]{:S(2)}, u32[]{:S(2)}) collective-permute-start(f32[256,1,2048]{2,0,1:T(8,128)S(1)} %copy.39), channel_id=1, source_target_pairs={{1,0},{2,1},{3,2},{4,3},{5,4},{6,5},{7,6},{8,7},{9,8},{10,9},{11,1... | collective-permute-start | bytes 6291464 | tf_op jit(solution)/shard_map/ppermute | solution.py:15
  21.4 13.6 %copy-start.3 = (f32[2,2048]{1,0:T(2,128)S(1)}, f32[2,2048]{1,0:T(2,128)}, u32[]{:S(2)}) copy-start(f32[2,2048]{1,0:T(2,128)} %param.3) | copy-start | bytes 49156
  21.4 40.6 %collective-permute-start.1 = (f32[256,1,2048]{2,0,1:T(8,128)}, f32[256,1,2048]{2,0,1:T(8,128)}, u32[]{:S(2)}, u32[]{:S(2)}) collective-permute-start(f32[256,1,2048]{2,0,1:T(8,128)} %copy.38), channel_id=1, source_target_pairs={{0,1},{1,2},{2,3},{3,4},{4,5},{5,6},{6,7},{7,8},{8,9},{9,10},{10,1... | collective-permute-start | bytes 6291464 | tf_op jit(solution)/shard_map/ppermute | solution.py:12
  24.6 77.4 %all-to-all-start = ((f32[256,2,2048]{2,1,0:T(2,128)}), f32[256,2,2048]{2,1,0:T(2,128)}, u32[]{:S(2)}, u32[]{:S(2)}) async-start(f32[256,2,2048]{2,1,0:T(2,128)} %param.2), calls=%async_computation | async-start | bytes 8388608 | tf_op jit(solution)/shard_map/all_to_all | solution.py:57
  46.6 19.1 %copy-start = (f32[256,2,2048]{2,1,0:T(2,128)S(1)}, f32[256,2,2048]{2,1,0:T(2,128)}, u32[]{:S(2)}) copy-start(f32[256,2,2048]{2,1,0:T(2,128)} %param.2) | copy-start | bytes 12582916
  46.6 19.2 %copy-start.2 = (f32[256,2,2047]{2,1,0:T(2,128)S(1)}, f32[256,2,2047]{2,1,0:T(2,128)}, u32[]{:S(2)}) copy-start(f32[256,2,2047]{2,1,0:T(2,128)} %get-tuple-element.13) | copy-start | bytes 12576772
  102.0 206.7 %all-to-all-start.1 = ((f32[256,2,2048]{2,1,0:T(2,128)}), f32[256,2,2048]{2,1,0:T(2,128)}, u32[]{:S(2)}, u32[]{:S(2)}) async-start(f32[256,2,2048]{2,1,0:T(2,128)} %fusion.3), calls=%async_computation.1 | async-start | bytes 8388608 | tf_op jit(solution)/shard_map/all_to_all | solution.py:58
  109.9 183.4 %all-reduce.3.cloned.1.call-start = ((), (), s32[]{:S(2)}) async-start(), calls=%async_computation.2 | async-start | bytes 1048576
  109.9 17.3 %copy-start.1 = (f32[256,2,2048]{2,1,0:T(2,128)S(1)}, f32[256,2,2048]{2,1,0:T(2,128)}, u32[]{:S(2)}) copy-start(f32[256,2,2048]{2,1,0:T(2,128)} %param.2) | copy-start | bytes 12582916
Sparse Core Ops, SparseCore 0:
  143.7 149.5 all-reduce.2
where the time goes:
time: 335 us; the launch traced here: 329 us
  waiting for transfers between devices  182 us (54%)
  local copies, waits for them, and re-layouts  60.4 us (18%)
  matrix products  32.8 us (10%)
  starting transfers between devices  22.7 us (7%)
  other arithmetic  16.7 us (5%)
  between operations  14.4 us (4%)
    unnamed x2, waiting for transfers between devices  150 us
    all_to_all x1, waiting for transfers between devices, local(): lax.all_to_all(orbitals, 'col', split_axis=0, concat_axis=1, tiled=True)  20.3 us
    dot_general x1, matrix products, local(): lax.dot_general(flattened, flattened, (((1,), (1,)), ((), ())), precision...  17.3 us
    sub x1, other arithmetic, apply_hamiltonian(): return (2.0 + potential)[None] * orbitals - 0.5 * across - 0.5 * within  15.9 us
    dot_general x1, matrix products, local(): lax.dot_general(flattened, applied_flat, (((1,), (1,)), ((), ())), precis...  15.5 us
    slice x2, local copies, waits for them, and re-layouts, apply_hamiltonian(): within = jnp.roll(orbitals, 1, axis=2) + jnp.roll(orbitals, -1, axis=2)  13.8 us
    all_to_all x2, local copies, waits for them, and re-layouts, local(): lax.all_to_all(orbitals, 'col', split_axis=0, concat_axis=1, tiled=True)  12.9 us
    all_to_all x2, local copies, waits for them, and re-layouts, local(): lax.all_to_all(applied, 'col', split_axis=0, concat_axis=1, tiled=True)  12.9 us
  transfers between devices with their start and end apart: 5, of which 4 were waited for; matrix products, arithmetic and copies ran while one was open for 25% of the time, Pallas kernels for 0%

commit v1 on v0

v1 whole, which is shorter than its diff:
```python
import functools

import jax
import jax.numpy as jnp
from jax import lax
from jax.experimental import pallas as pl
from jax.experimental.pallas import tpu as pltpu
from jax.sharding import PartitionSpec as P

LANES = 128
NT = (((1,), (1,)), ((), ()))


def tile_view(x):
    *lead, planes, points = x.shape
    tiles = points // LANES
    n = len(lead)
    x = x.reshape(*lead, planes, tiles, LANES)
    x = x.transpose(*range(n), n + 1, n, n + 2)
    return x.reshape(*lead, tiles * planes, LANES)


def split(x):
    high = x.astype(jnp.bfloat16)
    return high, (x - high.astype(jnp.float32)).astype(jnp.bfloat16)


def extract_kernel(count, rows, x_ref, first_ref, last_ref):
    half = rows // 4
    for o in range(count):
        first_ref[pl.ds(o * half, half), :] = x_ref[pl.ds(o * rows, half, stride=2), :]
        last_ref[pl.ds(o * half, half), :] = x_ref[pl.ds(o * rows + 2 * half + 1, half, stride=2), :]


def extract(x, count, rows):
    block = 32
    half = rows // 4
    return pl.pallas_call(
        functools.partial(extract_kernel, block, rows),
        grid=(count // block,),
        in_specs=[pl.BlockSpec((block * rows, LANES), lambda i: (i, 0))],
        out_specs=[pl.BlockSpec((block * half, LANES), lambda i: (i, 0))] * 2,
        out_shape=[jax.ShapeDtypeStruct((count * half, LANES), jnp.float32)] * 2,
        cost_estimate=pl.CostEstimate(flops=0, bytes_accessed=count * rows * LANES * 8, transcendentals=0),
    )(x)


def gram_kernel(count, rows, scale, x_ref, v_ref, after_ref, before_ref, g_ref):
    tiles = rows // 2
    half = tiles // 2
    lane = lax.broadcasted_iota(jnp.int32, (count, LANES), 1)

    def load(t, p):
        return x_ref[pl.ds(2 * t + p, count, stride=rows), :]

    def rolled(t, p):
        return pltpu.roll(load(t % tiles, p), LANES - 1, 1)

    step = 4
    with_self = with_low = with_half = None
    now = [rolled(0, p) for p in (0, 1)]
    for begin in range(0, tiles, step):
        xs, bs = [], []
        for t in range(begin, begin + step):
            here = [load(t, p) for p in (0, 1)]
            later = [rolled(t + 1, p) for p in (0, 1)]
            for p in (0, 1):
                beside = jnp.where(lane == LANES - 1, later[p], now[p])
                if p == 0:
                    beside = beside + here[1]
                if p == 1 and t < half:
                    beside = beside + after_ref[pl.ds(t, count, stride=half), :]
                if p == 0 and t >= half:
                    beside = beside + before_ref[pl.ds(t - half, count, stride=half), :]
                factor = 1.0 + 0.5 * v_ref[pl.ds(2 * t + p, 1), :]
                xs.append(here[p])
                bs.append(factor * here[p] - 0.5 * beside)
            now = later
        x_high, x_low = split(jnp.concatenate(xs, axis=1))
        b_high, b_low = split(jnp.concatenate(bs, axis=1))
        dot = functools.partial(lax.dot_general, dimension_numbers=NT, preferred_element_type=jnp.float32)
        a = dot(x_high, x_high)
        l = dot(x_high, x_low)
        q = dot(x_high, b_high) + dot(x_high, b_low) + dot(x_low, b_high)
        with_self = a if with_self is None else with_self + a
        with_low = l if with_low is None else with_low + l
        with_half = q if with_half is None else with_half + q
    g_ref[:, :count] = (with_self + with_low + with_low.T) * scale
    g_ref[:, count:] = (with_half + with_half.T) * scale


def gram(x, v, after, before, count, rows, scale):
    return pl.pallas_call(
        functools.partial(gram_kernel, count, rows, scale),
        out_shape=jax.ShapeDtypeStruct((count, 2 * count), jnp.float32),
        in_specs=[pl.BlockSpec(memory_space=pltpu.VMEM)] * 4,
        out_specs=pl.BlockSpec(memory_space=pltpu.VMEM),
        compiler_params=pltpu.CompilerParams(vmem_limit_bytes=48 * 2**20),
        cost_estimate=pl.CostEstimate(
            flops=10 * count * count * rows * LANES, bytes_accessed=count * rows * LANES * 6, transcendentals=0
        ),
    )(x, v, after, before)


def interleaved(source_ref, start, stride, sources, tiles, work_ref):
    planes = 2 * sources
    for t in range(tiles):
        for p in (0, 1):
            for h in range(0, sources, 8):
                work_ref[pl.ds(planes * t + 2 * h + p, 8, stride=2), :] = source_ref[
                    pl.ds(start + h * stride + 2 * t + p, 8, stride=stride), :
                ]
    return jnp.concatenate([work_ref[pl.ds(planes * t, planes), :] for t in range(tiles)], axis=1)


def block_kernel(sources, block, rows, x_ref, v_ref, before_ref, after_ref, out_ref, applied_ref, v_scr, work_ref):
    tiles = rows // 2
    planes = 2 * sources

    @pl.when(pl.program_id(0) == 0)
    def _():
        v_scr[...] = 2.0 + interleaved(v_ref, 0, rows, sources, tiles, work_ref.at[0])

    flat = x_ref.reshape(sources * block * rows, LANES)
    row = lax.broadcasted_iota(jnp.int32, (planes, tiles * LANES), 0)
    for o in range(block):
        psi = interleaved(flat, o * rows, block * rows, sources, tiles, work_ref.at[o])
        out_ref[o] = psi
        down = jnp.where(row == 0, before_ref[pl.ds(o, 1), :], pltpu.roll(psi, 1, 0))
        up = jnp.where(row == planes - 1, after_ref[pl.ds(o, 1), :], pltpu.roll(psi, planes - 1, 0))
        beside = pltpu.roll(psi, 1, 1) + pltpu.roll(psi, tiles * LANES - 1, 1)
        applied_ref[o] = v_scr[...] * psi - 0.5 * (down + up) - 0.5 * beside


def to_block(x, v, before, after):
    sources, count, rows, _ = x.shape
    block = 2
    points = rows // 2 * LANES
    out = jax.ShapeDtypeStruct((count, 2 * sources, points), jnp.float32)
    before = before.reshape(count // block, block, points)
    after = after.reshape(count // block, block, points)
    edge = pl.BlockSpec((None, block, points), lambda i: (i, 0, 0))
    return pl.pallas_call(
        functools.partial(block_kernel, sources, block, rows),
        grid=(count // block,),
        in_specs=[
            pl.BlockSpec((sources, block, rows, LANES), lambda i: (0, i, 0, 0)),
            pl.BlockSpec((sources * rows, LANES), lambda i: (0, 0)),
            edge,
            edge,
        ],
        out_specs=[pl.BlockSpec((block, 2 * sources, points), lambda i: (i, 0, 0))] * 2,
        out_shape=[out, out],
        scratch_shapes=[
            pltpu.VMEM((2 * sources, points), jnp.float32),
            pltpu.VMEM((block, sources * rows, LANES), jnp.float32),
        ],
        compiler_params=pltpu.CompilerParams(vmem_limit_bytes=32 * 2**20),
        cost_estimate=pl.CostEstimate(
            flops=10 * sources * count * rows * LANES,
            bytes_accessed=12 * sources * count * rows * LANES,
            transcendentals=0,
        ),
    )(x, v, before, after)


def local(orbitals, potential):
    count, planes, points = orbitals.shape
    every = ("row", "col")
    devices, n_row, n_col = lax.axis_size(every), lax.axis_size("row"), lax.axis_size("col")
    rows = planes * points // LANES
    scale = 1.0 / (devices * planes * points)
    forward = [(i, i + 1) for i in range(devices - 1)]
    backward = [(j, i) for i, j in forward]

    tiled = tile_view(orbitals).reshape(count * rows, LANES)
    first, last = extract(tiled, count, rows)
    after = lax.ppermute(first, every, backward)
    before = lax.ppermute(last, every, forward)
    received = lax.all_to_all(orbitals, "col", split_axis=0, concat_axis=0, tiled=True)
    received = received.reshape(n_col, count // n_col, planes, points)

    potentials = lax.all_gather(potential, "col", axis=0, tiled=False)

    g = gram(tiled, tile_view(potential), after, before, count, rows, scale)
    g = lax.all_to_all(g.reshape(n_row, count // n_row, 2 * count), "row", 0, 0).sum(axis=0)
    g = lax.all_to_all(g.reshape(n_col, count // devices, 2 * count), "col", 0, 0).sum(axis=0)

    up = [(i, i + 1) for i in range(n_row - 1)]
    down = [(j, i) for i, j in up]
    edge_before = lax.ppermute(received[n_col - 1, :, planes - 1, :], "row", up)
    edge_after = lax.ppermute(received[0, :, 0, :], "row", down)
    relayed, relayed_applied = to_block(
        tile_view(received), tile_view(potentials).reshape(n_col * rows, LANES), edge_before, edge_after
    )
    return g[:, :count], g[:, count:], relayed, relayed_applied


def solution(mesh):
    in_specs = (P(None, ("row", "col"), None), P(("row", "col"), None))
    out_specs = (
        P(("row", "col"), None),
        P(("row", "col"), None),
        P("col", "row", None),
        P("col", "row", None),
    )
    return jax.shard_map(local, mesh=mesh, in_specs=in_specs, out_specs=out_specs, check_vma=False)
```

time: 335 us -> 163 us (0.49)
  the two profiles are of different devices: /device:TPU:1 before, /device:TPU:24 now
where the time goes in v1:
time: 163 us; the launch traced here: 161 us
  blocking collectives  90 us (55%)
  Pallas kernels  23.3 us (14%)
  starting transfers between devices  22.5 us (14%)
  waiting for transfers between devices  22.5 us (14%)
  local copies, waits for them, and re-layouts  2.16 us (1%)
    all_gather x1, blocking collectives, local(): potentials = lax.all_gather(potential, 'col', axis=0, tiled=False)  69.2 us
    all_to_all x1, blocking collectives, local(): lax.all_to_all(g.reshape(n_row, count // n_row, 2 * count), 'row', 0, 0)  12 us
    ppermute x1, waiting for transfers between devices, local(): after = lax.ppermute(first, every, backward)  10.7 us
    pallas_call x1, Pallas kernels, to_block(): pl.pallas_call(functools.partial(block_kernel, sources, block, rows), gri...  9.49 us
    all_to_all x1, blocking collectives, local(): lax.all_to_all(g.reshape(n_col, count // devices, 2 * count), 'col', 0, 0)  8.69 us
    ppermute x1, waiting for transfers between devices, local(): before = lax.ppermute(last, every, forward)  7.94 us
    ppermute x1, starting transfers between devices, local(): after = lax.ppermute(first, every, backward)  7.75 us
    pallas_call x1, Pallas kernels, gram(): pl.pallas_call(functools.partial(gram_kernel, count, rows, scale), out_sh...  7.71 us
  transfers between devices with their start and end apart: 5, of which 4 were waited for; matrix products, arithmetic and copies ran while one was open for 0% of the time, Pallas kernels for 0%

profile of v1, /device:TPU:24, one launch (start us, length us, event | category | flops | bytes accessed | tf_op | source)
XLA Modules:
  0.0 161.1 jit_solution(6251444889500456750)
XLA Ops:
  0.6 0.0 copy-start
  0.6 6.1 %shard_map.57 = (f32[2048,128]{1,0:T(8,128)}, f32[2048,128]{1,0:T(8,128)}) custom-call(f32[8192,128]{1,0:T(8,128)} %bitcast.33), custom_call_target="tpu_custom_call" | custom-call | bytes 8388608 | tf_op jit(solution)/shard_map/pallas_call | solution.py:38
  6.7 7.7 %collective-permute-start = (f32[2048,128]{1,0:T(8,128)}, f32[2048,128]{1,0:T(8,128)S(1)}, u32[]{:S(2)}, u32[]{:S(2)}) collective-permute-start(f32[2048,128]{1,0:T(8,128)} %get-tuple-element.8), channel_id=1, source_target_pairs={{1,0},{2,1},{3,2},{4,3},{5,4},{6,5},{7,6},{8,7},{9,8},{10,9},{11,1... | collective-permute-start | bytes 3145736 | tf_op jit(solution)/shard_map/ppermute | solution.py:178
  14.5 1.9 %collective-permute-start.1 = (f32[2048,128]{1,0:T(8,128)}, f32[2048,128]{1,0:T(8,128)S(1)}, u32[]{:S(2)}, u32[]{:S(2)}) collective-permute-start(f32[2048,128]{1,0:T(8,128)} %get-tuple-element.9), channel_id=1, source_target_pairs={{0,1},{1,2},{2,3},{3,4},{4,5},{5,6},{6,7},{7,8},{8,9},{9,10},{10,1... | collective-permute-start | bytes 3145736 | tf_op jit(solution)/shard_map/ppermute | solution.py:179
  16.4 10.7 %collective-permute-done.after_ref = f32[2048,128]{1,0:T(8,128)S(1)} collective-permute-done((f32[2048,128]{1,0:T(8,128)}, f32[2048,128]{1,0:T(8,128)S(1)}, u32[]{:S(2)}, u32[]{:S(2)}) %collective-permute-start) | collective-permute-done | bytes 1048608 | tf_op jit(solution)/shard_map/ppermute | solution.py:178
  27.1 7.9 %collective-permute-done.1.before_ref = f32[2048,128]{1,0:T(8,128)S(1)} collective-permute-done((f32[2048,128]{1,0:T(8,128)}, f32[2048,128]{1,0:T(8,128)S(1)}, u32[]{:S(2)}, u32[]{:S(2)}) %collective-permute-start.1) | collective-permute-done | bytes 1048608 | tf_op jit(solution)/shard_map/ppermute | solution.py:179
  35.0 0.0 copy-done
  35.0 7.7 %shard_map.58 = f32[256,512]{1,0:T(8,128)S(1)} custom-call(f32[8192,128]{1,0:T(8,128)} %bitcast.34, f32[32,128]{1,0:T(8,128)S(1)} %bitcast.31, f32[2048,128]{1,0:T(8,128)S(1)} %collective-permute-done.after_ref, f32[2048,128]{1,0:T(8,128)S(1)} %collective-permute-done.1.before_ref), custom_call_target="tpu_custom_call" | custom-call | flops 2684354560 | bytes 6291456 | tf_op jit(solution)/shard_map/pallas_call | solution.py:93
  42.7 12.0 %all_to_all.15 = f32[8,32,512]{2,1,0:T(8,128)S(1)} all-to-all(f32[8,32,512]{2,1,0:T(8,128)S(1)} %bitcast.30), channel_id=1, replica_groups=mesh['row'=8,'col'=16] {'row'}, dimensions={0} | all-to-all | bytes 1048576 | tf_op jit(solution)/shard_map/all_to_all | solution.py:186
  54.8 8.7 %all_to_all.16 = f32[16,2,512]{2,1,0:T(2,128)S(1)} all-to-all(f32[16,2,512]{2,1,0:T(2,128)S(1)} %reshape.42), channel_id=1, replica_groups=mesh['row'=8,'col'=16] {'col'}, dimensions={0} | all-to-all | bytes 131072 | tf_op jit(solution)/shard_map/all_to_all | solution.py:187
  63.5 4.5 %all-to-all-start.2 = ((f32[256,2,2048]{2,1,0:T(2,128)}), f32[256,2,2048]{2,1,0:T(2,128)}, u32[]{:S(2)}, u32[]{:S(2)}) async-start(f32[256,2,2048]{2,1,0:T(2,128)} %param.2), calls=%async_computation.2 | async-start | bytes 8388608 | tf_op jit(solution)/shard_map/all_to_all | solution.py:180
  68.1 69.2 %all-gather.1 = f32[16,2,2048]{2,1,0:T(2,128)S(1)} all-gather(f32[1,2,2048]{2,1,0:T(2,128)S(1)} %bitcast.32), channel_id=2, replica_groups=mesh['row'=8,'col'=16] {'col'}, dimensions={0}, use_global_device_ids=true | all-gather | bytes 278528 | tf_op jit(solution)/shard_map/all_gather | solution.py:183
  137.3 0.0 all-to-all-done.2
  137.3 1.3 fusion
  138.7 3.2 %collective-permute-start.2 = (f32[16,2048]{1,0:T(8,128)S(1)}, f32[16,2048]{1,0:T(8,128)S(1)}, u32[]{:S(2)}, u32[]{:S(2)}) collective-permute-start(f32[16,2048]{1,0:T(8,128)S(1)} %bitcast.35), channel_id=1, source_target_pairs={{0,16},{16,32},{32,48},{48,64},{64,80},{80,96},{96,112},{1,17},{17... | collective-permute-start | bytes 393224 | tf_op jit(solution)/shard_map/ppermute | solution.py:191
  141.9 5.1 %collective-permute-start.3 = (f32[16,2048]{1,0:T(8,128)S(1)}, f32[16,2048]{1,0:T(8,128)S(1)}, u32[]{:S(2)}, u32[]{:S(2)}) collective-permute-start(f32[16,2048]{1,0:T(8,128)S(1)} %bitcast.36), channel_id=1, source_target_pairs={{16,0},{32,16},{48,32},{64,48},{80,64},{96,80},{112,96},{17,1},{33... | collective-permute-start | bytes 393224 | tf_op jit(solution)/shard_map/ppermute | solution.py:192
  147.0 0.6 fusion.1
  147.6 1.2 collective-permute-done.2
  148.8 0.1 reshape.46.before_ref
  148.9 2.6 %collective-permute-done.3 = f32[16,2048]{1,0:T(8,128)S(1)} collective-permute-done((f32[16,2048]{1,0:T(8,128)S(1)}, f32[16,2048]{1,0:T(8,128)S(1)}, u32[]{:S(2)}, u32[]{:S(2)}) %collective-permute-start.3) | collective-permute-done | bytes 131104 | tf_op jit(solution)/shard_map/ppermute | solution.py:192
  151.5 0.1 reshape.47.after_ref
  151.6 9.5 %shard_map.59 = (f32[16,32,2048]{2,1,0:T(8,128)}, f32[16,32,2048]{2,1,0:T(8,128)}) custom-call(f32[16,16,32,128]{3,2,1,0:T(8,128)} %bitcast.11.x_ref, f32[512,128]{1,0:T(8,128)S(1)} %bitcast.29, f32[8,2,2048]{2,1,0:T(2,128)S(1)} %reshape.46.before_ref, f32[8,2,2048]{2,1,0:T(2,128)S(1)} %reshape.47.after_ref), custom_call_target="tpu_custom_call" | custom-call | flops 10485760 | bytes 12582912 | tf_op jit(solution)/shard_map/pallas_call | solution.py:143
  (5 shorter events, 0.2 us)
Async XLA Ops:
  0.6 34.4 %copy-start = (f32[2,2048]{1,0:T(2,128)S(1)}, f32[2,2048]{1,0:T(2,128)}, u32[]{:S(2)}) copy-start(f32[2,2048]{1,0:T(2,128)} %param.3) | copy-start | bytes 49156
  6.7 20.4 %collective-permute-start = (f32[2048,128]{1,0:T(8,128)}, f32[2048,128]{1,0:T(8,128)S(1)}, u32[]{:S(2)}, u32[]{:S(2)}) collective-permute-start(f32[2048,128]{1,0:T(8,128)} %get-tuple-element.8), channel_id=1, source_target_pairs={{1,0},{2,1},{3,2},{4,3},{5,4},{6,5},{7,6},{8,7},{9,8},{10,9},{11,1... | collective-permute-start | bytes 3145736 | tf_op jit(solution)/shard_map/ppermute | solution.py:178
  14.5 20.5 %collective-permute-start.1 = (f32[2048,128]{1,0:T(8,128)}, f32[2048,128]{1,0:T(8,128)S(1)}, u32[]{:S(2)}, u32[]{:S(2)}) collective-permute-start(f32[2048,128]{1,0:T(8,128)} %get-tuple-element.9), channel_id=1, source_target_pairs={{0,1},{1,2},{2,3},{3,4},{4,5},{5,6},{6,7},{7,8},{8,9},{9,10},{10,1... | collective-permute-start | bytes 3145736 | tf_op jit(solution)/shard_map/ppermute | solution.py:179
  63.5 73.8 %all-to-all-start.2 = ((f32[256,2,2048]{2,1,0:T(2,128)}), f32[256,2,2048]{2,1,0:T(2,128)}, u32[]{:S(2)}, u32[]{:S(2)}) async-start(f32[256,2,2048]{2,1,0:T(2,128)} %param.2), calls=%async_computation.2 | async-start | bytes 8388608 | tf_op jit(solution)/shard_map/all_to_all | solution.py:180
  138.7 10.1 %collective-permute-start.2 = (f32[16,2048]{1,0:T(8,128)S(1)}, f32[16,2048]{1,0:T(8,128)S(1)}, u32[]{:S(2)}, u32[]{:S(2)}) collective-permute-start(f32[16,2048]{1,0:T(8,128)S(1)} %bitcast.35), channel_id=1, source_target_pairs={{0,16},{16,32},{32,48},{48,64},{64,80},{80,96},{96,112},{1,17},{17... | collective-permute-start | bytes 393224 | tf_op jit(solution)/shard_map/ppermute | solution.py:191
  141.9 9.6 %collective-permute-start.3 = (f32[16,2048]{1,0:T(8,128)S(1)}, f32[16,2048]{1,0:T(8,128)S(1)}, u32[]{:S(2)}, u32[]{:S(2)}) collective-permute-start(f32[16,2048]{1,0:T(8,128)S(1)} %bitcast.36), channel_id=1, source_target_pairs={{16,0},{32,16},{48,32},{64,48},{80,64},{96,80},{112,96},{17,1},{33... | collective-permute-start | bytes 393224 | tf_op jit(solution)/shard_map/ppermute | solution.py:192

commit v2 on v1

v2 whole, which is shorter than its diff:
```python
import functools

import jax
import jax.numpy as jnp
from jax import lax
from jax.experimental import pallas as pl
from jax.experimental.pallas import tpu as pltpu
from jax.sharding import PartitionSpec as P

LANES = 128
NT = (((1,), (1,)), ((), ()))


def tile_view(x):
    *lead, planes, points = x.shape
    tiles = points // LANES
    n = len(lead)
    x = x.reshape(*lead, planes, tiles, LANES)
    x = x.transpose(*range(n), n + 1, n, n + 2)
    return x.reshape(*lead, tiles * planes, LANES)


def split(x):
    high = x.astype(jnp.bfloat16)
    return high, (x - high.astype(jnp.float32)).astype(jnp.bfloat16)


def extract_kernel(count, rows, x_ref, v_ref, first_ref, last_ref, packed_ref):
    half = rows // 4
    for o in range(count):
        first_ref[pl.ds(o * half, half), :] = x_ref[pl.ds(o * rows, half, stride=2), :]
        last_ref[pl.ds(o * half, half), :] = x_ref[pl.ds(o * rows + 2 * half + 1, half, stride=2), :]
    parts, length = packed_ref.shape[0], count // packed_ref.shape[0] * rows
    for c in range(parts):
        packed_ref[c, :length] = x_ref[pl.ds(c * length, length), :]
        packed_ref[c, length:] = v_ref[...]


def extract(x, v, count, rows, parts):
    half = jax.ShapeDtypeStruct((count * rows // 4, LANES), jnp.float32)
    packed = jax.ShapeDtypeStruct((parts, (count // parts + 1) * rows, LANES), jnp.float32)
    return pl.pallas_call(
        functools.partial(extract_kernel, count, rows),
        in_specs=[pl.BlockSpec(memory_space=pltpu.VMEM)] * 2,
        out_specs=[pl.BlockSpec(memory_space=pltpu.VMEM)] * 3,
        out_shape=[half, half, packed],
        compiler_params=pltpu.CompilerParams(vmem_limit_bytes=16 * 2**20),
        cost_estimate=pl.CostEstimate(flops=0, bytes_accessed=count * rows * LANES * 10, transcendentals=0),
    )(x, v)


def gram_kernel(count, rows, scale, x_ref, v_ref, after_ref, before_ref, keep_ref, send_ref, work_ref):
    tiles = rows // 2
    half = tiles // 2
    lane = lax.broadcasted_iota(jnp.int32, (count, LANES), 1)

    def load(t, p):
        return x_ref[pl.ds(2 * t + p, count, stride=rows), :]

    def rolled(t, p):
        return pltpu.roll(load(t % tiles, p), LANES - 1, 1)

    step = 4
    with_self = with_low = with_half = None
    now = [rolled(0, p) for p in (0, 1)]
    for begin in range(0, tiles, step):
        xs, bs = [], []
        for t in range(begin, begin + step):
            here = [load(t, p) for p in (0, 1)]
            later = [rolled(t + 1, p) for p in (0, 1)]
            for p in (0, 1):
                beside = jnp.where(lane == LANES - 1, later[p], now[p])
                if p == 0:
                    beside = beside + here[1]
                if p == 1 and t < half:
                    beside = beside + after_ref[pl.ds(t, count, stride=half), :]
                if p == 0 and t >= half:
                    beside = beside + before_ref[pl.ds(t - half, count, stride=half), :]
                factor = 1.0 + 0.5 * v_ref[pl.ds(2 * t + p, 1), :]
                xs.append(here[p])
                bs.append(factor * here[p] - 0.5 * beside)
            now = later
        x_high, x_low = split(jnp.concatenate(xs, axis=1))
        b_high, b_low = split(jnp.concatenate(bs, axis=1))
        dot = functools.partial(lax.dot_general, dimension_numbers=NT, preferred_element_type=jnp.float32)
        a = dot(x_high, x_high)
        l = dot(x_high, x_low)
        q = dot(x_high, b_high) + dot(x_high, b_low) + dot(x_low, b_high)
        with_self = a if with_self is None else with_self + a
        with_low = l if with_low is None else with_low + l
        with_half = q if with_half is None else with_half + q
    first = (with_self + with_low + with_low.T) * scale
    second = (with_half + with_half.T) * scale
    blocks = count // LANES
    for m, matrix in enumerate((first, second)):
        for j in range(blocks):
            work_ref[m * blocks + j] = matrix[:, j * LANES : (j + 1) * LANES]
    core = lax.rem(lax.axis_index("col"), 2)
    chips = count // 4
    for ref, which in ((keep_ref, core), (send_ref, 1 - core)):
        for b in (0, 1):
            for j in range(2 * blocks):
                ref[:, pl.ds((b * 2 * blocks + j) * LANES, LANES)] = work_ref.at[j][
                    pl.ds(2 * which + b, chips, stride=4), :
                ]


def gram(x, v, after, before, count, rows, scale):
    part = jax.ShapeDtypeStruct((count // 4, 4 * count), jnp.float32)
    return pl.pallas_call(
        functools.partial(gram_kernel, count, rows, scale),
        out_shape=[part, part],
        in_specs=[pl.BlockSpec(memory_space=pltpu.VMEM)] * 4,
        out_specs=[pl.BlockSpec(memory_space=pltpu.VMEM)] * 2,
        scratch_shapes=[pltpu.VMEM((2 * count // LANES, count, LANES), jnp.float32)],
        compiler_params=pltpu.CompilerParams(vmem_limit_bytes=16 * 2**20),
        cost_estimate=pl.CostEstimate(
            flops=400 * count * count * rows * LANES, bytes_accessed=count * rows * LANES * 6, transcendentals=0
        ),
    )(x, v, after, before)


def edges_kernel(orbitals, rows, low_ref, high_ref, first_ref, last_ref):
    for t in range(rows // 2):
        lanes = pl.ds(t * LANES, LANES)
        first_ref[:, lanes] = low_ref[0, pl.ds(2 * t, orbitals, stride=rows), :]
        last_ref[:, lanes] = high_ref[0, pl.ds(2 * t + 1, orbitals, stride=rows), :]


def edges_of(received, orbitals, rows):
    sources, length, _ = received.shape
    out = jax.ShapeDtypeStruct((orbitals, rows // 2 * LANES), jnp.float32)
    return pl.pallas_call(
        functools.partial(edges_kernel, orbitals, rows),
        grid=(1,),
        in_specs=[
            pl.BlockSpec((1, length, LANES), lambda i: (0, 0, 0)),
            pl.BlockSpec((1, length, LANES), lambda i: (sources - 1, 0, 0)),
        ],
        out_specs=[pl.BlockSpec(out.shape, lambda i: (0, 0))] * 2,
        out_shape=[out, out],
        compiler_params=pltpu.CompilerParams(vmem_limit_bytes=8 * 2**20),
        cost_estimate=pl.CostEstimate(flops=0, bytes_accessed=2**18, transcendentals=0),
    )(received, received)


def block_kernel(sources, block, rows, x_ref, v_ref, out_ref, applied_ref, sides_ref, v_scr, work_ref):
    tiles, planes = rows // 2, 2 * sources
    points = tiles * LANES

    def interleaved(flat, start, stride, work):
        for k in range(sources):
            for q in range(0, tiles, 4):
                piece = flat[pl.ds(k * stride + start + 2 * q, 8), :]
                for i in range(4):
                    work[pl.ds(planes * (q + i) + 2 * k, 2), :] = piece[2 * i : 2 * i + 2, :]
        return jnp.concatenate([work[pl.ds(planes * t, planes), :] for t in range(tiles)], axis=1)

    @pl.when(pl.program_id(0) == 0)
    def _():
        v_scr[...] = 2.0 + interleaved(v_ref.reshape(sources * rows, LANES), 0, rows, work_ref.at[0])

    flat = x_ref.reshape(sources * block * rows, LANES)
    row = lax.broadcasted_iota(jnp.int32, (planes, points), 0)
    for o in range(block):
        psi = interleaved(flat, o * rows, block * rows, work_ref.at[o])
        out_ref[o] = psi
        down = jnp.where(row == 0, 0.0, pltpu.roll(psi, 1, 0))
        up = jnp.where(row == planes - 1, 0.0, pltpu.roll(psi, planes - 1, 0))
        beside = pltpu.roll(psi, 1, 1) + pltpu.roll(psi, points - 1, 1)
        applied = v_scr[...] * psi - 0.5 * (down + up) - 0.5 * beside
        applied_ref[o] = applied
        at = pl.program_id(0) * block + o
        sides_ref[0, at] = applied[:8]
        sides_ref[1, at] = applied[planes - 8 :]


def to_block(received, orbitals, rows):
    block, sources = 4, received.shape[0]
    planes, points = 2 * sources, rows // 2 * LANES
    received = received.reshape(sources, orbitals + 1, rows, LANES)
    out = jax.ShapeDtypeStruct((orbitals, planes, points), jnp.float32)
    return pl.pallas_call(
        functools.partial(block_kernel, sources, block, rows),
        grid=(orbitals // block,),
        in_specs=[
            pl.BlockSpec((sources, block, rows, LANES), lambda i: (0, i, 0, 0)),
            pl.BlockSpec((sources, 1, rows, LANES), lambda i: (0, orbitals, 0, 0)),
        ],
        out_specs=[pl.BlockSpec((block, planes, points), lambda i: (i, 0, 0))] * 2
        + [pl.BlockSpec(memory_space=pltpu.VMEM)],
        out_shape=[out, out, jax.ShapeDtypeStruct((2, orbitals, 8, points), jnp.float32)],
        scratch_shapes=[
            pltpu.VMEM((planes, points), jnp.float32),
            pltpu.VMEM((block, planes * points // LANES, LANES), jnp.float32),
        ],
        compiler_params=pltpu.CompilerParams(vmem_limit_bytes=24 * 2**20),
        cost_estimate=pl.CostEstimate(flops=0, bytes_accessed=12 * orbitals * planes * points, transcendentals=0),
    )(received, received)


def fix_kernel(before_ref, after_ref, sides_ref, applied_ref, out_ref, work_ref, sem):
    orbitals, planes, _ = applied_ref.shape
    copies = []
    for e, edge_ref in enumerate((before_ref, after_ref)):
        for o in range(orbitals):
            row = 7 * e
            work_ref[e, o] = sides_ref[e, o]
            work_ref[e, o, pl.ds(row, 1), :] = sides_ref[e, o, pl.ds(row, 1), :] - 0.5 * edge_ref[pl.ds(o, 1), :]
            target = out_ref.at[o, pl.ds(e * (planes - 8), 8), :]
            copies.append(pltpu.make_async_copy(work_ref.at[e, o], target, sem.at[e, o]))
            copies[-1].start()
    for copy in copies:
        copy.wait()


def fix_edges(applied, sides, before, after):
    orbitals, _, points = applied.shape
    return pl.pallas_call(
        fix_kernel,
        in_specs=[pl.BlockSpec(memory_space=pltpu.VMEM)] * 3 + [pl.BlockSpec(memory_space=pl.ANY)],
        out_specs=pl.BlockSpec(memory_space=pl.ANY),
        out_shape=jax.ShapeDtypeStruct(applied.shape, jnp.float32),
        input_output_aliases={3: 0},
        scratch_shapes=[
            pltpu.VMEM((2, orbitals, 8, points), jnp.float32),
            pltpu.SemaphoreType.DMA((2, orbitals)),
        ],
        compiler_params=pltpu.CompilerParams(vmem_limit_bytes=12 * 2**20),
        cost_estimate=pl.CostEstimate(flops=0, bytes_accessed=32 * orbitals * points, transcendentals=0),
    )(before, after, sides, applied)


def exchange(x, mask):
    every = ("row", "col")
    return lax.ppermute(x, every, [(i, i ^ mask) for i in range(lax.axis_size(every))])


def digit(position, radix):
    return (lax.axis_index(("row", "col")) // position) % radix


def reduce_digit(total, position):
    mine = digit(position, 4)
    parts = total.reshape(4, -1, total.shape[-1])
    pick = lambda k: lax.dynamic_index_in_dim(parts, mine ^ k, 0, keepdims=False)
    sent = [exchange(pick(k), k * position) for k in (1, 2, 3)]
    return pick(0) + sent[0] + sent[1] + sent[2]


def local(orbitals, potential):
    count, planes, points = orbitals.shape
    every = ("row", "col")
    devices, n_row, n_col = lax.axis_size(every), lax.axis_size("row"), lax.axis_size("col")
    rows = planes * points // LANES
    mine = count // n_col
    scale = 1.0 / (devices * planes * points)
    forward = [(i, i + 1) for i in range(devices - 1)]
    backward = [(j, i) for i, j in forward]

    tiled = tile_view(orbitals).reshape(count * rows, LANES)
    v = tile_view(potential)
    first, last, packed = extract(tiled, v, count, rows, n_col)
    after = lax.ppermute(first, every, backward)
    before = lax.ppermute(last, every, forward)
    received = lax.all_to_all(packed, "col", split_axis=0, concat_axis=0, tiled=True)

    keep, send = gram(tiled, v, after, before, count, rows, scale)
    g = reduce_digit(keep + exchange(send, 1), 32)
    g = reduce_digit(g, 8)
    g, _ = lax.optimization_barrier((g, received))
    g = reduce_digit(g, 2).reshape(planes, 2 * count)

    up = [(i, i + 1) for i in range(n_row - 1)]
    down = [(j, i) for i, j in up]
    first, last = edges_of(received, mine, rows)
    before, after = lax.ppermute(last, "row", up), lax.ppermute(first, "row", down)
    relayed, applied, sides = to_block(received, mine, rows)
    return g[:, :count], g[:, count:], relayed, fix_edges(applied, sides, before, after)


def solution(mesh):
    in_specs = (P(None, ("row", "col"), None), P(("row", "col"), None))
    out_specs = (
        P(("row", "col"), None),
        P(("row", "col"), None),
        P("col", "row", None),
        P("col", "row", None),
    )
    return jax.shard_map(local, mesh=mesh, in_specs=in_specs, out_specs=out_specs, check_vma=False)
```

time: 163 us -> 103 us (0.63)
  blocking collectives: 90 us -> 0 us
  waiting for transfers between devices: 22.5 us -> 41.6 us
  starting transfers between devices: 22.5 us -> 35.1 us
  Pallas kernels: 23.3 us -> 17.2 us
  local copies, waits for them, and re-layouts: 2.16 us -> 7.84 us
    all_gather x1 -> x0, blocking collectives: 69.2 us -> none  [local(): potentials = lax.all_gather(potential, 'col', axis=0, tiled=False)]
    all_to_all x2 -> x0, blocking collectives: 20.7 us -> none  [the longest x1 12 us: local(): lax.all_to_all(g.reshape(n_row, count // n_row, 2 * count), 'row', 0, 0)]
    ppermute x2 -> x12, starting transfers between devices: 8.25 us -> 20.8 us  [the longest x10 12.6 us: exchange(): lax.ppermute(x, every, [(i, i ^ mask) for i in range(lax.axis_size(every))])]
    unnamed x4 -> x10, local copies, waits for them, and re-layouts: 0.09 us -> 7.17 us
    ppermute x1, waiting for transfers between devices: 10.7 us -> 17.2 us  [local(): after = lax.ppermute(first, every, backward)]
    ppermute x1, waiting for transfers between devices: 7.94 us -> 13.8 us  [local(): before = lax.ppermute(last, every, forward)]
    ppermute x2 -> x12, waiting for transfers between devices: 3.88 us -> 9.47 us  [the longest x10 9.46 us: exchange(): lax.ppermute(x, every, [(i, i ^ mask) for i in range(lax.axis_size(every))])]
    pallas_call x1, Pallas kernels: 9.49 us -> 7.29 us  [to_block(): pl.pallas_call(functools.partial(block_kernel, sources, block, rows), gri...]
  transfers between devices with their start and end apart: 5 -> 15, of which waited for: 4 -> 9; matrix products, arithmetic and copies ran while one was open for 0% -> 1% of each run, Pallas kernels for 0% -> 14%
where the time goes in v2:
time: 103 us
  waiting for transfers between devices  41.6 us (40%)
  starting transfers between devices  35.1 us (34%)
  Pallas kernels  17.2 us (17%)
  local copies, waits for them, and re-layouts  7.84 us (8%)
    ppermute x1, waiting for transfers between devices, local(): after = lax.ppermute(first, every, backward)  17.2 us
    ppermute x1, waiting for transfers between devices, local(): before = lax.ppermute(last, every, forward)  13.8 us
    ppermute x10, starting transfers between devices, exchange(): lax.ppermute(x, every, [(i, i ^ mask) for i in range(lax.axis_size(every))])  12.6 us
    ppermute x10, waiting for transfers between devices, exchange(): lax.ppermute(x, every, [(i, i ^ mask) for i in range(lax.axis_size(every))])  9.46 us
    ppermute x1, starting transfers between devices, local(): after = lax.ppermute(first, every, backward)  7.75 us
    pallas_call x1, Pallas kernels, to_block(): pl.pallas_call(functools.partial(block_kernel, sources, block, rows), gri...  7.29 us
    unnamed x10, local copies, waits for them, and re-layouts  7.17 us
    pallas_call x1, Pallas kernels, gram(): pl.pallas_call(functools.partial(gram_kernel, count, rows, scale), out_sh...  5.62 us
  transfers between devices with their start and end apart: 15, of which 9 were waited for; matrix products, arithmetic and copies ran while one was open for 1% of the time, Pallas kernels for 14%

profile of v2, /device:TPU:24, one launch (start us, length us, event | category | flops | bytes accessed | tf_op | source)
XLA Modules:
  0.0 102.6 jit_solution(6295257763350699177)
XLA Ops:
  0.6 0.0 copy-start.1
  0.6 2.2 %copy-done.1 = f32[256,2,2048]{2,1,0:T(2,128)S(1)} copy-done((f32[256,2,2048]{2,1,0:T(2,128)S(1)}, f32[256,2,2048]{2,1,0:T(2,128)}, u32[]{:S(2)}) %copy-start.1) | copy-done | bytes 4194328
  2.8 0.0 copy-start.3
  2.8 0.7 copy-done.3
  3.5 1.5 %shard_map.57 = (f32[2048,128]{1,0:T(8,128)}, f32[2048,128]{1,0:T(8,128)S(1)}, f32[16,544,128]{2,1,0:T(8,128)S(1)}) custom-call(f32[8192,128]{1,0:T(8,128)S(1)} %bitcast.36, f32[32,128]{1,0:T(8,128)S(1)} %bitcast.38), custom_call_target="tpu_custom_call" | custom-call | bytes 10485760 | tf_op jit(solution)/shard_map/pallas_call | solution.py:42
  5.0 0.0 copy-start
  5.0 2.1 %copy-done = f32[16,544,128]{2,1,0:T(8,128)} copy-done((f32[16,544,128]{2,1,0:T(8,128)}, f32[16,544,128]{2,1,0:T(8,128)S(1)}, u32[]{:S(2)}) %copy-start) | copy-done | bytes 4456472
  7.1 7.7 %collective-permute-start = (f32[2048,128]{1,0:T(8,128)}, f32[2048,128]{1,0:T(8,128)S(1)}, u32[]{:S(2)}, u32[]{:S(2)}) collective-permute-start(f32[2048,128]{1,0:T(8,128)} %get-tuple-element.15), channel_id=1, source_target_pairs={{1,0},{2,1},{3,2},{4,3},{5,4},{6,5},{7,6},{8,7},{9,8},{10,9},{11,1... | collective-permute-start | bytes 3145736 | tf_op jit(solution)/shard_map/ppermute | solution.py:264
  14.8 1.9 %collective-permute-start.1 = (f32[2048,128]{1,0:T(8,128)S(1)}, f32[2048,128]{1,0:T(8,128)S(1)}, u32[]{:S(2)}, u32[]{:S(2)}) collective-permute-start(f32[2048,128]{1,0:T(8,128)S(1)} %get-tuple-element.16), channel_id=1, source_target_pairs={{0,1},{1,2},{2,3},{3,4},{4,5},{5,6},{6,7},{7,8},{8,9},{9,10},{10,1... | collective-permute-start | bytes 3145736 | tf_op jit(solution)/shard_map/ppermute | solution.py:265
  16.8 0.0 copy-start.4
  16.8 4.6 %all-to-all-start = ((f32[16,544,128]{2,1,0:T(8,128)}), f32[16,544,128]{2,1,0:T(8,128)}, u32[]{:S(2)}, u32[]{:S(2)}) async-start(f32[16,544,128]{2,1,0:T(8,128)} %copy-done), calls=%async_computation | async-start | bytes 8912896 | tf_op jit(solution)/shard_map/all_to_all | solution.py:266
  21.4 17.2 %collective-permute-done.after_ref = f32[2048,128]{1,0:T(8,128)S(1)} collective-permute-done((f32[2048,128]{1,0:T(8,128)}, f32[2048,128]{1,0:T(8,128)S(1)}, u32[]{:S(2)}, u32[]{:S(2)}) %collective-permute-start) | collective-permute-done | bytes 1048608 | tf_op jit(solution)/shard_map/ppermute | solution.py:264
  38.5 13.8 %collective-permute-done.1.before_ref = f32[2048,128]{1,0:T(8,128)S(1)} collective-permute-done((f32[2048,128]{1,0:T(8,128)S(1)}, f32[2048,128]{1,0:T(8,128)S(1)}, u32[]{:S(2)}, u32[]{:S(2)}) %collective-permute-start.1) | collective-permute-done | bytes 1048608 | tf_op jit(solution)/shard_map/ppermute | solution.py:265
  52.3 0.0 copy-done.4
  52.3 0.0 copy-start.2
  52.3 2.2 %copy-done.2 = f32[256,2,2048]{2,1,0:T(2,128)S(1)} copy-done((f32[256,2,2048]{2,1,0:T(2,128)S(1)}, f32[256,2,2048]{2,1,0:T(2,128)}, u32[]{:S(2)}) %copy-start.2) | copy-done | bytes 4194328
  54.5 5.6 %shard_map.58 = (f32[64,1024]{1,0:T(8,128)S(1)}, f32[64,1024]{1,0:T(8,128)S(1)}) custom-call(f32[8192,128]{1,0:T(8,128)S(1)} %bitcast.37, f32[32,128]{1,0:T(8,128)S(1)} %bitcast.39, f32[2048,128]{1,0:T(8,128)S(1)} %collective-permute-done.after_ref, f32[2048,128]{1,0:T(8,128)S(1)} %collective-permute-done.1.before_ref), custom_call_target="tpu_custom_call" | custom-call | flops 107374182400 | bytes 6291456 | tf_op jit(solution)/shard_map/pallas_call | solution.py:110
  60.1 0.1 collective-permute-start.2
  60.3 1.5 %collective-permute-done.2 = f32[64,1024]{1,0:T(8,128)S(1)} collective-permute-done((f32[64,1024]{1,0:T(8,128)S(1)}, f32[64,1024]{1,0:T(8,128)S(1)}, u32[]{:S(2)}, u32[]{:S(2)}) %collective-permute-start.2) | collective-permute-done | bytes 262176 | tf_op jit(solution)/shard_map/ppermute | solution.py:236
  61.8 0.5 collective-permute-start.3
  62.3 1.1 %collective-permute-start.5 = (f32[16,1024]{1,0:T(8,128)S(1)}, f32[16,1024]{1,0:T(8,128)S(1)}, u32[]{:S(2)}, u32[]{:S(2)}) collective-permute-start(f32[16,1024]{1,0:T(8,128)S(1)} %get-tuple-element.27), channel_id=1, source_target_pairs={{0,96},{1,97},{2,98},{3,99},{4,100},{5,101},{6,102},{7,103},{8,104... | collective-permute-start | bytes 196616 | tf_op jit(solution)/shard_map/ppermute | solution.py:236
  63.4 2.6 %collective-permute-start.4 = (f32[16,1024]{1,0:T(8,128)S(1)}, f32[16,1024]{1,0:T(8,128)S(1)}, u32[]{:S(2)}, u32[]{:S(2)}) collective-permute-start(f32[16,1024]{1,0:T(8,128)S(1)} %get-tuple-element.28), channel_id=1, source_target_pairs={{0,64},{1,65},{2,66},{3,67},{4,68},{5,69},{6,70},{7,71},{8,72},{9,... | collective-permute-start | bytes 196616 | tf_op jit(solution)/shard_map/ppermute | solution.py:236
  66.0 0.2 collective-permute-done.3
  66.1 2.4 %collective-permute-done.5 = f32[16,1024]{1,0:T(8,128)S(1)} collective-permute-done((f32[16,1024]{1,0:T(8,128)S(1)}, f32[16,1024]{1,0:T(8,128)S(1)}, u32[]{:S(2)}, u32[]{:S(2)}) %collective-permute-start.5) | collective-permute-done | bytes 65568 | tf_op jit(solution)/shard_map/ppermute | solution.py:236
  68.5 0.7 collective-permute-done.4
  69.2 0.1 collective-permute-start.6
  69.3 0.1 collective-permute-start.8
  69.4 4.0 %collective-permute-start.7 = (f32[4,1024]{1,0:T(4,128)S(1)}, f32[4,1024]{1,0:T(4,128)S(1)}, u32[]{:S(2)}, u32[]{:S(2)}) collective-permute-start(f32[4,1024]{1,0:T(4,128)S(1)} %get-tuple-element.31), channel_id=1, source_target_pairs={{0,16},{1,17},{2,18},{3,19},{4,20},{5,21},{6,22},{7,23},{8,24},{9,... | collective-permute-start | bytes 49160 | tf_op jit(solution)/shard_map/ppermute | solution.py:236
  73.4 0.0 collective-permute-done.6
  73.4 0.9 collective-permute-done.8
  74.4 3.8 %collective-permute-done.7 = f32[4,1024]{1,0:T(4,128)S(1)} collective-permute-done((f32[4,1024]{1,0:T(4,128)S(1)}, f32[4,1024]{1,0:T(4,128)S(1)}, u32[]{:S(2)}, u32[]{:S(2)}) %collective-permute-start.7) | collective-permute-done | bytes 16416 | tf_op jit(solution)/shard_map/ppermute | solution.py:236
  78.2 1.2 %all-to-all-done.low_ref.high_ref = f32[16,544,128]{2,1,0:T(8,128)} async-done(((f32[16,544,128]{2,1,0:T(8,128)}), f32[16,544,128]{2,1,0:T(8,128)}, u32[]{:S(2)}, u32[]{:S(2)}) %all-to-all-start) | async-done | bytes 4456480 | tf_op jit(solution)/shard_map/all_to_all | solution.py:266
  79.4 1.5 %collective-permute-start.9 = (f32[1,1024]{1,0:T(1,128)S(1)}, f32[1,1024]{1,0:T(1,128)S(1)}, u32[]{:S(2)}, u32[]{:S(2)}) collective-permute-start(f32[1,1024]{1,0:T(1,128)S(1)} %get-tuple-element.32), channel_id=1, source_target_pairs={{0,2},{1,3},{2,0},{3,1},{4,6},{5,7},{6,4},{7,5},{8,10},{9,11},{10,... | collective-permute-start | bytes 12296 | tf_op jit(solution)/shard_map/ppermute | solution.py:236
  81.0 0.8 collective-permute-start.11
  81.8 1.8 %collective-permute-start.10 = (f32[1,1024]{1,0:T(1,128)S(1)}, f32[1,1024]{1,0:T(1,128)S(1)}, u32[]{:S(2)}, u32[]{:S(2)}) collective-permute-start(f32[1,1024]{1,0:T(1,128)S(1)} %get-tuple-element.34), channel_id=1, source_target_pairs={{0,4},{1,5},{2,6},{3,7},{4,0},{5,1},{6,2},{7,3},{8,12},{9,13},{10,... | collective-permute-start | bytes 12296 | tf_op jit(solution)/shard_map/ppermute | solution.py:236
  83.6 1.2 %shard_map.60 = (f32[16,2048]{1,0:T(8,128)S(1)}, f32[16,2048]{1,0:T(8,128)S(1)}) custom-call(f32[16,544,128]{2,1,0:T(8,128)} %all-to-all-done.low_ref.high_ref, f32[16,544,128]{2,1,0:T(8,128)} %all-to-all-done.low_ref.high_ref), custom_call_target="tpu_custom_call" | custom-call | bytes 262144 | tf_op jit(solution)/shard_map/pallas_call | solution.py:133
  84.8 4.0 %collective-permute-start.12 = (f32[16,2048]{1,0:T(8,128)S(1)}, f32[16,2048]{1,0:T(8,128)S(1)}, u32[]{:S(2)}, u32[]{:S(2)}) collective-permute-start(f32[16,2048]{1,0:T(8,128)S(1)} %get-tuple-element.22), channel_id=1, source_target_pairs={{0,16},{16,32},{32,48},{48,64},{64,80},{80,96},{96,112},{1,17},{17... | collective-permute-start | bytes 393224 | tf_op jit(solution)/shard_map/ppermute | solution.py:277
  88.8 4.3 %collective-permute-start.13 = (f32[16,2048]{1,0:T(8,128)S(1)}, f32[16,2048]{1,0:T(8,128)S(1)}, u32[]{:S(2)}, u32[]{:S(2)}) collective-permute-start(f32[16,2048]{1,0:T(8,128)S(1)} %get-tuple-element.23), channel_id=1, source_target_pairs={{16,0},{32,16},{48,32},{64,48},{80,64},{96,80},{112,96},{17,1},{33... | collective-permute-start | bytes 393224 | tf_op jit(solution)/shard_map/ppermute | solution.py:277
  93.1 7.3 %shard_map.59 = (f32[16,32,2048]{2,1,0:T(8,128)}, f32[16,32,2048]{2,1,0:T(8,128)}, f32[2,16,8,2048]{3,2,1,0:T(8,128)S(1)}) custom-call(f32[16,17,32,128]{3,2,1,0:T(8,128)} %bitcast.19.x_ref.v_ref, f32[16,17,32,128]{3,2,1,0:T(8,128)} %bitcast.19.x_ref.v_ref), custom_call_target="tpu_custom_call" | custom-call | bytes 12582912 | tf_op jit(solution)/shard_map/pallas_call | solution.py:183
  100.4 0.0 collective-permute-done.9
  100.4 0.0 collective-permute-done.11
  100.4 0.0 collective-permute-done.10
  100.4 0.6 fusion.4
  101.0 0.0 collective-permute-done.12.before_ref
  101.0 0.0 collective-permute-done.13.after_ref
  101.0 1.6 %shard_map.61 = f32[16,32,2048]{2,1,0:T(8,128)} custom-call(f32[16,2048]{1,0:T(8,128)S(1)} %collective-permute-done.12.before_ref, f32[16,2048]{1,0:T(8,128)S(1)} %collective-permute-done.13.after_ref, f32[2,16,8,2048]{3,2,1,0:T(8,128)S(1)} %get-tuple-element.24.sides_ref, f32[16,32,2048]{2,1,0:T(8,128)} %get-tuple-element.25.applied_ref), custom_call_target="tpu_custom_call", output_to_operand_aliasing={{}: (3, {})} | custom-call | bytes 1048576 | tf_op jit(solution)/shard_map/pallas_call | solution.py:219
  (9 shorter events, 0.2 us)
Async XLA Ops:
  0.6 2.2 %copy-start.1 = (f32[256,2,2048]{2,1,0:T(2,128)S(1)}, f32[256,2,2048]{2,1,0:T(2,128)}, u32[]{:S(2)}) copy-start(f32[256,2,2048]{2,1,0:T(2,128)} %param.2) | copy-start | bytes 12582916
  2.8 0.7 copy-start.3
  5.0 2.1 %copy-start = (f32[16,544,128]{2,1,0:T(8,128)}, f32[16,544,128]{2,1,0:T(8,128)S(1)}, u32[]{:S(2)}) copy-start(f32[16,544,128]{2,1,0:T(8,128)S(1)} %get-tuple-element.19) | copy-start | bytes 13369348
  7.1 31.4 %collective-permute-start = (f32[2048,128]{1,0:T(8,128)}, f32[2048,128]{1,0:T(8,128)S(1)}, u32[]{:S(2)}, u32[]{:S(2)}) collective-permute-start(f32[2048,128]{1,0:T(8,128)} %get-tuple-element.15), channel_id=1, source_target_pairs={{1,0},{2,1},{3,2},{4,3},{5,4},{6,5},{7,6},{8,7},{9,8},{10,9},{11,1... | collective-permute-start | bytes 3145736 | tf_op jit(solution)/shard_map/ppermute | solution.py:264
  14.8 37.5 %collective-permute-start.1 = (f32[2048,128]{1,0:T(8,128)S(1)}, f32[2048,128]{1,0:T(8,128)S(1)}, u32[]{:S(2)}, u32[]{:S(2)}) collective-permute-start(f32[2048,128]{1,0:T(8,128)S(1)} %get-tuple-element.16), channel_id=1, source_target_pairs={{0,1},{1,2},{2,3},{3,4},{4,5},{5,6},{6,7},{7,8},{8,9},{9,10},{10,1... | collective-permute-start | bytes 3145736 | tf_op jit(solution)/shard_map/ppermute | solution.py:265
  16.8 35.5 %copy-start.4 = (f32[2,2048]{1,0:T(2,128)S(1)}, f32[2,2048]{1,0:T(2,128)}, u32[]{:S(2)}) copy-start(f32[2,2048]{1,0:T(2,128)} %param.3) | copy-start | bytes 49156
  16.8 62.6 %all-to-all-start = ((f32[16,544,128]{2,1,0:T(8,128)}), f32[16,544,128]{2,1,0:T(8,128)}, u32[]{:S(2)}, u32[]{:S(2)}) async-start(f32[16,544,128]{2,1,0:T(8,128)} %copy-done), calls=%async_computation | async-start | bytes 8912896 | tf_op jit(solution)/shard_map/all_to_all | solution.py:266
  52.3 2.2 %copy-start.2 = (f32[256,2,2048]{2,1,0:T(2,128)S(1)}, f32[256,2,2048]{2,1,0:T(2,128)}, u32[]{:S(2)}) copy-start(f32[256,2,2048]{2,1,0:T(2,128)} %param.2) | copy-start | bytes 12582916
  60.1 1.6 %collective-permute-start.2 = (f32[64,1024]{1,0:T(8,128)S(1)}, f32[64,1024]{1,0:T(8,128)S(1)}, u32[]{:S(2)}, u32[]{:S(2)}) collective-permute-start(f32[64,1024]{1,0:T(8,128)S(1)} %get-tuple-element.18), channel_id=1, source_target_pairs={{0,1},{1,0},{2,3},{3,2},{4,5},{5,4},{6,7},{7,6},{8,9},{9,8},{10,11... | collective-permute-start | bytes 786440 | tf_op jit(solution)/shard_map/ppermute | solution.py:236
  61.8 4.3 %collective-permute-start.3 = (f32[16,1024]{1,0:T(8,128)S(1)}, f32[16,1024]{1,0:T(8,128)S(1)}, u32[]{:S(2)}, u32[]{:S(2)}) collective-permute-start(f32[16,1024]{1,0:T(8,128)S(1)} %get-tuple-element.26), channel_id=1, source_target_pairs={{0,32},{1,33},{2,34},{3,35},{4,36},{5,37},{6,38},{7,39},{8,40},{9,... | collective-permute-start | bytes 196616 | tf_op jit(solution)/shard_map/ppermute | solution.py:236
  62.3 6.2 %collective-permute-start.5 = (f32[16,1024]{1,0:T(8,128)S(1)}, f32[16,1024]{1,0:T(8,128)S(1)}, u32[]{:S(2)}, u32[]{:S(2)}) collective-permute-start(f32[16,1024]{1,0:T(8,128)S(1)} %get-tuple-element.27), channel_id=1, source_target_pairs={{0,96},{1,97},{2,98},{3,99},{4,100},{5,101},{6,102},{7,103},{8,104... | collective-permute-start | bytes 196616 | tf_op jit(solution)/shard_map/ppermute | solution.py:236
  63.4 5.8 %collective-permute-start.4 = (f32[16,1024]{1,0:T(8,128)S(1)}, f32[16,1024]{1,0:T(8,128)S(1)}, u32[]{:S(2)}, u32[]{:S(2)}) collective-permute-start(f32[16,1024]{1,0:T(8,128)S(1)} %get-tuple-element.28), channel_id=1, source_target_pairs={{0,64},{1,65},{2,66},{3,67},{4,68},{5,69},{6,70},{7,71},{8,72},{9,... | collective-permute-start | bytes 196616 | tf_op jit(solution)/shard_map/ppermute | solution.py:236
  69.2 4.2 %collective-permute-start.6 = (f32[4,1024]{1,0:T(4,128)S(1)}, f32[4,1024]{1,0:T(4,128)S(1)}, u32[]{:S(2)}, u32[]{:S(2)}) collective-permute-start(f32[4,1024]{1,0:T(4,128)S(1)} %get-tuple-element.29), channel_id=1, source_target_pairs={{0,8},{1,9},{2,10},{3,11},{4,12},{5,13},{6,14},{7,15},{8,0},{9,1},... | collective-permute-start | bytes 49160 | tf_op jit(solution)/shard_map/ppermute | solution.py:236
  69.3 5.0 %collective-permute-start.8 = (f32[4,1024]{1,0:T(4,128)S(1)}, f32[4,1024]{1,0:T(4,128)S(1)}, u32[]{:S(2)}, u32[]{:S(2)}) collective-permute-start(f32[4,1024]{1,0:T(4,128)S(1)} %get-tuple-element.30), channel_id=1, source_target_pairs={{0,24},{1,25},{2,26},{3,27},{4,28},{5,29},{6,30},{7,31},{8,16},{9,... | collective-permute-start | bytes 49160 | tf_op jit(solution)/shard_map/ppermute | solution.py:236
  69.4 8.8 %collective-permute-start.7 = (f32[4,1024]{1,0:T(4,128)S(1)}, f32[4,1024]{1,0:T(4,128)S(1)}, u32[]{:S(2)}, u32[]{:S(2)}) collective-permute-start(f32[4,1024]{1,0:T(4,128)S(1)} %get-tuple-element.31), channel_id=1, source_target_pairs={{0,16},{1,17},{2,18},{3,19},{4,20},{5,21},{6,22},{7,23},{8,24},{9,... | collective-permute-start | bytes 49160 | tf_op jit(solution)/shard_map/ppermute | solution.py:236
  79.4 20.9 %collective-permute-start.9 = (f32[1,1024]{1,0:T(1,128)S(1)}, f32[1,1024]{1,0:T(1,128)S(1)}, u32[]{:S(2)}, u32[]{:S(2)}) collective-permute-start(f32[1,1024]{1,0:T(1,128)S(1)} %get-tuple-element.32), channel_id=1, source_target_pairs={{0,2},{1,3},{2,0},{3,1},{4,6},{5,7},{6,4},{7,5},{8,10},{9,11},{10,... | collective-permute-start | bytes 12296 | tf_op jit(solution)/shard_map/ppermute | solution.py:236
  81.0 19.4 %collective-permute-start.11 = (f32[1,1024]{1,0:T(1,128)S(1)}, f32[1,1024]{1,0:T(1,128)S(1)}, u32[]{:S(2)}, u32[]{:S(2)}) collective-permute-start(f32[1,1024]{1,0:T(1,128)S(1)} %get-tuple-element.33), channel_id=1, source_target_pairs={{0,6},{1,7},{2,4},{3,5},{4,2},{5,3},{6,0},{7,1},{8,14},{9,15},{10,... | collective-permute-start | bytes 12296 | tf_op jit(solution)/shard_map/ppermute | solution.py:236
  81.8 18.6 %collective-permute-start.10 = (f32[1,1024]{1,0:T(1,128)S(1)}, f32[1,1024]{1,0:T(1,128)S(1)}, u32[]{:S(2)}, u32[]{:S(2)}) collective-permute-start(f32[1,1024]{1,0:T(1,128)S(1)} %get-tuple-element.34), channel_id=1, source_target_pairs={{0,4},{1,5},{2,6},{3,7},{4,0},{5,1},{6,2},{7,3},{8,12},{9,13},{10,... | collective-permute-start | bytes 12296 | tf_op jit(solution)/shard_map/ppermute | solution.py:236
  84.8 16.2 %collective-permute-start.12 = (f32[16,2048]{1,0:T(8,128)S(1)}, f32[16,2048]{1,0:T(8,128)S(1)}, u32[]{:S(2)}, u32[]{:S(2)}) collective-permute-start(f32[16,2048]{1,0:T(8,128)S(1)} %get-tuple-element.22), channel_id=1, source_target_pairs={{0,16},{16,32},{32,48},{48,64},{64,80},{80,96},{96,112},{1,17},{17... | collective-permute-start | bytes 393224 | tf_op jit(solution)/shard_map/ppermute | solution.py:277
  88.8 12.2 %collective-permute-start.13 = (f32[16,2048]{1,0:T(8,128)S(1)}, f32[16,2048]{1,0:T(8,128)S(1)}, u32[]{:S(2)}, u32[]{:S(2)}) collective-permute-start(f32[16,2048]{1,0:T(8,128)S(1)} %get-tuple-element.23), channel_id=1, source_target_pairs={{16,0},{32,16},{48,32},{64,48},{80,64},{96,80},{112,96},{17,1},{33... | collective-permute-start | bytes 393224 | tf_op jit(solution)/shard_map/ppermute | solution.py:277

commit v3 on v2

--- a/solution.py
+++ b/solution.py
@@ -25,33 +25,41 @@
     return high, (x - high.astype(jnp.float32)).astype(jnp.bfloat16)
 
 
-def extract_kernel(count, rows, x_ref, v_ref, first_ref, last_ref, packed_ref):
+def extract_kernel(count, rows, x_ref, *refs):
     half = rows // 4
-    for o in range(count):
-        first_ref[pl.ds(o * half, half), :] = x_ref[pl.ds(o * rows, half, stride=2), :]
-        last_ref[pl.ds(o * half, half), :] = x_ref[pl.ds(o * rows + 2 * half + 1, half, stride=2), :]
-    parts, length = packed_ref.shape[0], count // packed_ref.shape[0] * rows
-    for c in range(parts):
-        packed_ref[c, :length] = x_ref[pl.ds(c * length, length), :]
-        packed_ref[c, length:] = v_ref[...]
-
-
-def extract(x, v, count, rows, parts):
-    half = jax.ShapeDtypeStruct((count * rows // 4, LANES), jnp.float32)
-    packed = jax.ShapeDtypeStruct((parts, (count // parts + 1) * rows, LANES), jnp.float32)
+    far = 2 * half
+
+    def run(*starts):
+        for o in range(count):
+            for ref, start in zip(refs, starts):
+                ref[pl.ds(o * half, half), :] = x_ref[pl.ds(o * rows + start, half, stride=2), :]
+
+    core = lax.rem(lax.axis_index("col"), 2)
+    pl.when(core == 0)(lambda: run(far + 1, 0, 1, far))
+    pl.when(core == 1)(lambda: run(0, far + 1, far, 1))
+
+
+def extract(x, count, rows):
+    half = pltpu.VMEM((count * rows // 4, LANES), jnp.float32)
     return pl.pallas_call(
         functools.partial(extract_kernel, count, rows),
-        in_specs=[pl.BlockSpec(memory_space=pltpu.VMEM)] * 2,
-        out_specs=[pl.BlockSpec(memory_space=pltpu.VMEM)] * 3,
-        out_shape=[half, half, packed],
-        compiler_params=pltpu.CompilerParams(vmem_limit_bytes=16 * 2**20),
-        cost_estimate=pl.CostEstimate(flops=0, bytes_accessed=count * rows * LANES * 10, transcendentals=0),
-    )(x, v)
-
-
-def gram_kernel(count, rows, scale, x_ref, v_ref, after_ref, before_ref, keep_ref, send_ref, work_ref):
+        in_specs=[pl.BlockSpec(memory_space=pltpu.VMEM)],
+        out_specs=[pl.BlockSpec(memory_space=pltpu.VMEM)] * 4,
+        out_shape=[half] * 4,
+        compiler_params=pltpu.CompilerParams(vmem_limit_bytes=10 * 2**20),
+        cost_estimate=pl.CostEstimate(flops=0, bytes_accessed=count * rows * LANES * 8, transcendentals=0),
+    )(x)
+
+
+def three_passes(a, b):
+    a_high, a_low = split(a)
+    b_high, b_low = split(b)
+    dot = functools.partial(lax.dot_general, dimension_numbers=NT, preferred_element_type=jnp.float32)
+    return dot(a_high, b_high) + dot(a_high, b_low) + dot(a_low, b_high)
+
+
+def gram_kernel(count, rows, x_ref, v_ref, g_ref):
     tiles = rows // 2
-    half = tiles // 2
     lane = lax.broadcasted_iota(jnp.int32, (count, LANES), 1)
 
     def load(t, p):
@@ -72,10 +80,6 @@
                 beside = jnp.where(lane == LANES - 1, later[p], now[p])
                 if p == 0:
                     beside = beside + here[1]
-                if p == 1 and t < half:
-                    beside = beside + after_ref[pl.ds(t, count, stride=half), :]
-                if p == 0 and t >= half:
-                    beside = beside + before_ref[pl.ds(t - half, count, stride=half), :]
                 factor = 1.0 + 0.5 * v_ref[pl.ds(2 * t + p, 1), :]
                 xs.append(here[p])
                 bs.append(factor * here[p] - 0.5 * beside)
@@ -89,7 +93,33 @@
         with_self = a if with_self is None else with_self + a
         with_low = l if with_low is None else with_low + l
         with_half = q if with_half is None else with_half + q
-    first = (with_self + with_low + with_low.T) * scale
+    g_ref[:, :count] = with_self + with_low + with_low.T
+    g_ref[:, count:] = with_half
+
+
+def gram(x, v, count, rows):
+    return pl.pallas_call(
+        functools.partial(gram_kernel, count, rows),
+        out_shape=jax.ShapeDtypeStruct((count, 2 * count), jnp.float32),
+        in_specs=[pl.BlockSpec(memory_space=pltpu.VMEM)] * 2,
+        out_specs=pl.BlockSpec(memory_space=pltpu.VMEM),
+        compiler_params=pltpu.CompilerParams(vmem_limit_bytes=16 * 2**20),
+        cost_estimate=pl.CostEstimate(
+            flops=400 * count * count * rows * LANES, bytes_accessed=count * rows * LANES * 6, transcendentals=0
+        ),
+    )(x, v)
+
+
+def finish_kernel(count, rows, scale, g_ref, by_core_ref, core_ref, by_chip_ref, chip_ref, *refs):
+    keep_ref, send_ref, work_ref = refs
+    half = rows // 4
+
+    def load(ref):
+        return jnp.concatenate([ref[pl.ds(t, count, stride=half), :] for t in range(half)], axis=1)
+
+    beside = three_passes(load(by_core_ref), load(core_ref)) + three_passes(load(by_chip_ref), load(chip_ref))
+    with_half = g_ref[:, count:] - 0.5 * beside
+    first = g_ref[:, :count] * scale
     second = (with_half + with_half.T) * scale
     blocks = count // LANES
     for m, matrix in enumerate((first, second)):
@@ -105,26 +135,37 @@
                 ]
 
 
-def gram(x, v, after, before, count, rows, scale):
+def finish(g, by_core, from_core, by_chip, from_chip, count, rows, scale):
     part = jax.ShapeDtypeStruct((count // 4, 4 * count), jnp.float32)
     return pl.pallas_call(
-        functools.partial(gram_kernel, count, rows, scale),
+        functools.partial(finish_kernel, count, rows, scale),
         out_shape=[part, part],
-        in_specs=[pl.BlockSpec(memory_space=pltpu.VMEM)] * 4,
+        in_specs=[pl.BlockSpec(memory_space=pltpu.VMEM)] * 5,
         out_specs=[pl.BlockSpec(memory_space=pltpu.VMEM)] * 2,
         scratch_shapes=[pltpu.VMEM((2 * count // LANES, count, LANES), jnp.float32)],
         compiler_params=pltpu.CompilerParams(vmem_limit_bytes=16 * 2**20),
         cost_estimate=pl.CostEstimate(
-            flops=400 * count * count * rows * LANES, bytes_accessed=count * rows * LANES * 6, transcendentals=0
+            flops=3 * count * count * rows * LANES, bytes_accessed=count * rows * LANES * 4, transcendentals=0
         ),
-    )(x, v, after, before)
-
-
-def edges_kernel(orbitals, rows, low_ref, high_ref, first_ref, last_ref):
-    for t in range(rows // 2):
-        lanes = pl.ds(t * LANES, LANES)
-        first_ref[:, lanes] = low_ref[0, pl.ds(2 * t, orbitals, stride=rows), :]
-        last_ref[:, lanes] = high_ref[0, pl.ds(2 * t + 1, orbitals, stride=rows), :]
+    )(g, by_core, from_core, by_chip, from_chip)
+
+
+def edges_kernel(orbitals, rows, low_ref, high_ref, near_ref, far_ref):
+    def take(ref, source_ref, start):
+        for t in range(rows // 2):
+            ref[:, pl.ds(t * LANES, LANES)] = source_ref[0, pl.ds(start + 2 * t, orbitals, stride=rows), :]
+
+    even = lax.rem(lax.axis_index("row"), 2) == 0
+
+    @pl.when(even)
+    def _():
+        take(near_ref, high_ref, 1)
+        take(far_ref, low_ref, 0)
+
+    @pl.when(jnp.logical_not(even))
+    def _():
+        take(near_ref, low_ref, 0)
+        take(far_ref, high_ref, 1)
 
 
 def edges_of(received, orbitals, rows):
@@ -144,7 +185,8 @@
     )(received, received)
 
 
-def block_kernel(sources, block, rows, x_ref, v_ref, out_ref, applied_ref, sides_ref, v_scr, work_ref):
+def block_kernel(sources, block, rows, x_ref, v_own_ref, v1_ref, v2_ref, v3_ref, out_ref, applied_ref, sides_ref, *refs):
+    v_scr, v_held_ref, work_ref = refs
     tiles, planes = rows // 2, 2 * sources
     points = tiles * LANES
 
@@ -158,7 +200,13 @@
 
     @pl.when(pl.program_id(0) == 0)
     def _():
-        v_scr[...] = 2.0 + interleaved(v_ref.reshape(sources * rows, LANES), 0, rows, work_ref.at[0])
+        column = lax.axis_index("col")
+        for b, ref in enumerate((v_own_ref, v1_ref, v2_ref, v3_ref)):
+            for a in (0, 1):
+                for c in (0, 1):
+                    start = ref.shape[0] + (2 * a + c - 4) * rows
+                    v_held_ref[column ^ (8 * a + 2 * b + c)] = ref[pl.ds(start, rows), :]
+        v_scr[...] = 2.0 + interleaved(v_held_ref.reshape(sources * rows, LANES), 0, rows, work_ref.at[0])
 
     flat = x_ref.reshape(sources * block * rows, LANES)
     row = lax.broadcasted_iota(jnp.int32, (planes, points), 0)
@@ -175,38 +223,47 @@
         sides_ref[1, at] = applied[planes - 8 :]
 
 
-def to_block(received, orbitals, rows):
+def to_block(received, v_parts, orbitals, rows):
     block, sources = 4, received.shape[0]
     planes, points = 2 * sources, rows // 2 * LANES
-    received = received.reshape(sources, orbitals + 1, rows, LANES)
+    received = received.reshape(sources, orbitals, rows, LANES)
     out = jax.ShapeDtypeStruct((orbitals, planes, points), jnp.float32)
     return pl.pallas_call(
         functools.partial(block_kernel, sources, block, rows),
         grid=(orbitals // block,),
         in_specs=[
             pl.BlockSpec((sources, block, rows, LANES), lambda i: (0, i, 0, 0)),
-            pl.BlockSpec((sources, 1, rows, LANES), lambda i: (0, orbitals, 0, 0)),
+            *[pl.BlockSpec(part.shape, lambda i: (0, 0)) for part in v_parts],
         ],
         out_specs=[pl.BlockSpec((block, planes, points), lambda i: (i, 0, 0))] * 2
         + [pl.BlockSpec(memory_space=pltpu.VMEM)],
         out_shape=[out, out, jax.ShapeDtypeStruct((2, orbitals, 8, points), jnp.float32)],
         scratch_shapes=[
             pltpu.VMEM((planes, points), jnp.float32),
+            pltpu.VMEM((sources, rows, LANES), jnp.float32),
             pltpu.VMEM((block, planes * points // LANES, LANES), jnp.float32),
         ],
         compiler_params=pltpu.CompilerParams(vmem_limit_bytes=24 * 2**20),
         cost_estimate=pl.CostEstimate(flops=0, bytes_accessed=12 * orbitals * planes * points, transcendentals=0),
-    )(received, received)
-
-
-def fix_kernel(before_ref, after_ref, sides_ref, applied_ref, out_ref, work_ref, sem):
+    )(received, *v_parts)
+
+
+def fix_kernel(near_ref, far_ref, sides_ref, applied_ref, out_ref, work_ref, sem):
     orbitals, planes, _ = applied_ref.shape
+
+    def run(edge_refs):
+        for e, edge_ref in enumerate(edge_refs):
+            for o in range(orbitals):
+                row = 7 * e
+                work_ref[e, o] = sides_ref[e, o]
+                work_ref[e, o, pl.ds(row, 1), :] = sides_ref[e, o, pl.ds(row, 1), :] - 0.5 * edge_ref[pl.ds(o, 1), :]
+
+    even = lax.rem(lax.axis_index("row"), 2) == 0
+    pl.when(even)(lambda: run((far_ref, near_ref)))
+    pl.when(jnp.logical_not(even))(lambda: run((near_ref, far_ref)))
     copies = []
-    for e, edge_ref in enumerate((before_ref, after_ref)):
+    for e in (0, 1):
         for o in range(orbitals):
-            row = 7 * e
-            work_ref[e, o] = sides_ref[e, o]
-            work_ref[e, o, pl.ds(row, 1), :] = sides_ref[e, o, pl.ds(row, 1), :] - 0.5 * edge_ref[pl.ds(o, 1), :]
             target = out_ref.at[o, pl.ds(e * (planes - 8), 8), :]
             copies.append(pltpu.make_async_copy(work_ref.at[e, o], target, sem.at[e, o]))
             copies[-1].start()
@@ -214,7 +271,7 @@
         copy.wait()
 
 
-def fix_edges(applied, sides, before, after):
+def fix_edges(applied, sides, near, far):
     orbitals, _, points = applied.shape
     return pl.pallas_call(
         fix_kernel,
@@ -228,7 +285,7 @@
         ],
         compiler_params=pltpu.CompilerParams(vmem_limit_bytes=12 * 2**20),
         cost_estimate=pl.CostEstimate(flops=0, bytes_accessed=32 * orbitals * points, transcendentals=0),
-    )(before, after, sides, applied)
+    )(near, far, sides, applied)
 
 
 def exchange(x, mask):
@@ -246,6 +303,31 @@
     pick = lambda k: lax.dynamic_index_in_dim(parts, mine ^ k, 0, keepdims=False)
     sent = [exchange(pick(k), k * position) for k in (1, 2, 3)]
     return pick(0) + sent[0] + sent[1] + sent[2]
+
+
+def reduce_z_hi(total):
+    parts = total.reshape(2, -1, total.shape[-1])
+    mine = digit(16, 2)
+    pick = lambda k: lax.dynamic_index_in_dim(parts, mine ^ k, 0, keepdims=False)
+    z = lambda i: i // 8 % 4
+    pairs = [(i, i + 8 * (3 - 2 * z(i))) for i in range(lax.axis_size(("row", "col")))]
+    return pick(0) + lax.ppermute(pick(1), ("row", "col"), pairs)
+
+
+def reduce_chips(total, v):
+    total = total.reshape(8, -1, LANES)
+    height = total.shape[1]
+
+    def pick(x, mine, k):
+        return lax.dynamic_index_in_dim(x, mine ^ k, 0, keepdims=False).reshape(-1, LANES)
+
+    z, x = digit(8, 2), digit(2, 4)
+    pair = total.reshape(2, 4, height, LANES)
+    got = exchange(jnp.concatenate([pick(pair, z, 1), v]), 8)
+    total = (pick(pair, z, 0) + got[: 4 * height]).reshape(4, height, LANES)
+    v = jnp.concatenate([v, got[4 * height :]])
+    got = [exchange(jnp.concatenate([pick(total, x, k), v]), 2 * k) for k in (1, 2, 3)]
+    return sum([part[:height] for part in got], pick(total, x, 0)), [v, *got]
 
 
 def local(orbitals, potential):
@@ -255,28 +337,29 @@
     rows = planes * points // LANES
     mine = count // n_col
     scale = 1.0 / (devices * planes * points)
-    forward = [(i, i + 1) for i in range(devices - 1)]
-    backward = [(j, i) for i, j in forward]
 
     tiled = tile_view(orbitals).reshape(count * rows, LANES)
     v = tile_view(potential)
-    first, last, packed = extract(tiled, v, count, rows, n_col)
-    after = lax.ppermute(first, every, backward)
-    before = lax.ppermute(last, every, forward)
-    received = lax.all_to_all(packed, "col", split_axis=0, concat_axis=0, tiled=True)
-
-    keep, send = gram(tiled, v, after, before, count, rows, scale)
+    to_core, to_chip, by_core, by_chip = extract(tiled, count, rows)
+    orbitals, to_core, to_chip, v = lax.optimization_barrier((orbitals, to_core, to_chip, v))
+    from_core = exchange(to_core, 1)
+    from_chip = lax.ppermute(to_chip, every, [(i, (i + 1 ^ 1) - 1) for i in range(1, devices - 1)])
+    received = lax.all_to_all(orbitals, "col", split_axis=0, concat_axis=0, tiled=True)
+    received = tile_view(received.reshape(n_col, mine, planes, points)).reshape(n_col, mine * rows, LANES)
+
+    g = gram(tiled, v, count, rows)
+    keep, send = finish(g, by_core, from_core, by_chip, from_chip, count, rows, scale)
+    v = jnp.concatenate([v, exchange(v, 1)])
     g = reduce_digit(keep + exchange(send, 1), 32)
-    g = reduce_digit(g, 8)
-    g, _ = lax.optimization_barrier((g, received))
-    g = reduce_digit(g, 2).reshape(planes, 2 * count)
-
-    up = [(i, i + 1) for i in range(n_row - 1)]
-    down = [(j, i) for i, j in up]
-    first, last = edges_of(received, mine, rows)
-    before, after = lax.ppermute(last, "row", up), lax.ppermute(first, "row", down)
-    relayed, applied, sides = to_block(received, mine, rows)
-    return g[:, :count], g[:, count:], relayed, fix_edges(applied, sides, before, after)
+    g = reduce_z_hi(g)
+    g, v_parts = reduce_chips(g, v)
+    g = g.reshape(planes, 2 * count)
+
+    near, far = edges_of(received, mine, rows)
+    near = lax.ppermute(near, "row", [(i, i ^ 1) for i in range(n_row)])
+    far = lax.ppermute(far, "row", [(i, (i + 1 ^ 1) - 1) for i in range(1, n_row - 1)])
+    relayed, applied, sides = to_block(received, v_parts, mine, rows)
+    return g[:, :count], g[:, count:], relayed, fix_edges(applied, sides, near, far)
 
 
 def solution(mesh):

time: 103 us -> 96.2 us (0.934)
  the two profiles are of different devices: /device:TPU:24 before, /device:TPU:8 now
where the time goes in v3:
time: 96.2 us; the launch traced here: 95.8 us
  waiting for transfers between devices  36.7 us (38%)
  starting transfers between devices  32.3 us (34%)
  Pallas kernels  20.7 us (22%)
  local copies, waits for them, and re-layouts  5.06 us (5%)
    ppermute x1, waiting for transfers between devices, local(): lax.ppermute(to_chip, every, [(i, (i + 1 ^ 1) - 1) for i in range(1, devi...  18.9 us
    ppermute x10, waiting for transfers between devices, exchange(): lax.ppermute(x, every, [(i, i ^ mask) for i in range(lax.axis_size(every))])  15.9 us
    ppermute x10, starting transfers between devices, exchange(): lax.ppermute(x, every, [(i, i ^ mask) for i in range(lax.axis_size(every))])  8.44 us
    ppermute x1, starting transfers between devices, local(): lax.ppermute(to_chip, every, [(i, (i + 1 ^ 1) - 1) for i in range(1, devi...  8.13 us
    pallas_call x1, Pallas kernels, to_block(): pl.pallas_call(functools.partial(block_kernel, sources, block, rows), gri...  7.46 us
    pallas_call x1, Pallas kernels, gram(): pl.pallas_call(functools.partial(gram_kernel, count, rows), out_shape=jax...  5.17 us
    all_to_all x1, starting transfers between devices, local(): lax.all_to_all(orbitals, 'col', split_axis=0, concat_axis=0, tiled=True)  4.56 us
    ppermute x1, starting transfers between devices, local(): lax.ppermute(far, 'row', [(i, (i + 1 ^ 1) - 1) for i in range(1, n_row -...  4.46 us
  transfers between devices with their start and end apart: 15, of which 8 were waited for; matrix products, arithmetic and copies ran while one was open for 1% of the time, Pallas kernels for 17%

profile of v3, /device:TPU:8, one launch (start us, length us, event | category | flops | bytes accessed | tf_op | source)
XLA Modules:
  0.0 95.8 jit_solution(11925445597524889387)
XLA Ops:
  0.6 0.0 copy-start
  0.6 2.2 %copy-done = f32[256,2,2048]{2,1,0:T(2,128)S(1)} copy-done((f32[256,2,2048]{2,1,0:T(2,128)S(1)}, f32[256,2,2048]{2,1,0:T(2,128)}, u32[]{:S(2)}) %copy-start) | copy-done | bytes 4194328
  2.8 1.6 %shard_map.57 = (f32[2048,128]{1,0:T(8,128)}, f32[2048,128]{1,0:T(8,128)}, f32[2048,128]{1,0:T(8,128)S(1)}, f32[2048,128]{1,0:T(8,128)S(1)}) custom-call(f32[8192,128]{1,0:T(8,128)S(1)} %bitcast.58), custom_call_target="tpu_custom_call" | custom-call | bytes 8388608 | tf_op jit(solution)/shard_map/pallas_call | solution.py:44
  4.4 0.0 copy-start.2
  4.4 0.0 collective-permute-start
  4.4 8.1 %collective-permute-start.1 = (f32[2048,128]{1,0:T(8,128)}, f32[2048,128]{1,0:T(8,128)}, u32[]{:S(2)}, u32[]{:S(2)}) collective-permute-start(f32[2048,128]{1,0:T(8,128)} %get-tuple-element.25), channel_id=1, source_target_pairs={{1,2},{2,1},{3,4},{4,3},{5,6},{6,5},{7,8},{8,7},{9,10},{10,9},{11,... | collective-permute-start | bytes 3145736 | tf_op jit(solution)/shard_map/ppermute | solution.py:346
  12.6 4.6 %all-to-all-start = ((f32[256,2,2048]{2,1,0:T(2,128)}), f32[256,2,2048]{2,1,0:T(2,128)}, u32[]{:S(2)}, u32[]{:S(2)}) async-start(f32[256,2,2048]{2,1,0:T(2,128)} %param.2), calls=%async_computation | async-start | bytes 8388608 | tf_op jit(solution)/shard_map/all_to_all | solution.py:347
  17.1 0.0 copy-done.2
  17.1 0.0 copy-start.1
  17.1 2.2 %copy-done.1 = f32[256,2,2048]{2,1,0:T(2,128)S(1)} copy-done((f32[256,2,2048]{2,1,0:T(2,128)S(1)}, f32[256,2,2048]{2,1,0:T(2,128)}, u32[]{:S(2)}) %copy-start.1) | copy-done | bytes 4194328
  19.3 5.2 %shard_map.58.g_ref = f32[256,512]{1,0:T(8,128)S(1)} custom-call(f32[8192,128]{1,0:T(8,128)S(1)} %bitcast.59, f32[32,128]{1,0:T(8,128)S(1)} %bitcast.60), custom_call_target="tpu_custom_call" | custom-call | flops 107374182400 | bytes 6291456 | tf_op jit(solution)/shard_map/pallas_call | solution.py:101
  24.5 0.0 collective-permute-done.core_ref
  24.5 18.9 %collective-permute-done.1.chip_ref = f32[2048,128]{1,0:T(8,128)} collective-permute-done((f32[2048,128]{1,0:T(8,128)}, f32[2048,128]{1,0:T(8,128)}, u32[]{:S(2)}, u32[]{:S(2)}) %collective-permute-start.1) | collective-permute-done | bytes 1048608 | tf_op jit(solution)/shard_map/ppermute | solution.py:346
  43.4 3.5 %shard_map.59 = (f32[64,1024]{1,0:T(8,128)S(1)}, f32[64,1024]{1,0:T(8,128)}) custom-call(f32[256,512]{1,0:T(8,128)S(1)} %shard_map.58.g_ref, f32[2048,128]{1,0:T(8,128)S(1)} %get-tuple-element.22.by_core_ref, f32[2048,128]{1,0:T(8,128)S(1)} %collective-permute-done.core_ref, f32[2048,128]{1,0:T(8,128)S(1)} %get-tuple-element.24.by_chip_ref, ...), custom_call_target="tpu_custom_call" | custom-call | flops 805306368 | bytes 4194304 | tf_op jit(solution)/shard_map/pallas_call | solution.py:140
  46.9 0.0 collective-permute-start.2
  46.9 1.7 %collective-permute-done.2 = f32[64,1024]{1,0:T(8,128)S(1)} collective-permute-done((f32[64,1024]{1,0:T(8,128)}, f32[64,1024]{1,0:T(8,128)S(1)}, u32[]{:S(2)}, u32[]{:S(2)}) %collective-permute-start.2) | collective-permute-done | bytes 262176 | tf_op jit(solution)/shard_map/ppermute | solution.py:293
  48.7 1.7 %collective-permute-start.5 = (f32[16,1024]{1,0:T(8,128)S(1)}, f32[16,1024]{1,0:T(8,128)S(1)}, u32[]{:S(2)}, u32[]{:S(2)}) collective-permute-start(f32[16,1024]{1,0:T(8,128)S(1)} %get-tuple-element.35), channel_id=1, source_target_pairs={{0,96},{1,97},{2,98},{3,99},{4,100},{5,101},{6,102},{7,103},{8,104... | collective-permute-start | bytes 196616 | tf_op jit(solution)/shard_map/ppermute | solution.py:293
  50.4 1.1 %collective-permute-start.4 = (f32[16,1024]{1,0:T(8,128)S(1)}, f32[16,1024]{1,0:T(8,128)S(1)}, u32[]{:S(2)}, u32[]{:S(2)}) collective-permute-start(f32[16,1024]{1,0:T(8,128)S(1)} %get-tuple-element.36), channel_id=1, source_target_pairs={{0,64},{1,65},{2,66},{3,67},{4,68},{5,69},{6,70},{7,71},{8,72},{9,... | collective-permute-start | bytes 196616 | tf_op jit(solution)/shard_map/ppermute | solution.py:293
  51.5 1.4 %collective-permute-start.3 = (f32[16,1024]{1,0:T(8,128)S(1)}, f32[16,1024]{1,0:T(8,128)S(1)}, u32[]{:S(2)}, u32[]{:S(2)}) collective-permute-start(f32[16,1024]{1,0:T(8,128)S(1)} %get-tuple-element.34), channel_id=1, source_target_pairs={{0,32},{1,33},{2,34},{3,35},{4,36},{5,37},{6,38},{7,39},{8,40},{9,... | collective-permute-start | bytes 196616 | tf_op jit(solution)/shard_map/ppermute | solution.py:293
  52.9 0.2 collective-permute-done.5
  53.1 3.6 %collective-permute-done.4 = f32[16,1024]{1,0:T(8,128)S(1)} collective-permute-done((f32[16,1024]{1,0:T(8,128)S(1)}, f32[16,1024]{1,0:T(8,128)S(1)}, u32[]{:S(2)}, u32[]{:S(2)}) %collective-permute-start.4) | collective-permute-done | bytes 65568 | tf_op jit(solution)/shard_map/ppermute | solution.py:293
  56.7 0.0 collective-permute-done.3
  56.7 3.8 %collective-permute-start.6 = (f32[8,1024]{1,0:T(8,128)S(1)}, f32[8,1024]{1,0:T(8,128)S(1)}, u32[]{:S(2)}, u32[]{:S(2)}) collective-permute-start(f32[8,1024]{1,0:T(8,128)S(1)} %dynamic-slice_bitcast_fusion.3), channel_id=1, source_target_pairs={{0,24},{1,25},{2,26},{3,27},{4,28},{5,29},{6,30},{7,31},{8,16},{9,... | collective-permute-start | bytes 98312 | tf_op jit(solution)/shard_map/ppermute | solution.py:314
  60.5 0.0 collective-permute-start.7
  60.5 1.9 %collective-permute-done.6 = f32[8,1024]{1,0:T(8,128)S(1)} collective-permute-done((f32[8,1024]{1,0:T(8,128)S(1)}, f32[8,1024]{1,0:T(8,128)S(1)}, u32[]{:S(2)}, u32[]{:S(2)}) %collective-permute-start.6) | collective-permute-done | bytes 32800 | tf_op jit(solution)/shard_map/ppermute | solution.py:314
  62.5 0.0 collective-permute-done.7
  62.5 0.1 collective-permute-start.8
  62.6 5.8 %collective-permute-done.8 = f32[96,128]{1,0:T(8,128)S(1)} collective-permute-done((f32[96,128]{1,0:T(8,128)S(1)}, f32[96,128]{1,0:T(8,128)S(1)}, u32[]{:S(2)}, u32[]{:S(2)}) %collective-permute-start.8) | collective-permute-done | bytes 49184 | tf_op jit(solution)/shard_map/ppermute | solution.py:293
  68.5 3.0 %collective-permute-start.11 = (f32[136,128]{1,0:T(8,128)S(1)}, f32[136,128]{1,0:T(8,128)S(1)}, u32[]{:S(2)}, u32[]{:S(2)}) collective-permute-start(f32[136,128]{1,0:T(8,128)S(1)} %get-tuple-element.39), channel_id=1, source_target_pairs={{0,6},{1,7},{2,4},{3,5},{4,2},{5,3},{6,0},{7,1},{8,14},{9,15},{10,... | collective-permute-start | bytes 208904 | tf_op jit(solution)/shard_map/ppermute | solution.py:293
  71.5 0.0 collective-permute-start.10
  71.5 1.2 %collective-permute-start.9 = (f32[136,128]{1,0:T(8,128)S(1)}, f32[136,128]{1,0:T(8,128)S(1)}, u32[]{:S(2)}, u32[]{:S(2)}) collective-permute-start(f32[136,128]{1,0:T(8,128)S(1)} %get-tuple-element.37), channel_id=1, source_target_pairs={{0,2},{1,3},{2,0},{3,1},{4,6},{5,7},{6,4},{7,5},{8,10},{9,11},{10,... | collective-permute-start | bytes 208904 | tf_op jit(solution)/shard_map/ppermute | solution.py:293
  72.6 1.7 %collective-permute-done.11.v3_ref = f32[136,128]{1,0:T(8,128)S(1)} collective-permute-done((f32[136,128]{1,0:T(8,128)S(1)}, f32[136,128]{1,0:T(8,128)S(1)}, u32[]{:S(2)}, u32[]{:S(2)}) %collective-permute-start.11) | collective-permute-done | bytes 69664 | tf_op jit(solution)/shard_map/ppermute | solution.py:293
  74.3 2.9 %collective-permute-done.10.v2_ref = f32[136,128]{1,0:T(8,128)S(1)} collective-permute-done((f32[136,128]{1,0:T(8,128)S(1)}, f32[136,128]{1,0:T(8,128)S(1)}, u32[]{:S(2)}, u32[]{:S(2)}) %collective-permute-start.10) | collective-permute-done | bytes 69664 | tf_op jit(solution)/shard_map/ppermute | solution.py:293
  77.3 0.0 collective-permute-done.9.v1_ref
  77.3 0.0 all-to-all-done
  77.3 1.2 %shard_map.61 = (f32[16,2048]{1,0:T(8,128)S(1)}, f32[16,2048]{1,0:T(8,128)S(1)}) custom-call(f32[16,512,128]{2,1,0:T(8,128)} %bitcast.27.low_ref.high_ref, f32[16,512,128]{2,1,0:T(8,128)} %bitcast.27.low_ref.high_ref), custom_call_target="tpu_custom_call" | custom-call | bytes 262144 | tf_op jit(solution)/shard_map/pallas_call | solution.py:174
  78.5 2.9 %collective-permute-start.12 = (f32[16,2048]{1,0:T(8,128)S(1)}, f32[16,2048]{1,0:T(8,128)S(1)}, u32[]{:S(2)}, u32[]{:S(2)}) collective-permute-start(f32[16,2048]{1,0:T(8,128)S(1)} %get-tuple-element.30), channel_id=1, source_target_pairs={{0,16},{16,0},{32,48},{48,32},{64,80},{80,64},{96,112},{112,96},{1... | collective-permute-start | bytes 393224 | tf_op jit(solution)/shard_map/ppermute | solution.py:359
  81.4 4.5 %collective-permute-start.13 = (f32[16,2048]{1,0:T(8,128)S(1)}, f32[16,2048]{1,0:T(8,128)S(1)}, u32[]{:S(2)}, u32[]{:S(2)}) collective-permute-start(f32[16,2048]{1,0:T(8,128)S(1)} %get-tuple-element.31), channel_id=1, source_target_pairs={{16,32},{32,16},{48,64},{64,48},{80,96},{96,80},{17,33},{33,17},{4... | collective-permute-start | bytes 393224 | tf_op jit(solution)/shard_map/ppermute | solution.py:360
  85.9 0.6 fusion.5
  86.4 7.5 %shard_map.60 = (f32[16,32,2048]{2,1,0:T(8,128)}, f32[16,32,2048]{2,1,0:T(8,128)}, f32[2,16,8,2048]{3,2,1,0:T(8,128)S(1)}) custom-call(f32[16,16,32,128]{3,2,1,0:T(8,128)} %bitcast.25.x_ref, f32[128,128]{1,0:T(8,128)S(1)} %pad_maximum_fusion.9.v_own_ref, f32[136,128]{1,0:T(8,128)S(1)} %collective-permute-done.9.v1_ref, ...), custom_call_target="tpu_custom_call" | custom-call | bytes 12582912 | tf_op jit(solution)/shard_map/pallas_call | solution.py:231
  93.9 0.0 collective-permute-done.12.near_ref
  93.9 0.0 collective-permute-done.13.far_ref
  93.9 1.8 %shard_map.62 = f32[16,32,2048]{2,1,0:T(8,128)} custom-call(f32[16,2048]{1,0:T(8,128)S(1)} %collective-permute-done.12.near_ref, f32[16,2048]{1,0:T(8,128)S(1)} %collective-permute-done.13.far_ref, f32[2,16,8,2048]{3,2,1,0:T(8,128)S(1)} %get-tuple-element.32.sides_ref, f32[16,32,2048]{2,1,0:T(8,128)} %get-tuple-element.33.applied_ref), custom_call_target="tpu_custom_call", output_to_operand_aliasing={{}: (3, {})} | custom-call | bytes 1048576 | tf_op jit(solution)/shard_map/pallas_call | solution.py:276
  (15 shorter events, 0.2 us)
Async XLA Ops:
  0.6 2.2 %copy-start = (f32[256,2,2048]{2,1,0:T(2,128)S(1)}, f32[256,2,2048]{2,1,0:T(2,128)}, u32[]{:S(2)}) copy-start(f32[256,2,2048]{2,1,0:T(2,128)} %param.2) | copy-start | bytes 12582916
  4.4 12.7 %copy-start.2 = (f32[2,2048]{1,0:T(2,128)S(1)}, f32[2,2048]{1,0:T(2,128)}, u32[]{:S(2)}) copy-start(f32[2,2048]{1,0:T(2,128)} %param.3) | copy-start | bytes 49156
  4.4 20.1 %collective-permute-start = (f32[2048,128]{1,0:T(8,128)}, f32[2048,128]{1,0:T(8,128)S(1)}, u32[]{:S(2)}, u32[]{:S(2)}) collective-permute-start(f32[2048,128]{1,0:T(8,128)} %get-tuple-element.23), channel_id=1, source_target_pairs={{0,1},{1,0},{2,3},{3,2},{4,5},{5,4},{6,7},{7,6},{8,9},{9,8},{10,11... | collective-permute-start | bytes 3145736 | tf_op jit(solution)/shard_map/ppermute | solution.py:293
  4.4 39.0 %collective-permute-start.1 = (f32[2048,128]{1,0:T(8,128)}, f32[2048,128]{1,0:T(8,128)}, u32[]{:S(2)}, u32[]{:S(2)}) collective-permute-start(f32[2048,128]{1,0:T(8,128)} %get-tuple-element.25), channel_id=1, source_target_pairs={{1,2},{2,1},{3,4},{4,3},{5,6},{6,5},{7,8},{8,7},{9,10},{10,9},{11,... | collective-permute-start | bytes 3145736 | tf_op jit(solution)/shard_map/ppermute | solution.py:346
  12.6 64.8 %all-to-all-start = ((f32[256,2,2048]{2,1,0:T(2,128)}), f32[256,2,2048]{2,1,0:T(2,128)}, u32[]{:S(2)}, u32[]{:S(2)}) async-start(f32[256,2,2048]{2,1,0:T(2,128)} %param.2), calls=%async_computation | async-start | bytes 8388608 | tf_op jit(solution)/shard_map/all_to_all | solution.py:347
  17.1 2.2 %copy-start.1 = (f32[256,2,2048]{2,1,0:T(2,128)S(1)}, f32[256,2,2048]{2,1,0:T(2,128)}, u32[]{:S(2)}) copy-start(f32[256,2,2048]{2,1,0:T(2,128)} %param.2) | copy-start | bytes 12582916
  46.9 1.7 %collective-permute-start.2 = (f32[64,1024]{1,0:T(8,128)}, f32[64,1024]{1,0:T(8,128)S(1)}, u32[]{:S(2)}, u32[]{:S(2)}) collective-permute-start(f32[64,1024]{1,0:T(8,128)} %get-tuple-element.27), channel_id=1, source_target_pairs={{0,1},{1,0},{2,3},{3,2},{4,5},{5,4},{6,7},{7,6},{8,9},{9,8},{10,11... | collective-permute-start | bytes 786440 | tf_op jit(solution)/shard_map/ppermute | solution.py:293
  48.7 4.3 %collective-permute-start.5 = (f32[16,1024]{1,0:T(8,128)S(1)}, f32[16,1024]{1,0:T(8,128)S(1)}, u32[]{:S(2)}, u32[]{:S(2)}) collective-permute-start(f32[16,1024]{1,0:T(8,128)S(1)} %get-tuple-element.35), channel_id=1, source_target_pairs={{0,96},{1,97},{2,98},{3,99},{4,100},{5,101},{6,102},{7,103},{8,104... | collective-permute-start | bytes 196616 | tf_op jit(solution)/shard_map/ppermute | solution.py:293
  50.4 6.3 %collective-permute-start.4 = (f32[16,1024]{1,0:T(8,128)S(1)}, f32[16,1024]{1,0:T(8,128)S(1)}, u32[]{:S(2)}, u32[]{:S(2)}) collective-permute-start(f32[16,1024]{1,0:T(8,128)S(1)} %get-tuple-element.36), channel_id=1, source_target_pairs={{0,64},{1,65},{2,66},{3,67},{4,68},{5,69},{6,70},{7,71},{8,72},{9,... | collective-permute-start | bytes 196616 | tf_op jit(solution)/shard_map/ppermute | solution.py:293
  51.5 5.2 %collective-permute-start.3 = (f32[16,1024]{1,0:T(8,128)S(1)}, f32[16,1024]{1,0:T(8,128)S(1)}, u32[]{:S(2)}, u32[]{:S(2)}) collective-permute-start(f32[16,1024]{1,0:T(8,128)S(1)} %get-tuple-element.34), channel_id=1, source_target_pairs={{0,32},{1,33},{2,34},{3,35},{4,36},{5,37},{6,38},{7,39},{8,40},{9,... | collective-permute-start | bytes 196616 | tf_op jit(solution)/shard_map/ppermute | solution.py:293
  56.7 5.7 %collective-permute-start.6 = (f32[8,1024]{1,0:T(8,128)S(1)}, f32[8,1024]{1,0:T(8,128)S(1)}, u32[]{:S(2)}, u32[]{:S(2)}) collective-permute-start(f32[8,1024]{1,0:T(8,128)S(1)} %dynamic-slice_bitcast_fusion.3), channel_id=1, source_target_pairs={{0,24},{1,25},{2,26},{3,27},{4,28},{5,29},{6,30},{7,31},{8,16},{9,... | collective-permute-start | bytes 98312 | tf_op jit(solution)/shard_map/ppermute | solution.py:314
  60.5 1.9 %collective-permute-start.7 = (f32[32,128]{1,0:T(8,128)S(1)}, f32[32,128]{1,0:T(8,128)S(1)}, u32[]{:S(2)}, u32[]{:S(2)}) collective-permute-start(f32[32,128]{1,0:T(8,128)S(1)} %bitcast.61), channel_id=1, source_target_pairs={{0,1},{1,0},{2,3},{3,2},{4,5},{5,4},{6,7},{7,6},{8,9},{9,8},{10,11... | collective-permute-start | bytes 49160 | tf_op jit(solution)/shard_map/ppermute | solution.py:293
  62.5 5.9 %collective-permute-start.8 = (f32[96,128]{1,0:T(8,128)S(1)}, f32[96,128]{1,0:T(8,128)S(1)}, u32[]{:S(2)}, u32[]{:S(2)}) collective-permute-start(f32[96,128]{1,0:T(8,128)S(1)} %pad_maximum_fusion.10), channel_id=1, source_target_pairs={{0,8},{1,9},{2,10},{3,11},{4,12},{5,13},{6,14},{7,15},{8,0},{9,1},... | collective-permute-start | bytes 147464 | tf_op jit(solution)/shard_map/ppermute | solution.py:293
  68.5 5.9 %collective-permute-start.11 = (f32[136,128]{1,0:T(8,128)S(1)}, f32[136,128]{1,0:T(8,128)S(1)}, u32[]{:S(2)}, u32[]{:S(2)}) collective-permute-start(f32[136,128]{1,0:T(8,128)S(1)} %get-tuple-element.39), channel_id=1, source_target_pairs={{0,6},{1,7},{2,4},{3,5},{4,2},{5,3},{6,0},{7,1},{8,14},{9,15},{10,... | collective-permute-start | bytes 208904 | tf_op jit(solution)/shard_map/ppermute | solution.py:293
  71.5 5.8 %collective-permute-start.10 = (f32[136,128]{1,0:T(8,128)S(1)}, f32[136,128]{1,0:T(8,128)S(1)}, u32[]{:S(2)}, u32[]{:S(2)}) collective-permute-start(f32[136,128]{1,0:T(8,128)S(1)} %get-tuple-element.38), channel_id=1, source_target_pairs={{0,4},{1,5},{2,6},{3,7},{4,0},{5,1},{6,2},{7,3},{8,12},{9,13},{10,... | collective-permute-start | bytes 208904 | tf_op jit(solution)/shard_map/ppermute | solution.py:293
  71.5 5.8 %collective-permute-start.9 = (f32[136,128]{1,0:T(8,128)S(1)}, f32[136,128]{1,0:T(8,128)S(1)}, u32[]{:S(2)}, u32[]{:S(2)}) collective-permute-start(f32[136,128]{1,0:T(8,128)S(1)} %get-tuple-element.37), channel_id=1, source_target_pairs={{0,2},{1,3},{2,0},{3,1},{4,6},{5,7},{6,4},{7,5},{8,10},{9,11},{10,... | collective-permute-start | bytes 208904 | tf_op jit(solution)/shard_map/ppermute | solution.py:293
  78.5 15.4 %collective-permute-start.12 = (f32[16,2048]{1,0:T(8,128)S(1)}, f32[16,2048]{1,0:T(8,128)S(1)}, u32[]{:S(2)}, u32[]{:S(2)}) collective-permute-start(f32[16,2048]{1,0:T(8,128)S(1)} %get-tuple-element.30), channel_id=1, source_target_pairs={{0,16},{16,0},{32,48},{48,32},{64,80},{80,64},{96,112},{112,96},{1... | collective-permute-start | bytes 393224 | tf_op jit(solution)/shard_map/ppermute | solution.py:359
  81.4 12.5 %collective-permute-start.13 = (f32[16,2048]{1,0:T(8,128)S(1)}, f32[16,2048]{1,0:T(8,128)S(1)}, u32[]{:S(2)}, u32[]{:S(2)}) collective-permute-start(f32[16,2048]{1,0:T(8,128)S(1)} %get-tuple-element.31), channel_id=1, source_target_pairs={{16,32},{32,16},{48,64},{64,48},{80,96},{96,80},{17,33},{33,17},{4... | collective-permute-start | bytes 393224 | tf_op jit(solution)/shard_map/ppermute | solution.py:360

commit v4 on v3

--- a/solution.py
+++ b/solution.py
@@ -25,29 +25,28 @@
     return high, (x - high.astype(jnp.float32)).astype(jnp.bfloat16)
 
 
+def cut(count, rows, x_ref, starts, refs):
+    half = rows // 4
+    for o in range(count):
+        for ref, start in zip(refs, starts):
+            ref[pl.ds(o * half, half), :] = x_ref[pl.ds(o * rows + start, half, stride=2), :]
+
+
 def extract_kernel(count, rows, x_ref, *refs):
-    half = rows // 4
-    far = 2 * half
-
-    def run(*starts):
-        for o in range(count):
-            for ref, start in zip(refs, starts):
-                ref[pl.ds(o * half, half), :] = x_ref[pl.ds(o * rows + start, half, stride=2), :]
-
     core = lax.rem(lax.axis_index("col"), 2)
-    pl.when(core == 0)(lambda: run(far + 1, 0, 1, far))
-    pl.when(core == 1)(lambda: run(0, far + 1, far, 1))
+    pl.when(core == 0)(lambda: cut(count, rows, x_ref, (rows // 2 + 1, 0), refs))
+    pl.when(core == 1)(lambda: cut(count, rows, x_ref, (0, rows // 2 + 1), refs))
 
 
 def extract(x, count, rows):
-    half = pltpu.VMEM((count * rows // 4, LANES), jnp.float32)
+    half = jax.ShapeDtypeStruct((count * rows // 4, LANES), jnp.float32)
     return pl.pallas_call(
         functools.partial(extract_kernel, count, rows),
         in_specs=[pl.BlockSpec(memory_space=pltpu.VMEM)],
-        out_specs=[pl.BlockSpec(memory_space=pltpu.VMEM)] * 4,
-        out_shape=[half] * 4,
-        compiler_params=pltpu.CompilerParams(vmem_limit_bytes=10 * 2**20),
-        cost_estimate=pl.CostEstimate(flops=0, bytes_accessed=count * rows * LANES * 8, transcendentals=0),
+        out_specs=[pl.BlockSpec(memory_space=pltpu.VMEM)] * 2,
+        out_shape=[half] * 2,
+        compiler_params=pltpu.CompilerParams(vmem_limit_bytes=8 * 2**20),
+        cost_estimate=pl.CostEstimate(flops=0, bytes_accessed=count * rows * LANES * 6, transcendentals=0),
     )(x)
 
 
@@ -58,7 +57,7 @@
     return dot(a_high, b_high) + dot(a_high, b_low) + dot(a_low, b_high)
 
 
-def gram_kernel(count, rows, x_ref, v_ref, g_ref):
+def gram_kernel(count, rows, x_ref, v_ref, g_ref, by_core_ref, by_chip_ref):
     tiles = rows // 2
     lane = lax.broadcasted_iota(jnp.int32, (count, LANES), 1)
 
@@ -95,14 +94,19 @@
         with_half = q if with_half is None else with_half + q
     g_ref[:, :count] = with_self + with_low + with_low.T
     g_ref[:, count:] = with_half
+    refs = (by_core_ref, by_chip_ref)
+    core = lax.rem(lax.axis_index("col"), 2)
+    pl.when(core == 0)(lambda: cut(count, rows, x_ref, (1, rows // 2), refs))
+    pl.when(core == 1)(lambda: cut(count, rows, x_ref, (rows // 2, 1), refs))
 
 
 def gram(x, v, count, rows):
+    half = jax.ShapeDtypeStruct((count * rows // 4, LANES), jnp.float32)
     return pl.pallas_call(
         functools.partial(gram_kernel, count, rows),
-        out_shape=jax.ShapeDtypeStruct((count, 2 * count), jnp.float32),
+        out_shape=[jax.ShapeDtypeStruct((count, 2 * count), jnp.float32), half, half],
         in_specs=[pl.BlockSpec(memory_space=pltpu.VMEM)] * 2,
-        out_specs=pl.BlockSpec(memory_space=pltpu.VMEM),
+        out_specs=[pl.BlockSpec(memory_space=pltpu.VMEM)] * 3,
         compiler_params=pltpu.CompilerParams(vmem_limit_bytes=16 * 2**20),
         cost_estimate=pl.CostEstimate(
             flops=400 * count * count * rows * LANES, bytes_accessed=count * rows * LANES * 6, transcendentals=0
@@ -204,7 +208,7 @@
         for b, ref in enumerate((v_own_ref, v1_ref, v2_ref, v3_ref)):
             for a in (0, 1):
                 for c in (0, 1):
-                    start = ref.shape[0] + (2 * a + c - 4) * rows
+                    start = ref.shape[0] + (2 * c + a - 4) * rows
                     v_held_ref[column ^ (8 * a + 2 * b + c)] = ref[pl.ds(start, rows), :]
         v_scr[...] = 2.0 + interleaved(v_held_ref.reshape(sources * rows, LANES), 0, rows, work_ref.at[0])
 
@@ -314,20 +318,20 @@
     return pick(0) + lax.ppermute(pick(1), ("row", "col"), pairs)
 
 
-def reduce_chips(total, v):
-    total = total.reshape(8, -1, LANES)
-    height = total.shape[1]
-
-    def pick(x, mine, k):
-        return lax.dynamic_index_in_dim(x, mine ^ k, 0, keepdims=False).reshape(-1, LANES)
-
-    z, x = digit(8, 2), digit(2, 4)
-    pair = total.reshape(2, 4, height, LANES)
-    got = exchange(jnp.concatenate([pick(pair, z, 1), v]), 8)
-    total = (pick(pair, z, 0) + got[: 4 * height]).reshape(4, height, LANES)
-    v = jnp.concatenate([v, got[4 * height :]])
-    got = [exchange(jnp.concatenate([pick(total, x, k), v]), 2 * k) for k in (1, 2, 3)]
-    return sum([part[:height] for part in got], pick(total, x, 0)), [v, *got]
+def reduce_x(total, v):
+    total = total.reshape(2, 4, -1, LANES)
+    x = digit(2, 4)
+    pick = lambda k: lax.dynamic_index_in_dim(total, x ^ k, 1, keepdims=False).reshape(-1, LANES)
+    got = [exchange(jnp.concatenate([pick(k), v]), 2 * k) for k in (1, 2, 3)]
+    height = got[0].shape[0] - v.shape[0]
+    return sum([part[:height] for part in got], pick(0)), [v, *got]
+
+
+def reduce_z_lo(total):
+    total = total.reshape(2, -1, LANES)
+    z = digit(8, 2)
+    pick = lambda k: lax.dynamic_index_in_dim(total, z ^ k, 0, keepdims=False)
+    return pick(0) + exchange(pick(1), 8)
 
 
 def local(orbitals, potential):
@@ -340,25 +344,27 @@
 
     tiled = tile_view(orbitals).reshape(count * rows, LANES)
     v = tile_view(potential)
-    to_core, to_chip, by_core, by_chip = extract(tiled, count, rows)
-    orbitals, to_core, to_chip, v = lax.optimization_barrier((orbitals, to_core, to_chip, v))
+    v_z = jnp.concatenate([v, exchange(v, 8)])
+    to_core, to_chip = extract(tiled, count, rows)
+    orbitals, to_core, to_chip, v, v_z = lax.optimization_barrier((orbitals, to_core, to_chip, v, v_z))
     from_core = exchange(to_core, 1)
     from_chip = lax.ppermute(to_chip, every, [(i, (i + 1 ^ 1) - 1) for i in range(1, devices - 1)])
     received = lax.all_to_all(orbitals, "col", split_axis=0, concat_axis=0, tiled=True)
     received = tile_view(received.reshape(n_col, mine, planes, points)).reshape(n_col, mine * rows, LANES)
 
-    g = gram(tiled, v, count, rows)
+    g, by_core, by_chip = gram(tiled, v, count, rows)
     keep, send = finish(g, by_core, from_core, by_chip, from_chip, count, rows, scale)
-    v = jnp.concatenate([v, exchange(v, 1)])
+    v_x = jnp.concatenate([v_z, exchange(v_z, 1)])
     g = reduce_digit(keep + exchange(send, 1), 32)
     g = reduce_z_hi(g)
-    g, v_parts = reduce_chips(g, v)
-    g = g.reshape(planes, 2 * count)
+    g, v_parts = reduce_x(g, v_x)
 
     near, far = edges_of(received, mine, rows)
+    g, near, far = lax.optimization_barrier((g, near, far))
     near = lax.ppermute(near, "row", [(i, i ^ 1) for i in range(n_row)])
     far = lax.ppermute(far, "row", [(i, (i + 1 ^ 1) - 1) for i in range(1, n_row - 1)])
     relayed, applied, sides = to_block(received, v_parts, mine, rows)
+    g = reduce_z_lo(g).reshape(planes, 2 * count)
     return g[:, :count], g[:, count:], relayed, fix_edges(applied, sides, near, far)
 
 

time: 96.2 us -> 96 us (level)
  the two profiles are of different devices: /device:TPU:8 before, /device:TPU:24 now
where the time goes in v4:
time: 96 us; the launch traced here: 94.7 us
  starting transfers between devices  36.5 us (38%)
  waiting for transfers between devices  33.8 us (35%)
  Pallas kernels  18.5 us (19%)
  local copies, waits for them, and re-layouts  5.06 us (5%)
    ppermute x1, waiting for transfers between devices, local(): lax.ppermute(to_chip, every, [(i, (i + 1 ^ 1) - 1) for i in range(1, devi...  18.5 us
    ppermute x11, starting transfers between devices, exchange(): lax.ppermute(x, every, [(i, i ^ mask) for i in range(lax.axis_size(every))])  15.1 us
    ppermute x11, waiting for transfers between devices, exchange(): lax.ppermute(x, every, [(i, i ^ mask) for i in range(lax.axis_size(every))])  13.4 us
    pallas_call x1, Pallas kernels, to_block(): pl.pallas_call(functools.partial(block_kernel, sources, block, rows), gri...  7.47 us
    ppermute x1, starting transfers between devices, local(): lax.ppermute(to_chip, every, [(i, (i + 1 ^ 1) - 1) for i in range(1, devi...  7.06 us
    pallas_call x1, Pallas kernels, gram(): pl.pallas_call(functools.partial(gram_kernel, count, rows), out_shape=[ja...  5.3 us
    ppermute x1, starting transfers between devices, local(): lax.ppermute(far, 'row', [(i, (i + 1 ^ 1) - 1) for i in range(1, n_row -...  5.28 us
    all_to_all x1, starting transfers between devices, local(): lax.all_to_all(orbitals, 'col', split_axis=0, concat_axis=0, tiled=True)  4.57 us
  transfers between devices with their start and end apart: 16, of which 7 were waited for; matrix products, arithmetic and copies ran while one was open for 1% of the time, Pallas kernels for 16%

profile of v4, /device:TPU:24, one launch (start us, length us, event | category | flops | bytes accessed | tf_op | source)
XLA Modules:
  0.0 94.7 jit_solution(12312594395250757024)
XLA Ops:
  0.6 2.0 %collective-permute-start = (f32[32,128]{1,0:T(8,128)}, f32[32,128]{1,0:T(8,128)S(1)}, u32[]{:S(2)}, u32[]{:S(2)}) collective-permute-start(f32[32,128]{1,0:T(8,128)} %bitcast.59), channel_id=1, source_target_pairs={{0,8},{1,9},{2,10},{3,11},{4,12},{5,13},{6,14},{7,15},{8,0},{9,1},... | collective-permute-start | bytes 49160 | tf_op jit(solution)/shard_map/ppermute | solution.py:297
  2.6 0.0 copy-start
  2.6 2.2 %copy-done = f32[256,2,2048]{2,1,0:T(2,128)S(1)} copy-done((f32[256,2,2048]{2,1,0:T(2,128)S(1)}, f32[256,2,2048]{2,1,0:T(2,128)}, u32[]{:S(2)}) %copy-start) | copy-done | bytes 4194328
  4.8 0.0 copy-start.2
  4.8 1.1 %shard_map.57 = (f32[2048,128]{1,0:T(8,128)}, f32[2048,128]{1,0:T(8,128)S(1)}) custom-call(f32[8192,128]{1,0:T(8,128)S(1)} %bitcast.57), custom_call_target="tpu_custom_call" | custom-call | bytes 6291456 | tf_op jit(solution)/shard_map/pallas_call | solution.py:43
  5.9 0.0 collective-permute-done
  5.9 0.0 copy-done.2
  5.9 0.1 collective-permute-start.1
  6.0 7.1 %collective-permute-start.2 = (f32[2048,128]{1,0:T(8,128)S(1)}, f32[2048,128]{1,0:T(8,128)S(1)}, u32[]{:S(2)}, u32[]{:S(2)}) collective-permute-start(f32[2048,128]{1,0:T(8,128)S(1)} %get-tuple-element.31), channel_id=1, source_target_pairs={{1,2},{2,1},{3,4},{4,3},{5,6},{6,5},{7,8},{8,7},{9,10},{10,9},{11,... | collective-permute-start | bytes 3145736 | tf_op jit(solution)/shard_map/ppermute | solution.py:351
  13.1 4.6 %all-to-all-start = ((f32[256,2,2048]{2,1,0:T(2,128)}), f32[256,2,2048]{2,1,0:T(2,128)}, u32[]{:S(2)}, u32[]{:S(2)}) async-start(f32[256,2,2048]{2,1,0:T(2,128)} %param.2), calls=%async_computation | async-start | bytes 8388608 | tf_op jit(solution)/shard_map/all_to_all | solution.py:352
  17.7 0.0 copy-start.1
  17.7 2.2 %copy-done.1 = f32[256,2,2048]{2,1,0:T(2,128)S(1)} copy-done((f32[256,2,2048]{2,1,0:T(2,128)S(1)}, f32[256,2,2048]{2,1,0:T(2,128)}, u32[]{:S(2)}) %copy-start.1) | copy-done | bytes 4194328
  19.9 5.3 %shard_map.58 = (f32[256,512]{1,0:T(8,128)S(1)}, f32[2048,128]{1,0:T(8,128)S(1)}, f32[2048,128]{1,0:T(8,128)S(1)}) custom-call(f32[8192,128]{1,0:T(8,128)S(1)} %bitcast.58, f32[32,128]{1,0:T(8,128)S(1)} %bitcast.61), custom_call_target="tpu_custom_call" | custom-call | flops 107374182400 | bytes 6291456 | tf_op jit(solution)/shard_map/pallas_call | solution.py:105
  25.2 0.0 collective-permute-done.1.core_ref
  25.2 18.5 %collective-permute-done.2.chip_ref = f32[2048,128]{1,0:T(8,128)S(1)} collective-permute-done((f32[2048,128]{1,0:T(8,128)S(1)}, f32[2048,128]{1,0:T(8,128)S(1)}, u32[]{:S(2)}, u32[]{:S(2)}) %collective-permute-start.2) | collective-permute-done | bytes 1048608 | tf_op jit(solution)/shard_map/ppermute | solution.py:351
  43.7 1.6 %shard_map.59 = (f32[64,1024]{1,0:T(8,128)S(1)}, f32[64,1024]{1,0:T(8,128)S(1)}) custom-call(f32[256,512]{1,0:T(8,128)S(1)} %get-tuple-element.27.g_ref, f32[2048,128]{1,0:T(8,128)S(1)} %get-tuple-element.28.by_core_ref, f32[2048,128]{1,0:T(8,128)S(1)} %collective-permute-done.1.core_ref, f32[2048,128]{1,0:T(8,128)S(1)} %get-tuple-element.30.by_chip_ref, ...), custom_call_target="tpu_custom_call" | custom-call | flops 805306368 | bytes 4194304 | tf_op jit(solution)/shard_map/pallas_call | solution.py:144
  45.3 0.1 collective-permute-start.3
  45.4 1.5 %collective-permute-done.3 = f32[64,1024]{1,0:T(8,128)S(1)} collective-permute-done((f32[64,1024]{1,0:T(8,128)S(1)}, f32[64,1024]{1,0:T(8,128)S(1)}, u32[]{:S(2)}, u32[]{:S(2)}) %collective-permute-start.3) | collective-permute-done | bytes 262176 | tf_op jit(solution)/shard_map/ppermute | solution.py:297
  47.0 2.1 %collective-permute-start.4 = (f32[16,1024]{1,0:T(8,128)S(1)}, f32[16,1024]{1,0:T(8,128)S(1)}, u32[]{:S(2)}, u32[]{:S(2)}) collective-permute-start(f32[16,1024]{1,0:T(8,128)S(1)} %get-tuple-element.44), channel_id=1, source_target_pairs={{0,32},{1,33},{2,34},{3,35},{4,36},{5,37},{6,38},{7,39},{8,40},{9,... | collective-permute-start | bytes 196616 | tf_op jit(solution)/shard_map/ppermute | solution.py:297
  49.0 0.6 collective-permute-start.5
  49.6 2.2 %collective-permute-start.6 = (f32[16,1024]{1,0:T(8,128)S(1)}, f32[16,1024]{1,0:T(8,128)S(1)}, u32[]{:S(2)}, u32[]{:S(2)}) collective-permute-start(f32[16,1024]{1,0:T(8,128)S(1)} %get-tuple-element.45), channel_id=1, source_target_pairs={{0,96},{1,97},{2,98},{3,99},{4,100},{5,101},{6,102},{7,103},{8,104... | collective-permute-start | bytes 196616 | tf_op jit(solution)/shard_map/ppermute | solution.py:297
  51.8 0.0 collective-permute-done.4
  51.8 3.1 %collective-permute-done.5 = f32[16,1024]{1,0:T(8,128)S(1)} collective-permute-done((f32[16,1024]{1,0:T(8,128)S(1)}, f32[16,1024]{1,0:T(8,128)S(1)}, u32[]{:S(2)}, u32[]{:S(2)}) %collective-permute-start.5) | collective-permute-done | bytes 65568 | tf_op jit(solution)/shard_map/ppermute | solution.py:297
  54.9 0.9 collective-permute-done.6
  55.8 4.5 %collective-permute-start.7 = (f32[8,1024]{1,0:T(8,128)S(1)}, f32[8,1024]{1,0:T(8,128)S(1)}, u32[]{:S(2)}, u32[]{:S(2)}) collective-permute-start(f32[8,1024]{1,0:T(8,128)S(1)} %dynamic-slice_bitcast_fusion.3), channel_id=1, source_target_pairs={{0,24},{1,25},{2,26},{3,27},{4,28},{5,29},{6,30},{7,31},{8,16},{9,... | collective-permute-start | bytes 98312 | tf_op jit(solution)/shard_map/ppermute | solution.py:318
  60.3 0.0 collective-permute-start.8
  60.3 1.9 %collective-permute-done.7 = f32[8,1024]{1,0:T(8,128)S(1)} collective-permute-done((f32[8,1024]{1,0:T(8,128)S(1)}, f32[8,1024]{1,0:T(8,128)S(1)}, u32[]{:S(2)}, u32[]{:S(2)}) %collective-permute-start.7) | collective-permute-done | bytes 32800 | tf_op jit(solution)/shard_map/ppermute | solution.py:318
  62.2 0.0 collective-permute-done.8
  62.3 0.1 collective-permute-start.10
  62.4 4.1 %collective-permute-start.11 = (f32[144,128]{1,0:T(8,128)S(1)}, f32[144,128]{1,0:T(8,128)S(1)}, u32[]{:S(2)}, u32[]{:S(2)}) collective-permute-start(f32[144,128]{1,0:T(8,128)S(1)} %get-tuple-element.49), channel_id=1, source_target_pairs={{0,6},{1,7},{2,4},{3,5},{4,2},{5,3},{6,0},{7,1},{8,14},{9,15},{10,... | collective-permute-start | bytes 221192 | tf_op jit(solution)/shard_map/ppermute | solution.py:297
  66.5 0.8 collective-permute-start.9
  67.3 2.7 %collective-permute-done.10.v2_ref = f32[144,128]{1,0:T(8,128)S(1)} collective-permute-done((f32[144,128]{1,0:T(8,128)S(1)}, f32[144,128]{1,0:T(8,128)S(1)}, u32[]{:S(2)}, u32[]{:S(2)}) %collective-permute-start.10) | collective-permute-done | bytes 73760 | tf_op jit(solution)/shard_map/ppermute | solution.py:297
  69.9 5.2 %collective-permute-done.11.v3_ref = f32[144,128]{1,0:T(8,128)S(1)} collective-permute-done((f32[144,128]{1,0:T(8,128)S(1)}, f32[144,128]{1,0:T(8,128)S(1)}, u32[]{:S(2)}, u32[]{:S(2)}) %collective-permute-start.11) | collective-permute-done | bytes 73760 | tf_op jit(solution)/shard_map/ppermute | solution.py:297
  75.2 0.0 collective-permute-done.9.v1_ref
  75.2 0.0 all-to-all-done
  75.2 1.2 %shard_map.60 = (f32[16,2048]{1,0:T(8,128)S(1)}, f32[16,2048]{1,0:T(8,128)S(1)}) custom-call(f32[16,512,128]{2,1,0:T(8,128)} %bitcast.24.low_ref.high_ref, f32[16,512,128]{2,1,0:T(8,128)} %bitcast.24.low_ref.high_ref), custom_call_target="tpu_custom_call" | custom-call | bytes 262144 | tf_op jit(solution)/shard_map/pallas_call | solution.py:178
  76.4 3.1 %collective-permute-start.12 = (f32[8,128]{1,0:T(8,128)S(1)}, f32[8,128]{1,0:T(8,128)S(1)}, u32[]{:S(2)}, u32[]{:S(2)}) collective-permute-start(f32[8,128]{1,0:T(8,128)S(1)} %dynamic-slice_bitcast_fusion.7), channel_id=1, source_target_pairs={{0,8},{1,9},{2,10},{3,11},{4,12},{5,13},{6,14},{7,15},{8,0},{9,1},... | collective-permute-start | bytes 12296 | tf_op jit(solution)/shard_map/ppermute | solution.py:297
  79.5 0.0 collective-permute-start.13
  79.5 5.3 %collective-permute-start.14 = (f32[16,2048]{1,0:T(8,128)S(1)}, f32[16,2048]{1,0:T(8,128)S(1)}, u32[]{:S(2)}, u32[]{:S(2)}) collective-permute-start(f32[16,2048]{1,0:T(8,128)S(1)} %get-tuple-element.41), channel_id=1, source_target_pairs={{16,32},{32,16},{48,64},{64,48},{80,96},{96,80},{17,33},{33,17},{4... | collective-permute-start | bytes 393224 | tf_op jit(solution)/shard_map/ppermute | solution.py:365
  84.8 7.5 %shard_map.61 = (f32[16,32,2048]{2,1,0:T(8,128)}, f32[16,32,2048]{2,1,0:T(8,128)}, f32[2,16,8,2048]{3,2,1,0:T(8,128)S(1)}) custom-call(f32[16,16,32,128]{3,2,1,0:T(8,128)} %bitcast.29.x_ref, f32[128,128]{1,0:T(8,128)S(1)} %pad_maximum_fusion.6.v_own_ref, f32[144,128]{1,0:T(8,128)S(1)} %collective-permute-done.9.v1_ref, ...), custom_call_target="tpu_custom_call" | custom-call | bytes 12582912 | tf_op jit(solution)/shard_map/pallas_call | solution.py:235
  92.2 0.0 collective-permute-done.12
  92.2 0.6 fusion.4
  92.8 0.0 collective-permute-done.13.near_ref
  92.8 0.0 collective-permute-done.14.far_ref
  92.8 1.8 %shard_map.62 = f32[16,32,2048]{2,1,0:T(8,128)} custom-call(f32[16,2048]{1,0:T(8,128)S(1)} %collective-permute-done.13.near_ref, f32[16,2048]{1,0:T(8,128)S(1)} %collective-permute-done.14.far_ref, f32[2,16,8,2048]{3,2,1,0:T(8,128)S(1)} %get-tuple-element.42.sides_ref, f32[16,32,2048]{2,1,0:T(8,128)} %get-tuple-element.43.applied_ref), custom_call_target="tpu_custom_call", output_to_operand_aliasing={{}: (3, {})} | custom-call | bytes 1048576 | tf_op jit(solution)/shard_map/pallas_call | solution.py:280
  (14 shorter events, 0.2 us)
Async XLA Ops:
  0.6 5.3 %collective-permute-start = (f32[32,128]{1,0:T(8,128)}, f32[32,128]{1,0:T(8,128)S(1)}, u32[]{:S(2)}, u32[]{:S(2)}) collective-permute-start(f32[32,128]{1,0:T(8,128)} %bitcast.59), channel_id=1, source_target_pairs={{0,8},{1,9},{2,10},{3,11},{4,12},{5,13},{6,14},{7,15},{8,0},{9,1},... | collective-permute-start | bytes 49160 | tf_op jit(solution)/shard_map/ppermute | solution.py:297
  2.6 2.2 %copy-start = (f32[256,2,2048]{2,1,0:T(2,128)S(1)}, f32[256,2,2048]{2,1,0:T(2,128)}, u32[]{:S(2)}) copy-start(f32[256,2,2048]{2,1,0:T(2,128)} %param.2) | copy-start | bytes 12582916
  4.8 1.1 %copy-start.2 = (f32[2,2048]{1,0:T(2,128)S(1)}, f32[2,2048]{1,0:T(2,128)}, u32[]{:S(2)}) copy-start(f32[2,2048]{1,0:T(2,128)} %param.3) | copy-start | bytes 49156
  5.9 19.3 %collective-permute-start.1 = (f32[2048,128]{1,0:T(8,128)}, f32[2048,128]{1,0:T(8,128)S(1)}, u32[]{:S(2)}, u32[]{:S(2)}) collective-permute-start(f32[2048,128]{1,0:T(8,128)} %get-tuple-element.29), channel_id=1, source_target_pairs={{0,1},{1,0},{2,3},{3,2},{4,5},{5,4},{6,7},{7,6},{8,9},{9,8},{10,11... | collective-permute-start | bytes 3145736 | tf_op jit(solution)/shard_map/ppermute | solution.py:297
  6.0 37.7 %collective-permute-start.2 = (f32[2048,128]{1,0:T(8,128)S(1)}, f32[2048,128]{1,0:T(8,128)S(1)}, u32[]{:S(2)}, u32[]{:S(2)}) collective-permute-start(f32[2048,128]{1,0:T(8,128)S(1)} %get-tuple-element.31), channel_id=1, source_target_pairs={{1,2},{2,1},{3,4},{4,3},{5,6},{6,5},{7,8},{8,7},{9,10},{10,9},{11,... | collective-permute-start | bytes 3145736 | tf_op jit(solution)/shard_map/ppermute | solution.py:351
  13.1 62.1 %all-to-all-start = ((f32[256,2,2048]{2,1,0:T(2,128)}), f32[256,2,2048]{2,1,0:T(2,128)}, u32[]{:S(2)}, u32[]{:S(2)}) async-start(f32[256,2,2048]{2,1,0:T(2,128)} %param.2), calls=%async_computation | async-start | bytes 8388608 | tf_op jit(solution)/shard_map/all_to_all | solution.py:352
  17.7 2.2 %copy-start.1 = (f32[256,2,2048]{2,1,0:T(2,128)S(1)}, f32[256,2,2048]{2,1,0:T(2,128)}, u32[]{:S(2)}) copy-start(f32[256,2,2048]{2,1,0:T(2,128)} %param.2) | copy-start | bytes 12582916
  45.3 1.6 %collective-permute-start.3 = (f32[64,1024]{1,0:T(8,128)S(1)}, f32[64,1024]{1,0:T(8,128)S(1)}, u32[]{:S(2)}, u32[]{:S(2)}) collective-permute-start(f32[64,1024]{1,0:T(8,128)S(1)} %get-tuple-element.33), channel_id=1, source_target_pairs={{0,1},{1,0},{2,3},{3,2},{4,5},{5,4},{6,7},{7,6},{8,9},{9,8},{10,11... | collective-permute-start | bytes 786440 | tf_op jit(solution)/shard_map/ppermute | solution.py:297
  47.0 4.9 %collective-permute-start.4 = (f32[16,1024]{1,0:T(8,128)S(1)}, f32[16,1024]{1,0:T(8,128)S(1)}, u32[]{:S(2)}, u32[]{:S(2)}) collective-permute-start(f32[16,1024]{1,0:T(8,128)S(1)} %get-tuple-element.44), channel_id=1, source_target_pairs={{0,32},{1,33},{2,34},{3,35},{4,36},{5,37},{6,38},{7,39},{8,40},{9,... | collective-permute-start | bytes 196616 | tf_op jit(solution)/shard_map/ppermute | solution.py:297
  49.0 5.8 %collective-permute-start.5 = (f32[16,1024]{1,0:T(8,128)S(1)}, f32[16,1024]{1,0:T(8,128)S(1)}, u32[]{:S(2)}, u32[]{:S(2)}) collective-permute-start(f32[16,1024]{1,0:T(8,128)S(1)} %get-tuple-element.46), channel_id=1, source_target_pairs={{0,64},{1,65},{2,66},{3,67},{4,68},{5,69},{6,70},{7,71},{8,72},{9,... | collective-permute-start | bytes 196616 | tf_op jit(solution)/shard_map/ppermute | solution.py:297
  49.6 6.2 %collective-permute-start.6 = (f32[16,1024]{1,0:T(8,128)S(1)}, f32[16,1024]{1,0:T(8,128)S(1)}, u32[]{:S(2)}, u32[]{:S(2)}) collective-permute-start(f32[16,1024]{1,0:T(8,128)S(1)} %get-tuple-element.45), channel_id=1, source_target_pairs={{0,96},{1,97},{2,98},{3,99},{4,100},{5,101},{6,102},{7,103},{8,104... | collective-permute-start | bytes 196616 | tf_op jit(solution)/shard_map/ppermute | solution.py:297
  55.8 6.4 %collective-permute-start.7 = (f32[8,1024]{1,0:T(8,128)S(1)}, f32[8,1024]{1,0:T(8,128)S(1)}, u32[]{:S(2)}, u32[]{:S(2)}) collective-permute-start(f32[8,1024]{1,0:T(8,128)S(1)} %dynamic-slice_bitcast_fusion.3), channel_id=1, source_target_pairs={{0,24},{1,25},{2,26},{3,27},{4,28},{5,29},{6,30},{7,31},{8,16},{9,... | collective-permute-start | bytes 98312 | tf_op jit(solution)/shard_map/ppermute | solution.py:318
  60.3 1.9 %collective-permute-start.8 = (f32[64,128]{1,0:T(8,128)S(1)}, f32[64,128]{1,0:T(8,128)S(1)}, u32[]{:S(2)}, u32[]{:S(2)}) collective-permute-start(f32[64,128]{1,0:T(8,128)S(1)} %pad_maximum_fusion.7), channel_id=1, source_target_pairs={{0,1},{1,0},{2,3},{3,2},{4,5},{5,4},{6,7},{7,6},{8,9},{9,8},{10,11... | collective-permute-start | bytes 98312 | tf_op jit(solution)/shard_map/ppermute | solution.py:297
  62.3 7.7 %collective-permute-start.10 = (f32[144,128]{1,0:T(8,128)S(1)}, f32[144,128]{1,0:T(8,128)S(1)}, u32[]{:S(2)}, u32[]{:S(2)}) collective-permute-start(f32[144,128]{1,0:T(8,128)S(1)} %get-tuple-element.48), channel_id=1, source_target_pairs={{0,4},{1,5},{2,6},{3,7},{4,0},{5,1},{6,2},{7,3},{8,12},{9,13},{10,... | collective-permute-start | bytes 221192 | tf_op jit(solution)/shard_map/ppermute | solution.py:297
  62.4 12.8 %collective-permute-start.11 = (f32[144,128]{1,0:T(8,128)S(1)}, f32[144,128]{1,0:T(8,128)S(1)}, u32[]{:S(2)}, u32[]{:S(2)}) collective-permute-start(f32[144,128]{1,0:T(8,128)S(1)} %get-tuple-element.49), channel_id=1, source_target_pairs={{0,6},{1,7},{2,4},{3,5},{4,2},{5,3},{6,0},{7,1},{8,14},{9,15},{10,... | collective-permute-start | bytes 221192 | tf_op jit(solution)/shard_map/ppermute | solution.py:297
  66.5 8.6 %collective-permute-start.9 = (f32[144,128]{1,0:T(8,128)S(1)}, f32[144,128]{1,0:T(8,128)S(1)}, u32[]{:S(2)}, u32[]{:S(2)}) collective-permute-start(f32[144,128]{1,0:T(8,128)S(1)} %get-tuple-element.47), channel_id=1, source_target_pairs={{0,2},{1,3},{2,0},{3,1},{4,6},{5,7},{6,4},{7,5},{8,10},{9,11},{10,... | collective-permute-start | bytes 221192 | tf_op jit(solution)/shard_map/ppermute | solution.py:297
  76.4 15.8 %collective-permute-start.12 = (f32[8,128]{1,0:T(8,128)S(1)}, f32[8,128]{1,0:T(8,128)S(1)}, u32[]{:S(2)}, u32[]{:S(2)}) collective-permute-start(f32[8,128]{1,0:T(8,128)S(1)} %dynamic-slice_bitcast_fusion.7), channel_id=1, source_target_pairs={{0,8},{1,9},{2,10},{3,11},{4,12},{5,13},{6,14},{7,15},{8,0},{9,1},... | collective-permute-start | bytes 12296 | tf_op jit(solution)/shard_map/ppermute | solution.py:297
  79.5 13.4 %collective-permute-start.13 = (f32[16,2048]{1,0:T(8,128)S(1)}, f32[16,2048]{1,0:T(8,128)S(1)}, u32[]{:S(2)}, u32[]{:S(2)}) collective-permute-start(f32[16,2048]{1,0:T(8,128)S(1)} %get-tuple-element.40), channel_id=1, source_target_pairs={{0,16},{16,0},{32,48},{48,32},{64,80},{80,64},{96,112},{112,96},{1... | collective-permute-start | bytes 393224 | tf_op jit(solution)/shard_map/ppermute | solution.py:364
  79.5 13.4 %collective-permute-start.14 = (f32[16,2048]{1,0:T(8,128)S(1)}, f32[16,2048]{1,0:T(8,128)S(1)}, u32[]{:S(2)}, u32[]{:S(2)}) collective-permute-start(f32[16,2048]{1,0:T(8,128)S(1)} %get-tuple-element.41), channel_id=1, source_target_pairs={{16,32},{32,16},{48,64},{64,48},{80,96},{96,80},{17,33},{33,17},{4... | collective-permute-start | bytes 393224 | tf_op jit(solution)/shard_map/ppermute | solution.py:365

commit v5 on v4

--- a/solution.py
+++ b/solution.py
@@ -344,9 +344,9 @@
 
     tiled = tile_view(orbitals).reshape(count * rows, LANES)
     v = tile_view(potential)
+    to_core, to_chip = extract(tiled, count, rows)
+    orbitals, to_core, to_chip, v = lax.optimization_barrier((orbitals, to_core, to_chip, v))
     v_z = jnp.concatenate([v, exchange(v, 8)])
-    to_core, to_chip = extract(tiled, count, rows)
-    orbitals, to_core, to_chip, v, v_z = lax.optimization_barrier((orbitals, to_core, to_chip, v, v_z))
     from_core = exchange(to_core, 1)
     from_chip = lax.ppermute(to_chip, every, [(i, (i + 1 ^ 1) - 1) for i in range(1, devices - 1)])
     received = lax.all_to_all(orbitals, "col", split_axis=0, concat_axis=0, tiled=True)

time: 96 us -> 95.3 us (level)
  waiting for transfers between devices: 33.8 us -> 37.6 us
  starting transfers between devices: 36.5 us -> 32.9 us
    ppermute x11, waiting for transfers between devices: 13.4 us -> 19.3 us  [exchange(): lax.ppermute(x, every, [(i, i ^ mask) for i in range(lax.axis_size(every))])]
    ppermute x1, starting transfers between devices: 4.47 us -> 0.09 us  [reduce_z_hi(): return pick(0) + lax.ppermute(pick(1), ('row', 'col'), pairs)]
    ppermute x1, waiting for transfers between devices: 1.89 us -> 0.01 us  [reduce_z_hi(): return pick(0) + lax.ppermute(pick(1), ('row', 'col'), pairs)]
    ppermute x1, starting transfers between devices: 7.06 us -> 8.42 us  [local(): lax.ppermute(to_chip, every, [(i, (i + 1 ^ 1) - 1) for i in range(1, devi...]
  transfers between devices with their start and end apart: 16 -> 16, of which waited for: 7 -> 10; matrix products, arithmetic and copies ran while one was open for 1% -> 1% of each run, Pallas kernels for 16% -> 15%
where the time goes in v5:
time: 95.3 us; the launch traced here: 94.9 us
  waiting for transfers between devices  37.6 us (39%)
  starting transfers between devices  32.9 us (35%)
  Pallas kernels  18.5 us (19%)
  local copies, waits for them, and re-layouts  5.06 us (5%)
    ppermute x11, waiting for transfers between devices, exchange(): lax.ppermute(x, every, [(i, i ^ mask) for i in range(lax.axis_size(every))])  19.3 us
    ppermute x1, waiting for transfers between devices, local(): lax.ppermute(to_chip, every, [(i, (i + 1 ^ 1) - 1) for i in range(1, devi...  18.2 us
    ppermute x11, starting transfers between devices, exchange(): lax.ppermute(x, every, [(i, i ^ mask) for i in range(lax.axis_size(every))])  14.2 us
    ppermute x1, starting transfers between devices, local(): lax.ppermute(to_chip, every, [(i, (i + 1 ^ 1) - 1) for i in range(1, devi...  8.42 us
    pallas_call x1, Pallas kernels, to_block(): pl.pallas_call(functools.partial(block_kernel, sources, block, rows), gri...  7.47 us
    pallas_call x1, Pallas kernels, gram(): pl.pallas_call(functools.partial(gram_kernel, count, rows), out_shape=[ja...  5.3 us
    ppermute x1, starting transfers between devices, local(): lax.ppermute(far, 'row', [(i, (i + 1 ^ 1) - 1) for i in range(1, n_row -...  4.81 us
    all_to_all x1, starting transfers between devices, local(): lax.all_to_all(orbitals, 'col', split_axis=0, concat_axis=0, tiled=True)  4.57 us
  transfers between devices with their start and end apart: 16, of which 10 were waited for; matrix products, arithmetic and copies ran while one was open for 1% of the time, Pallas kernels for 15%

profile of v5, /device:TPU:24, one launch (start us, length us, event | category | flops | bytes accessed | tf_op | source)
XLA Modules:
  0.0 94.9 jit_solution(11178555435283761638)
XLA Ops:
  0.6 0.0 copy-start
  0.6 2.2 %copy-done = f32[256,2,2048]{2,1,0:T(2,128)S(1)} copy-done((f32[256,2,2048]{2,1,0:T(2,128)S(1)}, f32[256,2,2048]{2,1,0:T(2,128)}, u32[]{:S(2)}) %copy-start) | copy-done | bytes 4194328
  2.8 1.1 %shard_map.57 = (f32[2048,128]{1,0:T(8,128)}, f32[2048,128]{1,0:T(8,128)S(1)}) custom-call(f32[8192,128]{1,0:T(8,128)S(1)} %bitcast.57), custom_call_target="tpu_custom_call" | custom-call | bytes 6291456 | tf_op jit(solution)/shard_map/pallas_call | solution.py:43
  3.9 0.0 copy-start.2
  3.9 0.0 collective-permute-start
  3.9 8.4 %collective-permute-start.1 = (f32[2048,128]{1,0:T(8,128)S(1)}, f32[2048,128]{1,0:T(8,128)S(1)}, u32[]{:S(2)}, u32[]{:S(2)}) collective-permute-start(f32[2048,128]{1,0:T(8,128)S(1)} %get-tuple-element.30), channel_id=1, source_target_pairs={{1,2},{2,1},{3,4},{4,3},{5,6},{6,5},{7,8},{8,7},{9,10},{10,9},{11,... | collective-permute-start | bytes 3145736 | tf_op jit(solution)/shard_map/ppermute | solution.py:351
  12.4 4.6 %all-to-all-start = ((f32[256,2,2048]{2,1,0:T(2,128)}), f32[256,2,2048]{2,1,0:T(2,128)}, u32[]{:S(2)}, u32[]{:S(2)}) async-start(f32[256,2,2048]{2,1,0:T(2,128)} %param.2), calls=%async_computation | async-start | bytes 8388608 | tf_op jit(solution)/shard_map/all_to_all | solution.py:352
  16.9 0.0 copy-done.2
  16.9 0.0 copy-start.1
  17.0 2.2 %copy-done.1 = f32[256,2,2048]{2,1,0:T(2,128)S(1)} copy-done((f32[256,2,2048]{2,1,0:T(2,128)S(1)}, f32[256,2,2048]{2,1,0:T(2,128)}, u32[]{:S(2)}) %copy-start.1) | copy-done | bytes 4194328
  19.2 5.3 %shard_map.58 = (f32[256,512]{1,0:T(8,128)S(1)}, f32[2048,128]{1,0:T(8,128)S(1)}, f32[2048,128]{1,0:T(8,128)S(1)}) custom-call(f32[8192,128]{1,0:T(8,128)S(1)} %bitcast.58, f32[32,128]{1,0:T(8,128)S(1)} %bitcast.59), custom_call_target="tpu_custom_call" | custom-call | flops 107374182400 | bytes 6291456 | tf_op jit(solution)/shard_map/pallas_call | solution.py:105
  24.5 0.0 collective-permute-done.core_ref
  24.5 18.2 %collective-permute-done.1.chip_ref = f32[2048,128]{1,0:T(8,128)S(1)} collective-permute-done((f32[2048,128]{1,0:T(8,128)S(1)}, f32[2048,128]{1,0:T(8,128)S(1)}, u32[]{:S(2)}, u32[]{:S(2)}) %collective-permute-start.1) | collective-permute-done | bytes 1048608 | tf_op jit(solution)/shard_map/ppermute | solution.py:351
  42.7 1.6 %shard_map.59 = (f32[64,1024]{1,0:T(8,128)S(1)}, f32[64,1024]{1,0:T(8,128)S(1)}) custom-call(f32[256,512]{1,0:T(8,128)S(1)} %get-tuple-element.26.g_ref, f32[2048,128]{1,0:T(8,128)S(1)} %get-tuple-element.27.by_core_ref, f32[2048,128]{1,0:T(8,128)S(1)} %collective-permute-done.core_ref, f32[2048,128]{1,0:T(8,128)S(1)} %get-tuple-element.29.by_chip_ref, ...), custom_call_target="tpu_custom_call" | custom-call | flops 805306368 | bytes 4194304 | tf_op jit(solution)/shard_map/pallas_call | solution.py:144
  44.3 0.1 collective-permute-start.2
  44.4 1.5 %collective-permute-done.2 = f32[64,1024]{1,0:T(8,128)S(1)} collective-permute-done((f32[64,1024]{1,0:T(8,128)S(1)}, f32[64,1024]{1,0:T(8,128)S(1)}, u32[]{:S(2)}, u32[]{:S(2)}) %collective-permute-start.2) | collective-permute-done | bytes 262176 | tf_op jit(solution)/shard_map/ppermute | solution.py:297
  46.0 0.5 collective-permute-start.3
  46.5 0.6 collective-permute-start.4
  47.1 3.7 %collective-permute-start.5 = (f32[16,1024]{1,0:T(8,128)S(1)}, f32[16,1024]{1,0:T(8,128)S(1)}, u32[]{:S(2)}, u32[]{:S(2)}) collective-permute-start(f32[16,1024]{1,0:T(8,128)S(1)} %get-tuple-element.43), channel_id=1, source_target_pairs={{0,96},{1,97},{2,98},{3,99},{4,100},{5,101},{6,102},{7,103},{8,104... | collective-permute-start | bytes 196616 | tf_op jit(solution)/shard_map/ppermute | solution.py:297
  50.7 0.0 collective-permute-start.7
  50.7 0.1 collective-permute-done.3
  50.9 1.5 %collective-permute-done.4 = f32[16,1024]{1,0:T(8,128)S(1)} collective-permute-done((f32[16,1024]{1,0:T(8,128)S(1)}, f32[16,1024]{1,0:T(8,128)S(1)}, u32[]{:S(2)}, u32[]{:S(2)}) %collective-permute-start.4) | collective-permute-done | bytes 65568 | tf_op jit(solution)/shard_map/ppermute | solution.py:297
  52.4 0.9 collective-permute-done.5
  53.3 0.1 collective-permute-start.6
  53.4 10.0 %collective-permute-done.7 = f32[32,128]{1,0:T(8,128)S(1)} collective-permute-done((f32[32,128]{1,0:T(8,128)S(1)}, f32[32,128]{1,0:T(8,128)S(1)}, u32[]{:S(2)}, u32[]{:S(2)}) %collective-permute-start.7) | collective-permute-done | bytes 16416 | tf_op jit(solution)/shard_map/ppermute | solution.py:297
  63.4 0.2 collective-permute-start.8
  63.6 0.0 collective-permute-done.6
  63.6 0.9 collective-permute-done.8
  64.6 0.1 collective-permute-start.10
  64.7 5.4 %collective-permute-start.11 = (f32[144,128]{1,0:T(8,128)S(1)}, f32[144,128]{1,0:T(8,128)S(1)}, u32[]{:S(2)}, u32[]{:S(2)}) collective-permute-start(f32[144,128]{1,0:T(8,128)S(1)} %get-tuple-element.47), channel_id=1, source_target_pairs={{0,6},{1,7},{2,4},{3,5},{4,2},{5,3},{6,0},{7,1},{8,14},{9,15},{10,... | collective-permute-start | bytes 221192 | tf_op jit(solution)/shard_map/ppermute | solution.py:297
  70.0 0.0 collective-permute-start.9
  70.0 2.8 %collective-permute-done.10.v2_ref = f32[144,128]{1,0:T(8,128)S(1)} collective-permute-done((f32[144,128]{1,0:T(8,128)S(1)}, f32[144,128]{1,0:T(8,128)S(1)}, u32[]{:S(2)}, u32[]{:S(2)}) %collective-permute-start.10) | collective-permute-done | bytes 73760 | tf_op jit(solution)/shard_map/ppermute | solution.py:297
  72.9 0.4 collective-permute-done.11.v3_ref
  73.3 1.2 %collective-permute-done.9.v1_ref = f32[144,128]{1,0:T(8,128)S(1)} collective-permute-done((f32[144,128]{1,0:T(8,128)S(1)}, f32[144,128]{1,0:T(8,128)S(1)}, u32[]{:S(2)}, u32[]{:S(2)}) %collective-permute-start.9) | collective-permute-done | bytes 73760 | tf_op jit(solution)/shard_map/ppermute | solution.py:297
  74.5 0.0 all-to-all-done
  74.5 1.2 %shard_map.60 = (f32[16,2048]{1,0:T(8,128)S(1)}, f32[16,2048]{1,0:T(8,128)S(1)}) custom-call(f32[16,512,128]{2,1,0:T(8,128)} %bitcast.22.low_ref.high_ref, f32[16,512,128]{2,1,0:T(8,128)} %bitcast.22.low_ref.high_ref), custom_call_target="tpu_custom_call" | custom-call | bytes 262144 | tf_op jit(solution)/shard_map/pallas_call | solution.py:178
  75.7 3.7 %collective-permute-start.12 = (f32[8,128]{1,0:T(8,128)S(1)}, f32[8,128]{1,0:T(8,128)S(1)}, u32[]{:S(2)}, u32[]{:S(2)}) collective-permute-start(f32[8,128]{1,0:T(8,128)S(1)} %dynamic-slice_bitcast_fusion.7), channel_id=1, source_target_pairs={{0,8},{1,9},{2,10},{3,11},{4,12},{5,13},{6,14},{7,15},{8,0},{9,1},... | collective-permute-start | bytes 12296 | tf_op jit(solution)/shard_map/ppermute | solution.py:297
  79.4 0.8 collective-permute-start.13
  80.1 4.8 %collective-permute-start.14 = (f32[16,2048]{1,0:T(8,128)S(1)}, f32[16,2048]{1,0:T(8,128)S(1)}, u32[]{:S(2)}, u32[]{:S(2)}) collective-permute-start(f32[16,2048]{1,0:T(8,128)S(1)} %get-tuple-element.39), channel_id=1, source_target_pairs={{16,32},{32,16},{48,64},{64,48},{80,96},{96,80},{17,33},{33,17},{4... | collective-permute-start | bytes 393224 | tf_op jit(solution)/shard_map/ppermute | solution.py:365
  85.0 7.5 %shard_map.61 = (f32[16,32,2048]{2,1,0:T(8,128)}, f32[16,32,2048]{2,1,0:T(8,128)}, f32[2,16,8,2048]{3,2,1,0:T(8,128)S(1)}) custom-call(f32[16,16,32,128]{3,2,1,0:T(8,128)} %bitcast.27.x_ref, f32[128,128]{1,0:T(8,128)S(1)} %pad_maximum_fusion.9.v_own_ref, f32[144,128]{1,0:T(8,128)S(1)} %collective-permute-done.9.v1_ref, ...), custom_call_target="tpu_custom_call" | custom-call | bytes 12582912 | tf_op jit(solution)/shard_map/pallas_call | solution.py:235
  92.4 0.0 collective-permute-done.12
  92.5 0.6 fusion.4
  93.0 0.0 collective-permute-done.13.near_ref
  93.0 0.0 collective-permute-done.14.far_ref
  93.0 1.8 %shard_map.62 = f32[16,32,2048]{2,1,0:T(8,128)} custom-call(f32[16,2048]{1,0:T(8,128)S(1)} %collective-permute-done.13.near_ref, f32[16,2048]{1,0:T(8,128)S(1)} %collective-permute-done.14.far_ref, f32[2,16,8,2048]{3,2,1,0:T(8,128)S(1)} %get-tuple-element.40.sides_ref, f32[16,32,2048]{2,1,0:T(8,128)} %get-tuple-element.41.applied_ref), custom_call_target="tpu_custom_call", output_to_operand_aliasing={{}: (3, {})} | custom-call | bytes 1048576 | tf_op jit(solution)/shard_map/pallas_call | solution.py:280
  (14 shorter events, 0.2 us)
Async XLA Ops:
  0.6 2.2 %copy-start = (f32[256,2,2048]{2,1,0:T(2,128)S(1)}, f32[256,2,2048]{2,1,0:T(2,128)}, u32[]{:S(2)}) copy-start(f32[256,2,2048]{2,1,0:T(2,128)} %param.2) | copy-start | bytes 12582916
  3.9 13.0 %copy-start.2 = (f32[2,2048]{1,0:T(2,128)S(1)}, f32[2,2048]{1,0:T(2,128)}, u32[]{:S(2)}) copy-start(f32[2,2048]{1,0:T(2,128)} %param.3) | copy-start | bytes 49156
  3.9 20.5 %collective-permute-start = (f32[2048,128]{1,0:T(8,128)}, f32[2048,128]{1,0:T(8,128)S(1)}, u32[]{:S(2)}, u32[]{:S(2)}) collective-permute-start(f32[2048,128]{1,0:T(8,128)} %get-tuple-element.28), channel_id=1, source_target_pairs={{0,1},{1,0},{2,3},{3,2},{4,5},{5,4},{6,7},{7,6},{8,9},{9,8},{10,11... | collective-permute-start | bytes 3145736 | tf_op jit(solution)/shard_map/ppermute | solution.py:297
  3.9 38.8 %collective-permute-start.1 = (f32[2048,128]{1,0:T(8,128)S(1)}, f32[2048,128]{1,0:T(8,128)S(1)}, u32[]{:S(2)}, u32[]{:S(2)}) collective-permute-start(f32[2048,128]{1,0:T(8,128)S(1)} %get-tuple-element.30), channel_id=1, source_target_pairs={{1,2},{2,1},{3,4},{4,3},{5,6},{6,5},{7,8},{8,7},{9,10},{10,9},{11,... | collective-permute-start | bytes 3145736 | tf_op jit(solution)/shard_map/ppermute | solution.py:351
  12.4 62.1 %all-to-all-start = ((f32[256,2,2048]{2,1,0:T(2,128)}), f32[256,2,2048]{2,1,0:T(2,128)}, u32[]{:S(2)}, u32[]{:S(2)}) async-start(f32[256,2,2048]{2,1,0:T(2,128)} %param.2), calls=%async_computation | async-start | bytes 8388608 | tf_op jit(solution)/shard_map/all_to_all | solution.py:352
  16.9 2.2 %copy-start.1 = (f32[256,2,2048]{2,1,0:T(2,128)S(1)}, f32[256,2,2048]{2,1,0:T(2,128)}, u32[]{:S(2)}) copy-start(f32[256,2,2048]{2,1,0:T(2,128)} %param.2) | copy-start | bytes 12582916
  44.3 1.6 %collective-permute-start.2 = (f32[64,1024]{1,0:T(8,128)S(1)}, f32[64,1024]{1,0:T(8,128)S(1)}, u32[]{:S(2)}, u32[]{:S(2)}) collective-permute-start(f32[64,1024]{1,0:T(8,128)S(1)} %get-tuple-element.32), channel_id=1, source_target_pairs={{0,1},{1,0},{2,3},{3,2},{4,5},{5,4},{6,7},{7,6},{8,9},{9,8},{10,11... | collective-permute-start | bytes 786440 | tf_op jit(solution)/shard_map/ppermute | solution.py:297
  46.0 4.9 %collective-permute-start.3 = (f32[16,1024]{1,0:T(8,128)S(1)}, f32[16,1024]{1,0:T(8,128)S(1)}, u32[]{:S(2)}, u32[]{:S(2)}) collective-permute-start(f32[16,1024]{1,0:T(8,128)S(1)} %get-tuple-element.42), channel_id=1, source_target_pairs={{0,32},{1,33},{2,34},{3,35},{4,36},{5,37},{6,38},{7,39},{8,40},{9,... | collective-permute-start | bytes 196616 | tf_op jit(solution)/shard_map/ppermute | solution.py:297
  46.5 5.9 %collective-permute-start.4 = (f32[16,1024]{1,0:T(8,128)S(1)}, f32[16,1024]{1,0:T(8,128)S(1)}, u32[]{:S(2)}, u32[]{:S(2)}) collective-permute-start(f32[16,1024]{1,0:T(8,128)S(1)} %get-tuple-element.44), channel_id=1, source_target_pairs={{0,64},{1,65},{2,66},{3,67},{4,68},{5,69},{6,70},{7,71},{8,72},{9,... | collective-permute-start | bytes 196616 | tf_op jit(solution)/shard_map/ppermute | solution.py:297
  47.1 6.2 %collective-permute-start.5 = (f32[16,1024]{1,0:T(8,128)S(1)}, f32[16,1024]{1,0:T(8,128)S(1)}, u32[]{:S(2)}, u32[]{:S(2)}) collective-permute-start(f32[16,1024]{1,0:T(8,128)S(1)} %get-tuple-element.43), channel_id=1, source_target_pairs={{0,96},{1,97},{2,98},{3,99},{4,100},{5,101},{6,102},{7,103},{8,104... | collective-permute-start | bytes 196616 | tf_op jit(solution)/shard_map/ppermute | solution.py:297
  50.7 12.6 %collective-permute-start.7 = (f32[32,128]{1,0:T(8,128)S(1)}, f32[32,128]{1,0:T(8,128)S(1)}, u32[]{:S(2)}, u32[]{:S(2)}) collective-permute-start(f32[32,128]{1,0:T(8,128)S(1)} %bitcast.60), channel_id=1, source_target_pairs={{0,8},{1,9},{2,10},{3,11},{4,12},{5,13},{6,14},{7,15},{8,0},{9,1},... | collective-permute-start | bytes 49160 | tf_op jit(solution)/shard_map/ppermute | solution.py:297
  53.3 10.3 %collective-permute-start.6 = (f32[8,1024]{1,0:T(8,128)S(1)}, f32[8,1024]{1,0:T(8,128)S(1)}, u32[]{:S(2)}, u32[]{:S(2)}) collective-permute-start(f32[8,1024]{1,0:T(8,128)S(1)} %dynamic-slice_bitcast_fusion.3), channel_id=1, source_target_pairs={{0,24},{1,25},{2,26},{3,27},{4,28},{5,29},{6,30},{7,31},{8,16},{9,... | collective-permute-start | bytes 98312 | tf_op jit(solution)/shard_map/ppermute | solution.py:318
  63.4 1.2 %collective-permute-start.8 = (f32[64,128]{1,0:T(8,128)S(1)}, f32[64,128]{1,0:T(8,128)S(1)}, u32[]{:S(2)}, u32[]{:S(2)}) collective-permute-start(f32[64,128]{1,0:T(8,128)S(1)} %pad_maximum_fusion.10), channel_id=1, source_target_pairs={{0,1},{1,0},{2,3},{3,2},{4,5},{5,4},{6,7},{7,6},{8,9},{9,8},{10,11... | collective-permute-start | bytes 98312 | tf_op jit(solution)/shard_map/ppermute | solution.py:297
  64.6 8.3 %collective-permute-start.10 = (f32[144,128]{1,0:T(8,128)S(1)}, f32[144,128]{1,0:T(8,128)S(1)}, u32[]{:S(2)}, u32[]{:S(2)}) collective-permute-start(f32[144,128]{1,0:T(8,128)S(1)} %get-tuple-element.46), channel_id=1, source_target_pairs={{0,4},{1,5},{2,6},{3,7},{4,0},{5,1},{6,2},{7,3},{8,12},{9,13},{10,... | collective-permute-start | bytes 221192 | tf_op jit(solution)/shard_map/ppermute | solution.py:297
  64.7 8.6 %collective-permute-start.11 = (f32[144,128]{1,0:T(8,128)S(1)}, f32[144,128]{1,0:T(8,128)S(1)}, u32[]{:S(2)}, u32[]{:S(2)}) collective-permute-start(f32[144,128]{1,0:T(8,128)S(1)} %get-tuple-element.47), channel_id=1, source_target_pairs={{0,6},{1,7},{2,4},{3,5},{4,2},{5,3},{6,0},{7,1},{8,14},{9,15},{10,... | collective-permute-start | bytes 221192 | tf_op jit(solution)/shard_map/ppermute | solution.py:297
  70.0 4.4 %collective-permute-start.9 = (f32[144,128]{1,0:T(8,128)S(1)}, f32[144,128]{1,0:T(8,128)S(1)}, u32[]{:S(2)}, u32[]{:S(2)}) collective-permute-start(f32[144,128]{1,0:T(8,128)S(1)} %get-tuple-element.45), channel_id=1, source_target_pairs={{0,2},{1,3},{2,0},{3,1},{4,6},{5,7},{6,4},{7,5},{8,10},{9,11},{10,... | collective-permute-start | bytes 221192 | tf_op jit(solution)/shard_map/ppermute | solution.py:297
  75.7 16.7 %collective-permute-start.12 = (f32[8,128]{1,0:T(8,128)S(1)}, f32[8,128]{1,0:T(8,128)S(1)}, u32[]{:S(2)}, u32[]{:S(2)}) collective-permute-start(f32[8,128]{1,0:T(8,128)S(1)} %dynamic-slice_bitcast_fusion.7), channel_id=1, source_target_pairs={{0,8},{1,9},{2,10},{3,11},{4,12},{5,13},{6,14},{7,15},{8,0},{9,1},... | collective-permute-start | bytes 12296 | tf_op jit(solution)/shard_map/ppermute | solution.py:297
  79.4 13.7 %collective-permute-start.13 = (f32[16,2048]{1,0:T(8,128)S(1)}, f32[16,2048]{1,0:T(8,128)S(1)}, u32[]{:S(2)}, u32[]{:S(2)}) collective-permute-start(f32[16,2048]{1,0:T(8,128)S(1)} %get-tuple-element.38), channel_id=1, source_target_pairs={{0,16},{16,0},{32,48},{48,32},{64,80},{80,64},{96,112},{112,96},{1... | collective-permute-start | bytes 393224 | tf_op jit(solution)/shard_map/ppermute | solution.py:364
  80.1 12.9 %collective-permute-start.14 = (f32[16,2048]{1,0:T(8,128)S(1)}, f32[16,2048]{1,0:T(8,128)S(1)}, u32[]{:S(2)}, u32[]{:S(2)}) collective-permute-start(f32[16,2048]{1,0:T(8,128)S(1)} %get-tuple-element.39), channel_id=1, source_target_pairs={{16,32},{32,16},{48,64},{64,48},{80,96},{96,80},{17,33},{33,17},{4... | collective-permute-start | bytes 393224 | tf_op jit(solution)/shard_map/ppermute | solution.py:365

commit v6 on v5

--- a/solution.py
+++ b/solution.py
@@ -255,19 +255,15 @@
 def fix_kernel(near_ref, far_ref, sides_ref, applied_ref, out_ref, work_ref, sem):
     orbitals, planes, _ = applied_ref.shape
 
-    def run(edge_refs):
-        for e, edge_ref in enumerate(edge_refs):
-            for o in range(orbitals):
-                row = 7 * e
-                work_ref[e, o] = sides_ref[e, o]
-                work_ref[e, o, pl.ds(row, 1), :] = sides_ref[e, o, pl.ds(row, 1), :] - 0.5 * edge_ref[pl.ds(o, 1), :]
-
     even = lax.rem(lax.axis_index("row"), 2) == 0
-    pl.when(even)(lambda: run((far_ref, near_ref)))
-    pl.when(jnp.logical_not(even))(lambda: run((near_ref, far_ref)))
     copies = []
     for e in (0, 1):
+        row = pl.ds(7 * e, 1)
         for o in range(orbitals):
+            near, far = near_ref[pl.ds(o, 1), :], far_ref[pl.ds(o, 1), :]
+            edge = jnp.where(even, near, far) if e else jnp.where(even, far, near)
+            work_ref[e, o] = sides_ref[e, o]
+            work_ref[e, o, row, :] = sides_ref[e, o, row, :] - 0.5 * edge
             target = out_ref.at[o, pl.ds(e * (planes - 8), 8), :]
             copies.append(pltpu.make_async_copy(work_ref.at[e, o], target, sem.at[e, o]))
             copies[-1].start()

time: 95.3 us -> 95.1 us (level)
  no operation moved by 1% of the time
where the time goes in v6:
time: 95.1 us; the launch traced here: 94.6 us
  waiting for transfers between devices  37.6 us (40%)
  starting transfers between devices  32.9 us (35%)
  Pallas kernels  18.2 us (19%)
  local copies, waits for them, and re-layouts  5.06 us (5%)
    ppermute x11, waiting for transfers between devices, exchange(): lax.ppermute(x, every, [(i, i ^ mask) for i in range(lax.axis_size(every))])  19.3 us
    ppermute x1, waiting for transfers between devices, local(): lax.ppermute(to_chip, every, [(i, (i + 1 ^ 1) - 1) for i in range(1, devi...  18.2 us
    ppermute x11, starting transfers between devices, exchange(): lax.ppermute(x, every, [(i, i ^ mask) for i in range(lax.axis_size(every))])  14.2 us
    ppermute x1, starting transfers between devices, local(): lax.ppermute(to_chip, every, [(i, (i + 1 ^ 1) - 1) for i in range(1, devi...  8.42 us
    pallas_call x1, Pallas kernels, to_block(): pl.pallas_call(functools.partial(block_kernel, sources, block, rows), gri...  7.47 us
    pallas_call x1, Pallas kernels, gram(): pl.pallas_call(functools.partial(gram_kernel, count, rows), out_shape=[ja...  5.3 us
    ppermute x1, starting transfers between devices, local(): lax.ppermute(far, 'row', [(i, (i + 1 ^ 1) - 1) for i in range(1, n_row -...  4.81 us
    all_to_all x1, starting transfers between devices, local(): lax.all_to_all(orbitals, 'col', split_axis=0, concat_axis=0, tiled=True)  4.57 us
  transfers between devices with their start and end apart: 16, of which 10 were waited for; matrix products, arithmetic and copies ran while one was open for 1% of the time, Pallas kernels for 15%

profile of v6, /device:TPU:24, one launch (start us, length us, event | category | flops | bytes accessed | tf_op | source)
XLA Modules:
  0.0 94.6 jit_solution(14087518030212231638)
XLA Ops:
  0.6 0.0 copy-start
  0.6 2.2 %copy-done = f32[256,2,2048]{2,1,0:T(2,128)S(1)} copy-done((f32[256,2,2048]{2,1,0:T(2,128)S(1)}, f32[256,2,2048]{2,1,0:T(2,128)}, u32[]{:S(2)}) %copy-start) | copy-done | bytes 4194328
  2.8 1.1 %shard_map.57 = (f32[2048,128]{1,0:T(8,128)}, f32[2048,128]{1,0:T(8,128)S(1)}) custom-call(f32[8192,128]{1,0:T(8,128)S(1)} %bitcast.57), custom_call_target="tpu_custom_call" | custom-call | bytes 6291456 | tf_op jit(solution)/shard_map/pallas_call | solution.py:43
  3.9 0.0 copy-start.2
  3.9 0.0 collective-permute-start
  3.9 8.4 %collective-permute-start.1 = (f32[2048,128]{1,0:T(8,128)S(1)}, f32[2048,128]{1,0:T(8,128)S(1)}, u32[]{:S(2)}, u32[]{:S(2)}) collective-permute-start(f32[2048,128]{1,0:T(8,128)S(1)} %get-tuple-element.30), channel_id=1, source_target_pairs={{1,2},{2,1},{3,4},{4,3},{5,6},{6,5},{7,8},{8,7},{9,10},{10,9},{11,... | collective-permute-start | bytes 3145736 | tf_op jit(solution)/shard_map/ppermute | solution.py:347
  12.4 4.6 %all-to-all-start = ((f32[256,2,2048]{2,1,0:T(2,128)}), f32[256,2,2048]{2,1,0:T(2,128)}, u32[]{:S(2)}, u32[]{:S(2)}) async-start(f32[256,2,2048]{2,1,0:T(2,128)} %param.2), calls=%async_computation | async-start | bytes 8388608 | tf_op jit(solution)/shard_map/all_to_all | solution.py:348
  16.9 0.0 copy-done.2
  16.9 0.0 copy-start.1
  17.0 2.2 %copy-done.1 = f32[256,2,2048]{2,1,0:T(2,128)S(1)} copy-done((f32[256,2,2048]{2,1,0:T(2,128)S(1)}, f32[256,2,2048]{2,1,0:T(2,128)}, u32[]{:S(2)}) %copy-start.1) | copy-done | bytes 4194328
  19.2 5.3 %shard_map.58 = (f32[256,512]{1,0:T(8,128)S(1)}, f32[2048,128]{1,0:T(8,128)S(1)}, f32[2048,128]{1,0:T(8,128)S(1)}) custom-call(f32[8192,128]{1,0:T(8,128)S(1)} %bitcast.58, f32[32,128]{1,0:T(8,128)S(1)} %bitcast.59), custom_call_target="tpu_custom_call" | custom-call | flops 107374182400 | bytes 6291456 | tf_op jit(solution)/shard_map/pallas_call | solution.py:105
  24.5 0.0 collective-permute-done.core_ref
  24.5 18.2 %collective-permute-done.1.chip_ref = f32[2048,128]{1,0:T(8,128)S(1)} collective-permute-done((f32[2048,128]{1,0:T(8,128)S(1)}, f32[2048,128]{1,0:T(8,128)S(1)}, u32[]{:S(2)}, u32[]{:S(2)}) %collective-permute-start.1) | collective-permute-done | bytes 1048608 | tf_op jit(solution)/shard_map/ppermute | solution.py:347
  42.7 1.6 %shard_map.59 = (f32[64,1024]{1,0:T(8,128)S(1)}, f32[64,1024]{1,0:T(8,128)S(1)}) custom-call(f32[256,512]{1,0:T(8,128)S(1)} %get-tuple-element.26.g_ref, f32[2048,128]{1,0:T(8,128)S(1)} %get-tuple-element.27.by_core_ref, f32[2048,128]{1,0:T(8,128)S(1)} %collective-permute-done.core_ref, f32[2048,128]{1,0:T(8,128)S(1)} %get-tuple-element.29.by_chip_ref, ...), custom_call_target="tpu_custom_call" | custom-call | flops 805306368 | bytes 4194304 | tf_op jit(solution)/shard_map/pallas_call | solution.py:144
  44.3 0.1 collective-permute-start.2
  44.4 1.5 %collective-permute-done.2 = f32[64,1024]{1,0:T(8,128)S(1)} collective-permute-done((f32[64,1024]{1,0:T(8,128)S(1)}, f32[64,1024]{1,0:T(8,128)S(1)}, u32[]{:S(2)}, u32[]{:S(2)}) %collective-permute-start.2) | collective-permute-done | bytes 262176 | tf_op jit(solution)/shard_map/ppermute | solution.py:293
  46.0 0.5 collective-permute-start.3
  46.5 0.6 collective-permute-start.4
  47.1 3.7 %collective-permute-start.5 = (f32[16,1024]{1,0:T(8,128)S(1)}, f32[16,1024]{1,0:T(8,128)S(1)}, u32[]{:S(2)}, u32[]{:S(2)}) collective-permute-start(f32[16,1024]{1,0:T(8,128)S(1)} %get-tuple-element.43), channel_id=1, source_target_pairs={{0,96},{1,97},{2,98},{3,99},{4,100},{5,101},{6,102},{7,103},{8,104... | collective-permute-start | bytes 196616 | tf_op jit(solution)/shard_map/ppermute | solution.py:293
  50.7 0.0 collective-permute-start.7
  50.7 0.1 collective-permute-done.3
  50.9 1.5 %collective-permute-done.4 = f32[16,1024]{1,0:T(8,128)S(1)} collective-permute-done((f32[16,1024]{1,0:T(8,128)S(1)}, f32[16,1024]{1,0:T(8,128)S(1)}, u32[]{:S(2)}, u32[]{:S(2)}) %collective-permute-start.4) | collective-permute-done | bytes 65568 | tf_op jit(solution)/shard_map/ppermute | solution.py:293
  52.4 0.9 collective-permute-done.5
  53.3 0.1 collective-permute-start.6
  53.4 10.0 %collective-permute-done.7 = f32[32,128]{1,0:T(8,128)S(1)} collective-permute-done((f32[32,128]{1,0:T(8,128)S(1)}, f32[32,128]{1,0:T(8,128)S(1)}, u32[]{:S(2)}, u32[]{:S(2)}) %collective-permute-start.7) | collective-permute-done | bytes 16416 | tf_op jit(solution)/shard_map/ppermute | solution.py:293
  63.4 0.2 collective-permute-start.8
  63.6 0.0 collective-permute-done.6
  63.6 0.9 collective-permute-done.8
  64.6 0.1 collective-permute-start.10
  64.7 5.4 %collective-permute-start.11 = (f32[144,128]{1,0:T(8,128)S(1)}, f32[144,128]{1,0:T(8,128)S(1)}, u32[]{:S(2)}, u32[]{:S(2)}) collective-permute-start(f32[144,128]{1,0:T(8,128)S(1)} %get-tuple-element.47), channel_id=1, source_target_pairs={{0,6},{1,7},{2,4},{3,5},{4,2},{5,3},{6,0},{7,1},{8,14},{9,15},{10,... | collective-permute-start | bytes 221192 | tf_op jit(solution)/shard_map/ppermute | solution.py:293
  70.0 0.0 collective-permute-start.9
  70.0 2.8 %collective-permute-done.10.v2_ref = f32[144,128]{1,0:T(8,128)S(1)} collective-permute-done((f32[144,128]{1,0:T(8,128)S(1)}, f32[144,128]{1,0:T(8,128)S(1)}, u32[]{:S(2)}, u32[]{:S(2)}) %collective-permute-start.10) | collective-permute-done | bytes 73760 | tf_op jit(solution)/shard_map/ppermute | solution.py:293
  72.9 0.4 collective-permute-done.11.v3_ref
  73.3 1.2 %collective-permute-done.9.v1_ref = f32[144,128]{1,0:T(8,128)S(1)} collective-permute-done((f32[144,128]{1,0:T(8,128)S(1)}, f32[144,128]{1,0:T(8,128)S(1)}, u32[]{:S(2)}, u32[]{:S(2)}) %collective-permute-start.9) | collective-permute-done | bytes 73760 | tf_op jit(solution)/shard_map/ppermute | solution.py:293
  74.5 0.0 all-to-all-done
  74.5 1.2 %shard_map.60 = (f32[16,2048]{1,0:T(8,128)S(1)}, f32[16,2048]{1,0:T(8,128)S(1)}) custom-call(f32[16,512,128]{2,1,0:T(8,128)} %bitcast.22.low_ref.high_ref, f32[16,512,128]{2,1,0:T(8,128)} %bitcast.22.low_ref.high_ref), custom_call_target="tpu_custom_call" | custom-call | bytes 262144 | tf_op jit(solution)/shard_map/pallas_call | solution.py:178
  75.7 3.7 %collective-permute-start.12 = (f32[8,128]{1,0:T(8,128)S(1)}, f32[8,128]{1,0:T(8,128)S(1)}, u32[]{:S(2)}, u32[]{:S(2)}) collective-permute-start(f32[8,128]{1,0:T(8,128)S(1)} %dynamic-slice_bitcast_fusion.7), channel_id=1, source_target_pairs={{0,8},{1,9},{2,10},{3,11},{4,12},{5,13},{6,14},{7,15},{8,0},{9,1},... | collective-permute-start | bytes 12296 | tf_op jit(solution)/shard_map/ppermute | solution.py:293
  79.4 0.8 collective-permute-start.13
  80.1 4.8 %collective-permute-start.14 = (f32[16,2048]{1,0:T(8,128)S(1)}, f32[16,2048]{1,0:T(8,128)S(1)}, u32[]{:S(2)}, u32[]{:S(2)}) collective-permute-start(f32[16,2048]{1,0:T(8,128)S(1)} %get-tuple-element.39), channel_id=1, source_target_pairs={{16,32},{32,16},{48,64},{64,48},{80,96},{96,80},{17,33},{33,17},{4... | collective-permute-start | bytes 393224 | tf_op jit(solution)/shard_map/ppermute | solution.py:361
  85.0 7.5 %shard_map.61 = (f32[16,32,2048]{2,1,0:T(8,128)}, f32[16,32,2048]{2,1,0:T(8,128)}, f32[2,16,8,2048]{3,2,1,0:T(8,128)S(1)}) custom-call(f32[16,16,32,128]{3,2,1,0:T(8,128)} %bitcast.27.x_ref, f32[128,128]{1,0:T(8,128)S(1)} %pad_maximum_fusion.9.v_own_ref, f32[144,128]{1,0:T(8,128)S(1)} %collective-permute-done.9.v1_ref, ...), custom_call_target="tpu_custom_call" | custom-call | bytes 12582912 | tf_op jit(solution)/shard_map/pallas_call | solution.py:235
  92.4 0.0 collective-permute-done.12
  92.5 0.6 fusion.4
  93.0 0.0 collective-permute-done.13.near_ref
  93.0 0.0 collective-permute-done.14.far_ref
  93.0 1.6 %shard_map.62 = f32[16,32,2048]{2,1,0:T(8,128)} custom-call(f32[16,2048]{1,0:T(8,128)S(1)} %collective-permute-done.13.near_ref, f32[16,2048]{1,0:T(8,128)S(1)} %collective-permute-done.14.far_ref, f32[2,16,8,2048]{3,2,1,0:T(8,128)S(1)} %get-tuple-element.40.sides_ref, f32[16,32,2048]{2,1,0:T(8,128)} %get-tuple-element.41.applied_ref), custom_call_target="tpu_custom_call", output_to_operand_aliasing={{}: (3, {})} | custom-call | bytes 1048576 | tf_op jit(solution)/shard_map/pallas_call | solution.py:276
  (14 shorter events, 0.2 us)
Async XLA Ops:
  0.6 2.2 %copy-start = (f32[256,2,2048]{2,1,0:T(2,128)S(1)}, f32[256,2,2048]{2,1,0:T(2,128)}, u32[]{:S(2)}) copy-start(f32[256,2,2048]{2,1,0:T(2,128)} %param.2) | copy-start | bytes 12582916
  3.9 13.0 %copy-start.2 = (f32[2,2048]{1,0:T(2,128)S(1)}, f32[2,2048]{1,0:T(2,128)}, u32[]{:S(2)}) copy-start(f32[2,2048]{1,0:T(2,128)} %param.3) | copy-start | bytes 49156
  3.9 20.5 %collective-permute-start = (f32[2048,128]{1,0:T(8,128)}, f32[2048,128]{1,0:T(8,128)S(1)}, u32[]{:S(2)}, u32[]{:S(2)}) collective-permute-start(f32[2048,128]{1,0:T(8,128)} %get-tuple-element.28), channel_id=1, source_target_pairs={{0,1},{1,0},{2,3},{3,2},{4,5},{5,4},{6,7},{7,6},{8,9},{9,8},{10,11... | collective-permute-start | bytes 3145736 | tf_op jit(solution)/shard_map/ppermute | solution.py:293
  3.9 38.8 %collective-permute-start.1 = (f32[2048,128]{1,0:T(8,128)S(1)}, f32[2048,128]{1,0:T(8,128)S(1)}, u32[]{:S(2)}, u32[]{:S(2)}) collective-permute-start(f32[2048,128]{1,0:T(8,128)S(1)} %get-tuple-element.30), channel_id=1, source_target_pairs={{1,2},{2,1},{3,4},{4,3},{5,6},{6,5},{7,8},{8,7},{9,10},{10,9},{11,... | collective-permute-start | bytes 3145736 | tf_op jit(solution)/shard_map/ppermute | solution.py:347
  12.4 62.1 %all-to-all-start = ((f32[256,2,2048]{2,1,0:T(2,128)}), f32[256,2,2048]{2,1,0:T(2,128)}, u32[]{:S(2)}, u32[]{:S(2)}) async-start(f32[256,2,2048]{2,1,0:T(2,128)} %param.2), calls=%async_computation | async-start | bytes 8388608 | tf_op jit(solution)/shard_map/all_to_all | solution.py:348
  16.9 2.2 %copy-start.1 = (f32[256,2,2048]{2,1,0:T(2,128)S(1)}, f32[256,2,2048]{2,1,0:T(2,128)}, u32[]{:S(2)}) copy-start(f32[256,2,2048]{2,1,0:T(2,128)} %param.2) | copy-start | bytes 12582916
  44.3 1.6 %collective-permute-start.2 = (f32[64,1024]{1,0:T(8,128)S(1)}, f32[64,1024]{1,0:T(8,128)S(1)}, u32[]{:S(2)}, u32[]{:S(2)}) collective-permute-start(f32[64,1024]{1,0:T(8,128)S(1)} %get-tuple-element.32), channel_id=1, source_target_pairs={{0,1},{1,0},{2,3},{3,2},{4,5},{5,4},{6,7},{7,6},{8,9},{9,8},{10,11... | collective-permute-start | bytes 786440 | tf_op jit(solution)/shard_map/ppermute | solution.py:293
  46.0 4.9 %collective-permute-start.3 = (f32[16,1024]{1,0:T(8,128)S(1)}, f32[16,1024]{1,0:T(8,128)S(1)}, u32[]{:S(2)}, u32[]{:S(2)}) collective-permute-start(f32[16,1024]{1,0:T(8,128)S(1)} %get-tuple-element.42), channel_id=1, source_target_pairs={{0,32},{1,33},{2,34},{3,35},{4,36},{5,37},{6,38},{7,39},{8,40},{9,... | collective-permute-start | bytes 196616 | tf_op jit(solution)/shard_map/ppermute | solution.py:293
  46.5 5.9 %collective-permute-start.4 = (f32[16,1024]{1,0:T(8,128)S(1)}, f32[16,1024]{1,0:T(8,128)S(1)}, u32[]{:S(2)}, u32[]{:S(2)}) collective-permute-start(f32[16,1024]{1,0:T(8,128)S(1)} %get-tuple-element.44), channel_id=1, source_target_pairs={{0,64},{1,65},{2,66},{3,67},{4,68},{5,69},{6,70},{7,71},{8,72},{9,... | collective-permute-start | bytes 196616 | tf_op jit(solution)/shard_map/ppermute | solution.py:293
  47.1 6.2 %collective-permute-start.5 = (f32[16,1024]{1,0:T(8,128)S(1)}, f32[16,1024]{1,0:T(8,128)S(1)}, u32[]{:S(2)}, u32[]{:S(2)}) collective-permute-start(f32[16,1024]{1,0:T(8,128)S(1)} %get-tuple-element.43), channel_id=1, source_target_pairs={{0,96},{1,97},{2,98},{3,99},{4,100},{5,101},{6,102},{7,103},{8,104... | collective-permute-start | bytes 196616 | tf_op jit(solution)/shard_map/ppermute | solution.py:293
  50.7 12.6 %collective-permute-start.7 = (f32[32,128]{1,0:T(8,128)S(1)}, f32[32,128]{1,0:T(8,128)S(1)}, u32[]{:S(2)}, u32[]{:S(2)}) collective-permute-start(f32[32,128]{1,0:T(8,128)S(1)} %bitcast.60), channel_id=1, source_target_pairs={{0,8},{1,9},{2,10},{3,11},{4,12},{5,13},{6,14},{7,15},{8,0},{9,1},... | collective-permute-start | bytes 49160 | tf_op jit(solution)/shard_map/ppermute | solution.py:293
  53.3 10.3 %collective-permute-start.6 = (f32[8,1024]{1,0:T(8,128)S(1)}, f32[8,1024]{1,0:T(8,128)S(1)}, u32[]{:S(2)}, u32[]{:S(2)}) collective-permute-start(f32[8,1024]{1,0:T(8,128)S(1)} %dynamic-slice_bitcast_fusion.3), channel_id=1, source_target_pairs={{0,24},{1,25},{2,26},{3,27},{4,28},{5,29},{6,30},{7,31},{8,16},{9,... | collective-permute-start | bytes 98312 | tf_op jit(solution)/shard_map/ppermute | solution.py:314
  63.4 1.2 %collective-permute-start.8 = (f32[64,128]{1,0:T(8,128)S(1)}, f32[64,128]{1,0:T(8,128)S(1)}, u32[]{:S(2)}, u32[]{:S(2)}) collective-permute-start(f32[64,128]{1,0:T(8,128)S(1)} %pad_maximum_fusion.10), channel_id=1, source_target_pairs={{0,1},{1,0},{2,3},{3,2},{4,5},{5,4},{6,7},{7,6},{8,9},{9,8},{10,11... | collective-permute-start | bytes 98312 | tf_op jit(solution)/shard_map/ppermute | solution.py:293
  64.6 8.3 %collective-permute-start.10 = (f32[144,128]{1,0:T(8,128)S(1)}, f32[144,128]{1,0:T(8,128)S(1)}, u32[]{:S(2)}, u32[]{:S(2)}) collective-permute-start(f32[144,128]{1,0:T(8,128)S(1)} %get-tuple-element.46), channel_id=1, source_target_pairs={{0,4},{1,5},{2,6},{3,7},{4,0},{5,1},{6,2},{7,3},{8,12},{9,13},{10,... | collective-permute-start | bytes 221192 | tf_op jit(solution)/shard_map/ppermute | solution.py:293
  64.7 8.6 %collective-permute-start.11 = (f32[144,128]{1,0:T(8,128)S(1)}, f32[144,128]{1,0:T(8,128)S(1)}, u32[]{:S(2)}, u32[]{:S(2)}) collective-permute-start(f32[144,128]{1,0:T(8,128)S(1)} %get-tuple-element.47), channel_id=1, source_target_pairs={{0,6},{1,7},{2,4},{3,5},{4,2},{5,3},{6,0},{7,1},{8,14},{9,15},{10,... | collective-permute-start | bytes 221192 | tf_op jit(solution)/shard_map/ppermute | solution.py:293
  70.0 4.4 %collective-permute-start.9 = (f32[144,128]{1,0:T(8,128)S(1)}, f32[144,128]{1,0:T(8,128)S(1)}, u32[]{:S(2)}, u32[]{:S(2)}) collective-permute-start(f32[144,128]{1,0:T(8,128)S(1)} %get-tuple-element.45), channel_id=1, source_target_pairs={{0,2},{1,3},{2,0},{3,1},{4,6},{5,7},{6,4},{7,5},{8,10},{9,11},{10,... | collective-permute-start | bytes 221192 | tf_op jit(solution)/shard_map/ppermute | solution.py:293
  75.7 16.7 %collective-permute-start.12 = (f32[8,128]{1,0:T(8,128)S(1)}, f32[8,128]{1,0:T(8,128)S(1)}, u32[]{:S(2)}, u32[]{:S(2)}) collective-permute-start(f32[8,128]{1,0:T(8,128)S(1)} %dynamic-slice_bitcast_fusion.7), channel_id=1, source_target_pairs={{0,8},{1,9},{2,10},{3,11},{4,12},{5,13},{6,14},{7,15},{8,0},{9,1},... | collective-permute-start | bytes 12296 | tf_op jit(solution)/shard_map/ppermute | solution.py:293
  79.4 13.7 %collective-permute-start.13 = (f32[16,2048]{1,0:T(8,128)S(1)}, f32[16,2048]{1,0:T(8,128)S(1)}, u32[]{:S(2)}, u32[]{:S(2)}) collective-permute-start(f32[16,2048]{1,0:T(8,128)S(1)} %get-tuple-element.38), channel_id=1, source_target_pairs={{0,16},{16,0},{32,48},{48,32},{64,80},{80,64},{96,112},{112,96},{1... | collective-permute-start | bytes 393224 | tf_op jit(solution)/shard_map/ppermute | solution.py:360
  80.1 12.9 %collective-permute-start.14 = (f32[16,2048]{1,0:T(8,128)S(1)}, f32[16,2048]{1,0:T(8,128)S(1)}, u32[]{:S(2)}, u32[]{:S(2)}) collective-permute-start(f32[16,2048]{1,0:T(8,128)S(1)} %get-tuple-element.39), channel_id=1, source_target_pairs={{16,32},{32,16},{48,64},{64,48},{80,96},{96,80},{17,33},{33,17},{4... | collective-permute-start | bytes 393224 | tf_op jit(solution)/shard_map/ppermute | solution.py:361
